TPU v7x, 32 devices: a whole 2x2x4 slice. The times are simulated.
32 devices in a mesh: section: 4 (over y, x), strip: 8 (over z, core).
Axes of the slice: x: 2, y: 2, z: 4, core: 2. Of those that a mesh axis runs over, the one named last changes fastest.
Arguments:
- cotangent: bfloat16 [1, 512, 2048], P(None, 'strip'), may hold values from -6 to 6
- activations: bfloat16 [4, 1, 512, 2048], P('section', None, 'strip'), may hold values from -6 to 6
- weights: bfloat16 [4, 2, 3, 3, 64, 64], P('section'), may hold values from -0.25 to 0.25
- biases: float32 [4, 2, 64], P('section'), may hold values from -3 to 3
Outputs:
- noise_grad: bfloat16 [4, 1, 512, 2048], P('section', None, 'strip')
- weight_grad: float32 [4, 2, 3, 3, 64, 64], P('section')
- bias_grad: float32 [4, 2, 64], P('section')
All inputs are finite; a program needn't handle non-finite values.
Results may differ from a plain program's by a relative error of at most 0.01.
Values may be sent and summed in bfloat16 or wider, within the bound.
No kernel may reach another device: no remote copies, remote signals or barrier semaphores. Data moves between devices by JAX's collectives and lax.ppermute only.
A program may use at most 64 MiB of HBM per device.

v0:
```python
import jax
import jax.numpy as jnp
from jax import lax
from jax.sharding import PartitionSpec as P

LEAK = 0.05


def extended_2(cells, sides, width):
    for axis, dim in sides:
        count = lax.axis_size(axis)
        ends = count - 1
        head = lax.slice_in_dim(cells, 0, width, axis=dim)
        tail = lax.slice_in_dim(cells, cells.shape[dim] - width, cells.shape[dim], axis=dim)
        cells = jnp.concatenate(
            [
                lax.ppermute(tail, axis, [(i, (i + 1) % count) for i in range(ends)]),
                cells,
                lax.ppermute(head, axis, [((i + 1) % count, i) for i in range(ends)]),
            ],
            axis=dim,
        )
    return cells


def shifted_2(x, axis, by):
    peers = lax.axis_size(axis)
    pairs = [(i, i + by) for i in range(peers) if 0 <= i + by < peers]
    return lax.ppermute(x, axis, pairs)


def activate(value):
    return LEAK * value + (1.0 - LEAK) * jax.nn.softplus(value)


def steepness(value):
    return LEAK + (1.0 - LEAK) * jax.nn.sigmoid(value)


def conv_rows(field_in, kernel):
    return lax.conv_general_dilated(
        field_in,
        kernel,
        (1, 1),
        ((0, 0), (1, 1)),
        dimension_numbers=("NHWC", "HWIO", "NHWC"),
        preferred_element_type=jnp.float32,
    )


def flipped(kernel):
    return jnp.transpose(kernel[::-1, ::-1], (0, 1, 3, 2))


def weight_taps(extended, error):
    padded = jnp.pad(extended, ((0, 0), (0, 0), (1, 1), (0, 0)))
    height = error.shape[1]
    col_span = error.shape[2]
    channels = error.shape[3]
    tap_list = []
    for row_tap in range(3):
        for col_tap in range(3):
            window = padded[:, row_tap : row_tap + height, col_tap : col_tap + col_span]
            tap_list.append(
                lax.dot_general(
                    window,
                    error,
                    (((0, 1, 2), (0, 1, 2)), ((), ())),
                    preferred_element_type=jnp.float32,
                )
            )
    return jnp.stack(tap_list).reshape(3, 3, channels, channels)


def edge_rows(field_in, rim_depth, live_rows):
    upper_rows = field_in[:, :rim_depth]
    lower_rows = lax.dynamic_slice_in_dim(field_in, live_rows - rim_depth, rim_depth, 1)
    return jnp.concatenate([upper_rows, lower_rows], axis=1)


def attach(field_in, received, rim_depth, live_rows):
    upper_rows = received[:, :rim_depth]
    lower_rows = received[:, 3 * rim_depth :]
    filler = jnp.zeros_like(upper_rows)
    joined = jnp.concatenate([upper_rows, field_in, filler], axis=1)
    return lax.dynamic_update_slice_in_dim(joined, lower_rows, live_rows + rim_depth, 1)


def local(cotangent, activations, weights, biases):
    section_id = lax.axis_index("section")
    strip_id = lax.axis_index("strip")
    strip_count = lax.axis_size("strip")
    section_count = lax.axis_size("section")
    samples, row_count, flat_width = cotangent.shape
    channels = weights.shape[-1]
    col_count = flat_width // channels
    coarse_rows = row_count * 3 // 4
    coarse_cols = col_count * 3 // 4
    row_table = jnp.array(
        [
            row_count * 3**section_level // 4**section_level
            for section_level in range(section_count)
        ],
        jnp.int32,
    )
    col_table = jnp.array(
        [
            col_count * 3**section_level // 4**section_level
            for section_level in range(section_count)
        ],
        jnp.int32,
    )
    live_rows = row_table[section_id]
    live_cols = col_table[section_id]
    row_index = lax.iota(jnp.int32, row_count)
    col_index = lax.iota(jnp.int32, col_count)
    col_live = col_index < live_cols
    keep_mask = ((row_index < live_rows)[:, None, None] & col_live[None, :, None]).astype(
        jnp.float32
    )
    kernel_in = weights[0, 0]
    kernel_out = weights[0, 1]
    kernel_in_back = flipped(kernel_in)
    kernel_out_back = flipped(kernel_out)
    bias_in = biases[0, 0]
    bias_out = biases[0, 1]
    cot_grid = cotangent.reshape(samples, row_count, col_count, channels)
    act_grid = activations[0].reshape(samples, row_count, col_count, channels)
    group_count = samples // samples
    tick_count = group_count + section_count - 1

    def section_backward(grad_out, field_in):
        got_input = extended_2(edge_rows(field_in, 1, live_rows), (("strip", 1),), 1)
        input_ext = attach(field_in, got_input, 1, live_rows)
        pre_in = conv_rows(input_ext, kernel_in) + bias_in
        hidden = (activate(pre_in) * keep_mask).astype(jnp.bfloat16)
        got_hidden = extended_2(edge_rows(hidden, 1, live_rows), (("strip", 1),), 1)
        hidden_ext = attach(hidden, got_hidden, 1, live_rows)
        pre_out = conv_rows(hidden_ext, kernel_out) + bias_out
        error_out = (grad_out.astype(jnp.float32) * steepness(pre_out) * keep_mask).astype(
            jnp.bfloat16
        )
        got_error = extended_2(edge_rows(error_out, 1, live_rows), (("strip", 1),), 1)
        error_ext = attach(error_out, got_error, 1, live_rows)
        back_hidden = conv_rows(error_ext, kernel_out_back)
        error_in = (back_hidden * steepness(pre_in) * keep_mask).astype(jnp.bfloat16)
        got_inner = extended_2(edge_rows(error_in, 1, live_rows), (("strip", 1),), 1)
        inner_ext = attach(error_in, got_inner, 1, live_rows)
        back_input = conv_rows(inner_ext, kernel_in_back) * keep_mask
        noise_part = back_input.astype(jnp.bfloat16)
        grad_up = (grad_out.astype(jnp.float32) + back_input).astype(jnp.bfloat16)
        kernel_grads = jnp.stack(
            [weight_taps(input_ext, error_in), weight_taps(hidden_ext, error_out)]
        )
        bias_grads = jnp.stack(
            [
                jnp.sum(error_in, axis=(0, 1, 2), dtype=jnp.float32),
                jnp.sum(error_out, axis=(0, 1, 2), dtype=jnp.float32),
            ]
        )
        return (noise_part, grad_up, kernel_grads, bias_grads)

    def coarse_grad(grad_up, fine_level):
        coarse_level = jnp.minimum(fine_level + 1, section_count - 1)
        fine_height = row_table[fine_level]
        coarse_height = row_table[coarse_level]
        fine_width = col_table[fine_level]
        coarse_width = col_table[coarse_level]
        global_row = strip_id * fine_height + row_index
        row_num = jnp.maximum(6 * global_row - 1, 0)
        row_low = row_num // 8
        row_frac = (row_num - 8 * row_low).astype(jnp.float32) / 8.0
        row_high = jnp.minimum(row_low + 1, strip_count * coarse_height - 1)
        row_on = (row_index < fine_height).astype(jnp.float32)
        base_row = strip_id * coarse_height - 1
        target_row = lax.iota(jnp.int32, coarse_rows + 2)[:, None]
        row_matrix = (
            jnp.where(target_row == (row_low - base_row)[None, :], 1.0 - row_frac[None, :], 0.0)
            + jnp.where(target_row == (row_high - base_row)[None, :], row_frac[None, :], 0.0)
        ) * row_on[None, :]
        col_num = jnp.maximum((2 * col_index + 1) * coarse_width - fine_width, 0)
        col_den = 2 * fine_width
        col_low = col_num // col_den
        col_frac = (col_num - col_den * col_low).astype(jnp.float32) / col_den.astype(jnp.float32)
        col_high = jnp.minimum(col_low + 1, coarse_width - 1)
        col_on = (col_index < fine_width).astype(jnp.float32)
        target_col = lax.iota(jnp.int32, coarse_cols)[:, None]
        col_matrix = (
            jnp.where(target_col == col_low[None, :], 1.0 - col_frac[None, :], 0.0)
            + jnp.where(target_col == col_high[None, :], col_frac[None, :], 0.0)
        ) * col_on[None, :]
        wide_grad = grad_up.astype(jnp.float32)
        partial_cols = jnp.einsum(
            "gyxc,kx->gykc", wide_grad, col_matrix, precision=lax.Precision.HIGHEST
        )
        summed = jnp.einsum(
            "ry,gykc->grkc", row_matrix, partial_cols, precision=lax.Precision.HIGHEST
        )
        rim_pair = jnp.concatenate(
            [summed[:, :1], lax.dynamic_slice_in_dim(summed, coarse_height + 1, 1, 1)], axis=1
        )
        got_rims = extended_2(rim_pair, (("strip", 1),), 1)
        core_rows = summed[:, 1 : coarse_rows + 1]
        index_row = lax.iota(jnp.int32, coarse_rows)[None, :, None, None]
        core_rows = (
            core_rows
            + jnp.where(index_row == 0, got_rims[:, :1], 0.0)
            + jnp.where(index_row == coarse_height - 1, got_rims[:, 3:], 0.0)
        )
        coarse_mask = (
            (lax.iota(jnp.int32, coarse_rows) < coarse_height)[:, None, None]
            & (lax.iota(jnp.int32, coarse_cols) < coarse_width)[None, :, None]
        ).astype(jnp.float32)
        return (core_rows * coarse_mask).astype(jnp.bfloat16)

    def expand(coarse):
        return jnp.pad(
            coarse, ((0, 0), (0, row_count - coarse_rows), (0, col_count - coarse_cols), (0, 0))
        )

    def one_tick(tick_index, state_in):
        incoming, noise_acc, kernel_acc, bias_acc = state_in
        group_index = tick_index - section_id
        active = (group_index >= 0) & (group_index < group_count)
        start_row = jnp.clip(group_index, 0, group_count - 1) * samples
        grad_out = jnp.where(section_id == 0, cot_grid, incoming)
        field_in = (act_grid.astype(jnp.float32) * keep_mask).astype(jnp.bfloat16)
        noise_part, grad_up, kernel_grads, bias_grads = section_backward(grad_out, field_in)
        shifted = shifted_2(grad_up, "section", 1)
        next_in = expand(coarse_grad(shifted, jnp.maximum(section_id - 1, 0)))
        old_noise = noise_acc
        noise_acc = lax.dynamic_update_slice_in_dim(
            noise_acc, jnp.where(active, noise_part, old_noise), start_row, 0
        )
        weight_on = active.astype(jnp.float32)
        return (
            next_in,
            noise_acc,
            kernel_acc + weight_on * kernel_grads,
            bias_acc + weight_on * bias_grads,
        )

    initial = (
        jnp.zeros((samples, row_count, col_count, channels), jnp.bfloat16),
        jnp.zeros((samples, row_count, col_count, channels), jnp.bfloat16),
        jnp.zeros((2, 3, 3, channels, channels), jnp.float32),
        jnp.zeros((2, channels), jnp.float32),
    )
    final_state = lax.fori_loop(0, tick_count, one_tick, initial)
    noise_acc = final_state[1]
    kernel_sum, bias_sum = lax.psum((final_state[2], final_state[3]), "strip")
    pixel_count = (samples * strip_count * live_rows * live_cols).astype(jnp.float32)
    scale_back = 1.0 / jnp.sqrt(pixel_count)
    return (
        noise_acc.reshape(1, samples, row_count, flat_width),
        (kernel_sum * scale_back)[None],
        (bias_sum * scale_back)[None],
    )


def solution(mesh):
    return jax.shard_map(
        local,
        mesh=mesh,
        in_specs=(
            P(None, "strip", None),
            P("section", None, "strip", None),
            P("section", None, None, None, None, None),
            P("section", None, None),
        ),
        out_specs=(
            P("section", None, "strip", None),
            P("section", None, None, None, None, None),
            P("section", None, None),
        ),
        check_vma=False,
    )
```

profile of v0, /device:TPU:5, one launch (start us, length us, event | category | flops | bytes accessed | tf_op | source)
XLA Modules:
  0.0 389.0 jit_solution(14481895844583530607)
XLA Ops:
  13.2 3.8 collective-permute-start.11
  17.0 1.9 collective-permute-start.12
  30.3 3.8 dynamic_update_slice.63
  34.8 1.7 fusion.155
  37.5 3.6 collective-permute-start.13
  41.2 1.9 collective-permute-start.14
  43.5 1.6 copy.183
  49.5 276.5 %while.25 = (s32[]{:T(128)}, bf16[1,64,32,64]{3,1,2,0:T(8,128)(2,1)S(1)}, bf16[1,64,32,64]{3,2,1,0:T(8,128)(2,1)}, f32[2,3,3,64,64]{4,3,2,1,0:T(8,128)}, f32[2,6...) while((s32[]{:T(128)}, ...), condition=%wide.region_3.4_spmd.clone.clone, body=%wide.region_0.3_spmd.clone.clone.sunk | while | flops 787387328 | bytes 55671280 | solution.py:249
  50.7 2.7 collective-permute-start
  53.4 1.9 collective-permute-start.1
  61.1 2.0 convolution_select_fusion.6
  66.2 3.6 collective-permute-start.2
  69.8 1.9 collective-permute-start.3
  71.8 3.6 collective-permute-start.4
  75.4 1.9 collective-permute-start.10
  77.3 1.9 collective-permute-start.9
  79.3 1.9 collective-permute-start.5
  92.4 3.1 collective-permute-start.6
  96.5 9.8 %collective-permute-done.6 = bf16[1,64,32,64]{3,2,1,0:T(8,128)(2,1)S(1)} collective-permute-done((bf16[1,64,32,64]{3,2,1,0:T(8,128)(2,1)S(1)}, bf16[1,64,32,64]{3,2,1,0:T(8,128)(2,1)S(1)}, u32[]{:S(2)}, u32[]{:S(2)}) %collective-permute-start.6) | collective-permute-done | bytes 262176 | tf_op jit(solution)/shard_map/while/body/eval_jaxpr/ppermute | solution.py:29
  107.6 1.9 collective-permute-start.7
  109.5 6.9 %collective-permute-start.8 = (f32[1,1,24,64]{3,2,1,0:T(8,128)S(1)}, f32[1,1,24,64]{3,2,1,0:T(8,128)S(1)}, u32[]{:S(2)}, u32[]{:S(2)}) collective-permute-start(f32[1,1,24,64]{3,2,1,0:T(8,128)S(1)} %bitcast.499), channel_id=1, source_target_pairs={{0,1},{1,2},{2,3},{3,4},{4,5},{5,6},{6,7},{8,9},{9,10},{10,11},{11... | collective-permute-start | bytes 18440 | tf_op jit(solution)/shard_map/while/body/eval_jaxpr/ppermute | solution.py:17
  119.1 3.8 collective-permute-start
  122.9 1.9 collective-permute-start.1
  130.6 2.0 convolution_select_fusion.6
  135.6 3.6 collective-permute-start.2
  139.3 1.9 collective-permute-start.3
  141.2 3.6 collective-permute-start.4
  144.8 1.9 collective-permute-start.10
  146.8 1.9 collective-permute-start.9
  148.7 1.9 collective-permute-start.5
  161.8 2.2 collective-permute-start.6
  165.0 10.7 %collective-permute-done.6 = bf16[1,64,32,64]{3,2,1,0:T(8,128)(2,1)S(1)} collective-permute-done((bf16[1,64,32,64]{3,2,1,0:T(8,128)(2,1)S(1)}, bf16[1,64,32,64]{3,2,1,0:T(8,128)(2,1)S(1)}, u32[]{:S(2)}, u32[]{:S(2)}) %collective-permute-start.6) | collective-permute-done | bytes 262176 | tf_op jit(solution)/shard_map/while/body/eval_jaxpr/ppermute | solution.py:29
  177.1 1.9 collective-permute-start.7
  179.0 6.9 %collective-permute-start.8 = (f32[1,1,24,64]{3,2,1,0:T(8,128)S(1)}, f32[1,1,24,64]{3,2,1,0:T(8,128)S(1)}, u32[]{:S(2)}, u32[]{:S(2)}) collective-permute-start(f32[1,1,24,64]{3,2,1,0:T(8,128)S(1)} %bitcast.499), channel_id=1, source_target_pairs={{0,1},{1,2},{2,3},{3,4},{4,5},{5,6},{6,7},{8,9},{9,10},{10,11},{11... | collective-permute-start | bytes 18440 | tf_op jit(solution)/shard_map/while/body/eval_jaxpr/ppermute | solution.py:17
  188.6 3.8 collective-permute-start
  192.4 1.9 collective-permute-start.1
  200.1 2.0 convolution_select_fusion.6
  205.1 3.6 collective-permute-start.2
  208.8 1.9 collective-permute-start.3
  210.7 3.3 collective-permute-start.4
  214.1 1.9 collective-permute-start.10
  216.0 1.9 collective-permute-start.9
  218.0 1.9 collective-permute-start.5
  231.1 1.9 collective-permute-start.6
  233.9 11.2 %collective-permute-done.6 = bf16[1,64,32,64]{3,2,1,0:T(8,128)(2,1)S(1)} collective-permute-done((bf16[1,64,32,64]{3,2,1,0:T(8,128)(2,1)S(1)}, bf16[1,64,32,64]{3,2,1,0:T(8,128)(2,1)S(1)}, u32[]{:S(2)}, u32[]{:S(2)}) %collective-permute-start.6) | collective-permute-done | bytes 262176 | tf_op jit(solution)/shard_map/while/body/eval_jaxpr/ppermute | solution.py:29
  246.5 1.9 collective-permute-start.7
  248.5 6.7 %collective-permute-start.8 = (f32[1,1,24,64]{3,2,1,0:T(8,128)S(1)}, f32[1,1,24,64]{3,2,1,0:T(8,128)S(1)}, u32[]{:S(2)}, u32[]{:S(2)}) collective-permute-start(f32[1,1,24,64]{3,2,1,0:T(8,128)S(1)} %bitcast.499), channel_id=1, source_target_pairs={{0,1},{1,2},{2,3},{3,4},{4,5},{5,6},{6,7},{8,9},{9,10},{10,11},{11... | collective-permute-start | bytes 18440 | tf_op jit(solution)/shard_map/while/body/eval_jaxpr/ppermute | solution.py:17
  257.8 3.8 collective-permute-start
  261.6 1.9 collective-permute-start.1
  269.3 2.0 convolution_select_fusion.6
  274.3 3.6 collective-permute-start.2
  278.0 1.9 collective-permute-start.3
  279.9 3.3 collective-permute-start.4
  283.3 1.9 collective-permute-start.10
  285.2 1.9 collective-permute-start.9
  287.2 1.9 collective-permute-start.5
  300.3 1.9 collective-permute-start.6
  303.2 11.2 %collective-permute-done.6 = bf16[1,64,32,64]{3,2,1,0:T(8,128)(2,1)S(1)} collective-permute-done((bf16[1,64,32,64]{3,2,1,0:T(8,128)(2,1)S(1)}, bf16[1,64,32,64]{3,2,1,0:T(8,128)(2,1)S(1)}, u32[]{:S(2)}, u32[]{:S(2)}) %collective-permute-start.6) | collective-permute-done | bytes 262176 | tf_op jit(solution)/shard_map/while/body/eval_jaxpr/ppermute | solution.py:29
  315.8 1.9 collective-permute-start.7
  317.7 6.7 %collective-permute-start.8 = (f32[1,1,24,64]{3,2,1,0:T(8,128)S(1)}, f32[1,1,24,64]{3,2,1,0:T(8,128)S(1)}, u32[]{:S(2)}, u32[]{:S(2)}) collective-permute-start(f32[1,1,24,64]{3,2,1,0:T(8,128)S(1)} %bitcast.499), channel_id=1, source_target_pairs={{0,1},{1,2},{2,3},{3,4},{4,5},{5,6},{6,7},{8,9},{9,10},{10,11},{11... | collective-permute-start | bytes 18440 | tf_op jit(solution)/shard_map/while/body/eval_jaxpr/ppermute | solution.py:17
  326.1 2.2 reshape.737
  328.3 11.5 %psum.15 = f32[2,64]{1,0:T(2,128)S(1)} all-reduce(f32[2,64]{1,0:T(2,128)S(1)} %get-tuple-element.969), channel_id=1, replica_groups=mesh['section'=4,'strip'=8] {'strip'}, use_global_device_ids=true, to_apply=%region_5.6 | all-reduce | flops 128 | bytes 1024 | tf_op jit(solution)/shard_map/psum | solution.py:251
  340.4 39.9 %all-reduce.5.cloned.1.call-done = f32[2,3,3,64,64]{4,3,2,1,0:T(8,128)} async-done(((f32[2,3,3,64,64]{4,3,2,1,0:T(8,128)}), f32[2,3,3,64,64]{4,3,2,1,0:T(8,128)}) %all-reduce.5.cloned.1.call-update) | async-done | bytes 294928 | tf_op jit(solution)/shard_map/psum | solution.py:251
  380.2 1.9 multiply_bitcast_fusion
  (457 shorter events, 113.1 us)
Async XLA Ops:
  7.2 11.8 %copy-start.14 = (f32[1,2,64]{2,1,0:T(2,128)S(1)}, f32[1,2,64]{2,1,0:T(2,128)}, u32[]{:S(2)}) copy-start(f32[1,2,64]{2,1,0:T(2,128)} %param.11) | copy-start | bytes 1540
  7.2 11.8 %copy-start.11 = (bf16[1,2,3,3,64,64]{5,4,3,2,1,0:T(8,128)(2,1)S(1)}, bf16[1,2,3,3,64,64]{5,4,3,2,1,0:T(8,128)(2,1)}, u32[]{:S(2)}) copy-start(bf16[1,2,3,3,64,64]{5,4,3,2,1,0:T(8,128)(2,1)} %param.10) | copy-start | bytes 442372
  7.2 373.1 %all-reduce.5.cloned.1.call-start = ((), (), s32[]{:S(2)}) async-start(), calls=%async_computation | async-start | bytes 1179648 | tf_op jit(solution)/shard_map/psum | solution.py:251
  12.9 14.4 %copy-start.12 = (bf16[1,64,2048]{2,1,0:T(8,128)(2,1)S(1)}, bf16[1,64,2048]{2,1,0:T(8,128)(2,1)}, u32[]{:S(2)}) copy-start(bf16[1,64,2048]{2,1,0:T(8,128)(2,1)} %param.8) | copy-start | bytes 786436
  13.2 15.9 %collective-permute-start.11 = (bf16[1,1,32,64]{3,2,1,0:T(8,128)(2,1)S(1)}, bf16[1,1,32,64]{3,2,1,0:T(8,128)(2,1)S(1)}, u32[]{:S(2)}, u32[]{:S(2)}) collective-permute-start(bf16[1,1,32,64]{3,2,1,0:T(8,128)(2,1)S(1)} %get-tuple-element.1367), channel_id=1, source_target_pairs={{0,1},{1,2},{2,3},{3,4},{4,5},{5,6},{6,7},{8,9},{9,10},{10,11},{11... | collective-permute-start | bytes 12296 | tf_op jit(solution)/shard_map/while/body/eval_jaxpr/ppermute | solution.py:17
  17.0 12.9 %collective-permute-start.12 = (bf16[1,1,32,64]{3,2,1,0:T(8,128)(2,1)S(1)}, bf16[1,1,32,64]{3,2,1,0:T(8,128)(2,1)S(1)}, u32[]{:S(2)}, u32[]{:S(2)}) collective-permute-start(bf16[1,1,32,64]{3,2,1,0:T(8,128)(2,1)S(1)} %get-tuple-element.1366), channel_id=1, source_target_pairs={{1,0},{2,1},{3,2},{4,3},{5,4},{6,5},{7,6},{9,8},{10,9},{11,10},{12... | collective-permute-start | bytes 12296 | tf_op jit(solution)/shard_map/while/body/eval_jaxpr/ppermute | solution.py:19
  37.5 7.5 %collective-permute-start.13 = (bf16[1,1,32,64]{3,0,2,1:T(2,128)(2,1)S(1)}, bf16[1,1,32,64]{3,0,2,1:T(2,128)(2,1)S(1)}, u32[]{:S(2)}, u32[]{:S(2)}) collective-permute-start(bf16[1,1,32,64]{3,0,2,1:T(2,128)(2,1)S(1)} %constant_dynamic-slice_fusion.5), channel_id=1, source_target_pairs={{0,1},{1,2},{2,3},{3,4},{4,5},{5,6},{6,7},{8,9},{9,10},{10,11},{11... | collective-permute-start | bytes 12296 | tf_op jit(solution)/shard_map/while/body/eval_jaxpr/ppermute | solution.py:17
  41.2 5.1 %collective-permute-start.14 = (bf16[1,1,32,64]{3,0,2,1:T(2,128)(2,1)S(1)}, bf16[1,1,32,64]{3,0,2,1:T(2,128)(2,1)S(1)}, u32[]{:S(2)}, u32[]{:S(2)}) collective-permute-start(bf16[1,1,32,64]{3,0,2,1:T(2,128)(2,1)S(1)} %slice_bitcast_fusion.16), channel_id=1, source_target_pairs={{1,0},{2,1},{3,2},{4,3},{5,4},{6,5},{7,6},{9,8},{10,9},{11,10},{12... | collective-permute-start | bytes 12296 | tf_op jit(solution)/shard_map/while/body/eval_jaxpr/ppermute | solution.py:19
  50.7 8.9 %collective-permute-start = (bf16[1,1,32,64]{3,2,1,0:T(8,128)(2,1)S(1)}, bf16[1,1,32,64]{3,2,1,0:T(8,128)(2,1)S(1)}, u32[]{:S(2)}, u32[]{:S(2)}) collective-permute-start(bf16[1,1,32,64]{3,2,1,0:T(8,128)(2,1)S(1)} %get-tuple-element.1604), channel_id=1, source_target_pairs={{0,1},{1,2},{2,3},{3,4},{4,5},{5,6},{6,7},{8,9},{9,10},{10,11},{11... | collective-permute-start | bytes 12296 | tf_op jit(solution)/shard_map/while/body/eval_jaxpr/ppermute | solution.py:17
  53.4 6.3 %collective-permute-start.1 = (bf16[1,1,32,64]{3,2,1,0:T(8,128)(2,1)S(1)}, bf16[1,1,32,64]{3,2,1,0:T(8,128)(2,1)S(1)}, u32[]{:S(2)}, u32[]{:S(2)}) collective-permute-start(bf16[1,1,32,64]{3,2,1,0:T(8,128)(2,1)S(1)} %get-tuple-element.1605), channel_id=1, source_target_pairs={{1,0},{2,1},{3,2},{4,3},{5,4},{6,5},{7,6},{9,8},{10,9},{11,10},{12... | collective-permute-start | bytes 12296 | tf_op jit(solution)/shard_map/while/body/eval_jaxpr/ppermute | solution.py:19
  66.2 13.1 %collective-permute-start.2 = (bf16[1,1,32,64]{3,2,1,0:T(8,128)(2,1)S(1)}, bf16[1,1,32,64]{3,2,1,0:T(8,128)(2,1)S(1)}, u32[]{:S(2)}, u32[]{:S(2)}) collective-permute-start(bf16[1,1,32,64]{3,2,1,0:T(8,128)(2,1)S(1)} %get-tuple-element.1607), channel_id=1, source_target_pairs={{0,1},{1,2},{2,3},{3,4},{4,5},{5,6},{6,7},{8,9},{9,10},{10,11},{11... | collective-permute-start | bytes 12296 | tf_op jit(solution)/shard_map/while/body/eval_jaxpr/ppermute | solution.py:17
  69.8 11.4 %collective-permute-start.3 = (bf16[1,1,32,64]{3,2,1,0:T(8,128)(2,1)S(1)}, bf16[1,1,32,64]{3,2,1,0:T(8,128)(2,1)S(1)}, u32[]{:S(2)}, u32[]{:S(2)}) collective-permute-start(bf16[1,1,32,64]{3,2,1,0:T(8,128)(2,1)S(1)} %get-tuple-element.1609), channel_id=1, source_target_pairs={{0,1},{1,2},{2,3},{3,4},{4,5},{5,6},{6,7},{8,9},{9,10},{10,11},{11... | collective-permute-start | bytes 12296 | tf_op jit(solution)/shard_map/while/body/eval_jaxpr/ppermute | solution.py:17
  71.8 9.4 %collective-permute-start.4 = (bf16[1,1,32,64]{3,2,1,0:T(8,128)(2,1)S(1)}, bf16[1,1,32,64]{3,2,1,0:T(8,128)(2,1)S(1)}, u32[]{:S(2)}, u32[]{:S(2)}) collective-permute-start(bf16[1,1,32,64]{3,2,1,0:T(8,128)(2,1)S(1)} %get-tuple-element.1611), channel_id=1, source_target_pairs={{0,1},{1,2},{2,3},{3,4},{4,5},{5,6},{6,7},{8,9},{9,10},{10,11},{11... | collective-permute-start | bytes 12296 | tf_op jit(solution)/shard_map/while/body/eval_jaxpr/ppermute | solution.py:17
  75.4 6.2 %collective-permute-start.10 = (bf16[1,1,32,64]{3,2,1,0:T(8,128)(2,1)S(1)}, bf16[1,1,32,64]{3,2,1,0:T(8,128)(2,1)S(1)}, u32[]{:S(2)}, u32[]{:S(2)}) collective-permute-start(bf16[1,1,32,64]{3,2,1,0:T(8,128)(2,1)S(1)} %get-tuple-element.1624), channel_id=1, source_target_pairs={{1,0},{2,1},{3,2},{4,3},{5,4},{6,5},{7,6},{9,8},{10,9},{11,10},{12... | collective-permute-start | bytes 12296 | tf_op jit(solution)/shard_map/while/body/eval_jaxpr/ppermute | solution.py:19
  77.3 7.3 %collective-permute-start.9 = (bf16[1,1,32,64]{3,2,1,0:T(8,128)(2,1)S(1)}, bf16[1,1,32,64]{3,2,1,0:T(8,128)(2,1)S(1)}, u32[]{:S(2)}, u32[]{:S(2)}) collective-permute-start(bf16[1,1,32,64]{3,2,1,0:T(8,128)(2,1)S(1)} %get-tuple-element.1622), channel_id=1, source_target_pairs={{1,0},{2,1},{3,2},{4,3},{5,4},{6,5},{7,6},{9,8},{10,9},{11,10},{12... | collective-permute-start | bytes 12296 | tf_op jit(solution)/shard_map/while/body/eval_jaxpr/ppermute | solution.py:19
  79.3 8.3 %collective-permute-start.5 = (bf16[1,1,32,64]{3,2,1,0:T(8,128)(2,1)S(1)}, bf16[1,1,32,64]{3,2,1,0:T(8,128)(2,1)S(1)}, u32[]{:S(2)}, u32[]{:S(2)}) collective-permute-start(bf16[1,1,32,64]{3,2,1,0:T(8,128)(2,1)S(1)} %get-tuple-element.1613), channel_id=1, source_target_pairs={{1,0},{2,1},{3,2},{4,3},{5,4},{6,5},{7,6},{9,8},{10,9},{11,10},{12... | collective-permute-start | bytes 12296 | tf_op jit(solution)/shard_map/while/body/eval_jaxpr/ppermute | solution.py:19
  92.4 13.8 %collective-permute-start.6 = (bf16[1,64,32,64]{3,2,1,0:T(8,128)(2,1)S(1)}, bf16[1,64,32,64]{3,2,1,0:T(8,128)(2,1)S(1)}, u32[]{:S(2)}, u32[]{:S(2)}) collective-permute-start(bf16[1,64,32,64]{3,2,1,0:T(8,128)(2,1)S(1)} %fusion.298), channel_id=1, source_target_pairs={{0,8},{8,16},{16,24},{1,9},{9,17},{17,25},{2,10},{10,18},{18,26},{... | collective-permute-start | bytes 786440 | tf_op jit(solution)/shard_map/while/body/eval_jaxpr/ppermute | solution.py:29
  96.4 21.2 %copy-start.6 = (bf16[1,64,32,64]{3,2,1,0:T(8,128)(2,1)}, bf16[1,64,32,64]{3,2,1,0:T(8,128)(2,1)S(1)}, u32[]{:S(2)}) copy-start(bf16[1,64,32,64]{3,2,1,0:T(8,128)(2,1)S(1)} %fusion.301) | copy-start | bytes 786436 | tf_op jit(solution)/shard_map/while
  106.2 10.2 %copy-start.3 = (f32[2,3,3,64,64]{4,3,2,1,0:T(8,128)S(1)}, f32[2,3,3,64,64]{4,3,2,1,0:T(8,128)}, u32[]{:S(2)}) copy-start(f32[2,3,3,64,64]{4,3,2,1,0:T(8,128)} %get-tuple-element.1667) | copy-start | bytes 884740 | tf_op jit(solution)/shard_map/while
  106.2 10.2 %copy-start.8 = (f32[9,64,64]{2,1,0:T(8,128)S(1)}, f32[9,64,64]{2,1,0:T(8,128)}, u32[]{:S(2)}) copy-start(f32[9,64,64]{2,1,0:T(8,128)} %copy-done.7) | copy-start | bytes 442372 | tf_op jit(solution)/shard_map/while
  106.2 10.3 %copy-start.10 = (f32[9,64,64]{2,1,0:T(8,128)S(1)}, f32[9,64,64]{2,1,0:T(8,128)}, u32[]{:S(2)}) copy-start(f32[9,64,64]{2,1,0:T(8,128)} %copy-done.9) | copy-start | bytes 442372 | tf_op jit(solution)/shard_map/while
  107.6 9.1 %collective-permute-start.7 = (f32[1,1,24,64]{3,1,2,0:T(1,128)S(1)}, f32[1,1,24,64]{3,1,2,0:T(1,128)S(1)}, u32[]{:S(2)}, u32[]{:S(2)}) collective-permute-start(f32[1,1,24,64]{3,1,2,0:T(1,128)S(1)} %slice.546), channel_id=1, source_target_pairs={{1,0},{2,1},{3,2},{4,3},{5,4},{6,5},{7,6},{9,8},{10,9},{11,10},{12... | collective-permute-start | bytes 18440 | tf_op jit(solution)/shard_map/while/body/eval_jaxpr/ppermute | solution.py:19
  109.5 7.7 %collective-permute-start.8 = (f32[1,1,24,64]{3,2,1,0:T(8,128)S(1)}, f32[1,1,24,64]{3,2,1,0:T(8,128)S(1)}, u32[]{:S(2)}, u32[]{:S(2)}) collective-permute-start(f32[1,1,24,64]{3,2,1,0:T(8,128)S(1)} %bitcast.499), channel_id=1, source_target_pairs={{0,1},{1,2},{2,3},{3,4},{4,5},{5,6},{6,7},{8,9},{9,10},{10,11},{11... | collective-permute-start | bytes 18440 | tf_op jit(solution)/shard_map/while/body/eval_jaxpr/ppermute | solution.py:17
  119.1 9.9 %collective-permute-start = (bf16[1,1,32,64]{3,2,1,0:T(8,128)(2,1)S(1)}, bf16[1,1,32,64]{3,2,1,0:T(8,128)(2,1)S(1)}, u32[]{:S(2)}, u32[]{:S(2)}) collective-permute-start(bf16[1,1,32,64]{3,2,1,0:T(8,128)(2,1)S(1)} %get-tuple-element.1604), channel_id=1, source_target_pairs={{0,1},{1,2},{2,3},{3,4},{4,5},{5,6},{6,7},{8,9},{9,10},{10,11},{11... | collective-permute-start | bytes 12296 | tf_op jit(solution)/shard_map/while/body/eval_jaxpr/ppermute | solution.py:17
  122.9 6.3 %collective-permute-start.1 = (bf16[1,1,32,64]{3,2,1,0:T(8,128)(2,1)S(1)}, bf16[1,1,32,64]{3,2,1,0:T(8,128)(2,1)S(1)}, u32[]{:S(2)}, u32[]{:S(2)}) collective-permute-start(bf16[1,1,32,64]{3,2,1,0:T(8,128)(2,1)S(1)} %get-tuple-element.1605), channel_id=1, source_target_pairs={{1,0},{2,1},{3,2},{4,3},{5,4},{6,5},{7,6},{9,8},{10,9},{11,10},{12... | collective-permute-start | bytes 12296 | tf_op jit(solution)/shard_map/while/body/eval_jaxpr/ppermute | solution.py:19
  135.6 13.1 %collective-permute-start.2 = (bf16[1,1,32,64]{3,2,1,0:T(8,128)(2,1)S(1)}, bf16[1,1,32,64]{3,2,1,0:T(8,128)(2,1)S(1)}, u32[]{:S(2)}, u32[]{:S(2)}) collective-permute-start(bf16[1,1,32,64]{3,2,1,0:T(8,128)(2,1)S(1)} %get-tuple-element.1607), channel_id=1, source_target_pairs={{0,1},{1,2},{2,3},{3,4},{4,5},{5,6},{6,7},{8,9},{9,10},{10,11},{11... | collective-permute-start | bytes 12296 | tf_op jit(solution)/shard_map/while/body/eval_jaxpr/ppermute | solution.py:17
  139.3 11.4 %collective-permute-start.3 = (bf16[1,1,32,64]{3,2,1,0:T(8,128)(2,1)S(1)}, bf16[1,1,32,64]{3,2,1,0:T(8,128)(2,1)S(1)}, u32[]{:S(2)}, u32[]{:S(2)}) collective-permute-start(bf16[1,1,32,64]{3,2,1,0:T(8,128)(2,1)S(1)} %get-tuple-element.1609), channel_id=1, source_target_pairs={{0,1},{1,2},{2,3},{3,4},{4,5},{5,6},{6,7},{8,9},{9,10},{10,11},{11... | collective-permute-start | bytes 12296 | tf_op jit(solution)/shard_map/while/body/eval_jaxpr/ppermute | solution.py:17
  141.2 9.4 %collective-permute-start.4 = (bf16[1,1,32,64]{3,2,1,0:T(8,128)(2,1)S(1)}, bf16[1,1,32,64]{3,2,1,0:T(8,128)(2,1)S(1)}, u32[]{:S(2)}, u32[]{:S(2)}) collective-permute-start(bf16[1,1,32,64]{3,2,1,0:T(8,128)(2,1)S(1)} %get-tuple-element.1611), channel_id=1, source_target_pairs={{0,1},{1,2},{2,3},{3,4},{4,5},{5,6},{6,7},{8,9},{9,10},{10,11},{11... | collective-permute-start | bytes 12296 | tf_op jit(solution)/shard_map/while/body/eval_jaxpr/ppermute | solution.py:17
  144.8 6.2 %collective-permute-start.10 = (bf16[1,1,32,64]{3,2,1,0:T(8,128)(2,1)S(1)}, bf16[1,1,32,64]{3,2,1,0:T(8,128)(2,1)S(1)}, u32[]{:S(2)}, u32[]{:S(2)}) collective-permute-start(bf16[1,1,32,64]{3,2,1,0:T(8,128)(2,1)S(1)} %get-tuple-element.1624), channel_id=1, source_target_pairs={{1,0},{2,1},{3,2},{4,3},{5,4},{6,5},{7,6},{9,8},{10,9},{11,10},{12... | collective-permute-start | bytes 12296 | tf_op jit(solution)/shard_map/while/body/eval_jaxpr/ppermute | solution.py:19
  146.8 7.3 %collective-permute-start.9 = (bf16[1,1,32,64]{3,2,1,0:T(8,128)(2,1)S(1)}, bf16[1,1,32,64]{3,2,1,0:T(8,128)(2,1)S(1)}, u32[]{:S(2)}, u32[]{:S(2)}) collective-permute-start(bf16[1,1,32,64]{3,2,1,0:T(8,128)(2,1)S(1)} %get-tuple-element.1622), channel_id=1, source_target_pairs={{1,0},{2,1},{3,2},{4,3},{5,4},{6,5},{7,6},{9,8},{10,9},{11,10},{12... | collective-permute-start | bytes 12296 | tf_op jit(solution)/shard_map/while/body/eval_jaxpr/ppermute | solution.py:19
  148.7 8.3 %collective-permute-start.5 = (bf16[1,1,32,64]{3,2,1,0:T(8,128)(2,1)S(1)}, bf16[1,1,32,64]{3,2,1,0:T(8,128)(2,1)S(1)}, u32[]{:S(2)}, u32[]{:S(2)}) collective-permute-start(bf16[1,1,32,64]{3,2,1,0:T(8,128)(2,1)S(1)} %get-tuple-element.1613), channel_id=1, source_target_pairs={{1,0},{2,1},{3,2},{4,3},{5,4},{6,5},{7,6},{9,8},{10,9},{11,10},{12... | collective-permute-start | bytes 12296 | tf_op jit(solution)/shard_map/while/body/eval_jaxpr/ppermute | solution.py:19
  161.8 13.8 %collective-permute-start.6 = (bf16[1,64,32,64]{3,2,1,0:T(8,128)(2,1)S(1)}, bf16[1,64,32,64]{3,2,1,0:T(8,128)(2,1)S(1)}, u32[]{:S(2)}, u32[]{:S(2)}) collective-permute-start(bf16[1,64,32,64]{3,2,1,0:T(8,128)(2,1)S(1)} %fusion.298), channel_id=1, source_target_pairs={{0,8},{8,16},{16,24},{1,9},{9,17},{17,25},{2,10},{10,18},{18,26},{... | collective-permute-start | bytes 786440 | tf_op jit(solution)/shard_map/while/body/eval_jaxpr/ppermute | solution.py:29
  165.0 22.1 %copy-start.6 = (bf16[1,64,32,64]{3,2,1,0:T(8,128)(2,1)}, bf16[1,64,32,64]{3,2,1,0:T(8,128)(2,1)S(1)}, u32[]{:S(2)}) copy-start(bf16[1,64,32,64]{3,2,1,0:T(8,128)(2,1)S(1)} %fusion.301) | copy-start | bytes 786436 | tf_op jit(solution)/shard_map/while
  175.7 10.2 %copy-start.3 = (f32[2,3,3,64,64]{4,3,2,1,0:T(8,128)S(1)}, f32[2,3,3,64,64]{4,3,2,1,0:T(8,128)}, u32[]{:S(2)}) copy-start(f32[2,3,3,64,64]{4,3,2,1,0:T(8,128)} %get-tuple-element.1667) | copy-start | bytes 884740 | tf_op jit(solution)/shard_map/while
  175.7 10.2 %copy-start.8 = (f32[9,64,64]{2,1,0:T(8,128)S(1)}, f32[9,64,64]{2,1,0:T(8,128)}, u32[]{:S(2)}) copy-start(f32[9,64,64]{2,1,0:T(8,128)} %copy-done.7) | copy-start | bytes 442372 | tf_op jit(solution)/shard_map/while
  175.7 10.3 %copy-start.10 = (f32[9,64,64]{2,1,0:T(8,128)S(1)}, f32[9,64,64]{2,1,0:T(8,128)}, u32[]{:S(2)}) copy-start(f32[9,64,64]{2,1,0:T(8,128)} %copy-done.9) | copy-start | bytes 442372 | tf_op jit(solution)/shard_map/while
  177.1 9.1 %collective-permute-start.7 = (f32[1,1,24,64]{3,1,2,0:T(1,128)S(1)}, f32[1,1,24,64]{3,1,2,0:T(1,128)S(1)}, u32[]{:S(2)}, u32[]{:S(2)}) collective-permute-start(f32[1,1,24,64]{3,1,2,0:T(1,128)S(1)} %slice.546), channel_id=1, source_target_pairs={{1,0},{2,1},{3,2},{4,3},{5,4},{6,5},{7,6},{9,8},{10,9},{11,10},{12... | collective-permute-start | bytes 18440 | tf_op jit(solution)/shard_map/while/body/eval_jaxpr/ppermute | solution.py:19
  179.0 7.7 %collective-permute-start.8 = (f32[1,1,24,64]{3,2,1,0:T(8,128)S(1)}, f32[1,1,24,64]{3,2,1,0:T(8,128)S(1)}, u32[]{:S(2)}, u32[]{:S(2)}) collective-permute-start(f32[1,1,24,64]{3,2,1,0:T(8,128)S(1)} %bitcast.499), channel_id=1, source_target_pairs={{0,1},{1,2},{2,3},{3,4},{4,5},{5,6},{6,7},{8,9},{9,10},{10,11},{11... | collective-permute-start | bytes 18440 | tf_op jit(solution)/shard_map/while/body/eval_jaxpr/ppermute | solution.py:17
  188.6 9.9 %collective-permute-start = (bf16[1,1,32,64]{3,2,1,0:T(8,128)(2,1)S(1)}, bf16[1,1,32,64]{3,2,1,0:T(8,128)(2,1)S(1)}, u32[]{:S(2)}, u32[]{:S(2)}) collective-permute-start(bf16[1,1,32,64]{3,2,1,0:T(8,128)(2,1)S(1)} %get-tuple-element.1604), channel_id=1, source_target_pairs={{0,1},{1,2},{2,3},{3,4},{4,5},{5,6},{6,7},{8,9},{9,10},{10,11},{11... | collective-permute-start | bytes 12296 | tf_op jit(solution)/shard_map/while/body/eval_jaxpr/ppermute | solution.py:17
  192.4 6.3 %collective-permute-start.1 = (bf16[1,1,32,64]{3,2,1,0:T(8,128)(2,1)S(1)}, bf16[1,1,32,64]{3,2,1,0:T(8,128)(2,1)S(1)}, u32[]{:S(2)}, u32[]{:S(2)}) collective-permute-start(bf16[1,1,32,64]{3,2,1,0:T(8,128)(2,1)S(1)} %get-tuple-element.1605), channel_id=1, source_target_pairs={{1,0},{2,1},{3,2},{4,3},{5,4},{6,5},{7,6},{9,8},{10,9},{11,10},{12... | collective-permute-start | bytes 12296 | tf_op jit(solution)/shard_map/while/body/eval_jaxpr/ppermute | solution.py:19
  205.1 12.9 %collective-permute-start.2 = (bf16[1,1,32,64]{3,2,1,0:T(8,128)(2,1)S(1)}, bf16[1,1,32,64]{3,2,1,0:T(8,128)(2,1)S(1)}, u32[]{:S(2)}, u32[]{:S(2)}) collective-permute-start(bf16[1,1,32,64]{3,2,1,0:T(8,128)(2,1)S(1)} %get-tuple-element.1607), channel_id=1, source_target_pairs={{0,1},{1,2},{2,3},{3,4},{4,5},{5,6},{6,7},{8,9},{9,10},{10,11},{11... | collective-permute-start | bytes 12296 | tf_op jit(solution)/shard_map/while/body/eval_jaxpr/ppermute | solution.py:17
  208.8 11.1 %collective-permute-start.3 = (bf16[1,1,32,64]{3,2,1,0:T(8,128)(2,1)S(1)}, bf16[1,1,32,64]{3,2,1,0:T(8,128)(2,1)S(1)}, u32[]{:S(2)}, u32[]{:S(2)}) collective-permute-start(bf16[1,1,32,64]{3,2,1,0:T(8,128)(2,1)S(1)} %get-tuple-element.1609), channel_id=1, source_target_pairs={{0,1},{1,2},{2,3},{3,4},{4,5},{5,6},{6,7},{8,9},{9,10},{10,11},{11... | collective-permute-start | bytes 12296 | tf_op jit(solution)/shard_map/while/body/eval_jaxpr/ppermute | solution.py:17
  210.7 9.2 %collective-permute-start.4 = (bf16[1,1,32,64]{3,2,1,0:T(8,128)(2,1)S(1)}, bf16[1,1,32,64]{3,2,1,0:T(8,128)(2,1)S(1)}, u32[]{:S(2)}, u32[]{:S(2)}) collective-permute-start(bf16[1,1,32,64]{3,2,1,0:T(8,128)(2,1)S(1)} %get-tuple-element.1611), channel_id=1, source_target_pairs={{0,1},{1,2},{2,3},{3,4},{4,5},{5,6},{6,7},{8,9},{9,10},{10,11},{11... | collective-permute-start | bytes 12296 | tf_op jit(solution)/shard_map/while/body/eval_jaxpr/ppermute | solution.py:17
  214.1 6.2 %collective-permute-start.10 = (bf16[1,1,32,64]{3,2,1,0:T(8,128)(2,1)S(1)}, bf16[1,1,32,64]{3,2,1,0:T(8,128)(2,1)S(1)}, u32[]{:S(2)}, u32[]{:S(2)}) collective-permute-start(bf16[1,1,32,64]{3,2,1,0:T(8,128)(2,1)S(1)} %get-tuple-element.1624), channel_id=1, source_target_pairs={{1,0},{2,1},{3,2},{4,3},{5,4},{6,5},{7,6},{9,8},{10,9},{11,10},{12... | collective-permute-start | bytes 12296 | tf_op jit(solution)/shard_map/while/body/eval_jaxpr/ppermute | solution.py:19
  216.0 7.3 %collective-permute-start.9 = (bf16[1,1,32,64]{3,2,1,0:T(8,128)(2,1)S(1)}, bf16[1,1,32,64]{3,2,1,0:T(8,128)(2,1)S(1)}, u32[]{:S(2)}, u32[]{:S(2)}) collective-permute-start(bf16[1,1,32,64]{3,2,1,0:T(8,128)(2,1)S(1)} %get-tuple-element.1622), channel_id=1, source_target_pairs={{1,0},{2,1},{3,2},{4,3},{5,4},{6,5},{7,6},{9,8},{10,9},{11,10},{12... | collective-permute-start | bytes 12296 | tf_op jit(solution)/shard_map/while/body/eval_jaxpr/ppermute | solution.py:19
  218.0 8.3 %collective-permute-start.5 = (bf16[1,1,32,64]{3,2,1,0:T(8,128)(2,1)S(1)}, bf16[1,1,32,64]{3,2,1,0:T(8,128)(2,1)S(1)}, u32[]{:S(2)}, u32[]{:S(2)}) collective-permute-start(bf16[1,1,32,64]{3,2,1,0:T(8,128)(2,1)S(1)} %get-tuple-element.1613), channel_id=1, source_target_pairs={{1,0},{2,1},{3,2},{4,3},{5,4},{6,5},{7,6},{9,8},{10,9},{11,10},{12... | collective-permute-start | bytes 12296 | tf_op jit(solution)/shard_map/while/body/eval_jaxpr/ppermute | solution.py:19
  231.1 14.1 %collective-permute-start.6 = (bf16[1,64,32,64]{3,2,1,0:T(8,128)(2,1)S(1)}, bf16[1,64,32,64]{3,2,1,0:T(8,128)(2,1)S(1)}, u32[]{:S(2)}, u32[]{:S(2)}) collective-permute-start(bf16[1,64,32,64]{3,2,1,0:T(8,128)(2,1)S(1)} %fusion.298), channel_id=1, source_target_pairs={{0,8},{8,16},{16,24},{1,9},{9,17},{17,25},{2,10},{10,18},{18,26},{... | collective-permute-start | bytes 786440 | tf_op jit(solution)/shard_map/while/body/eval_jaxpr/ppermute | solution.py:29
  233.9 22.4 %copy-start.6 = (bf16[1,64,32,64]{3,2,1,0:T(8,128)(2,1)}, bf16[1,64,32,64]{3,2,1,0:T(8,128)(2,1)S(1)}, u32[]{:S(2)}) copy-start(bf16[1,64,32,64]{3,2,1,0:T(8,128)(2,1)S(1)} %fusion.301) | copy-start | bytes 786436 | tf_op jit(solution)/shard_map/while
  245.2 10.0 %copy-start.10 = (f32[9,64,64]{2,1,0:T(8,128)S(1)}, f32[9,64,64]{2,1,0:T(8,128)}, u32[]{:S(2)}) copy-start(f32[9,64,64]{2,1,0:T(8,128)} %copy-done.9) | copy-start | bytes 442372 | tf_op jit(solution)/shard_map/while
  246.5 8.9 %collective-permute-start.7 = (f32[1,1,24,64]{3,1,2,0:T(1,128)S(1)}, f32[1,1,24,64]{3,1,2,0:T(1,128)S(1)}, u32[]{:S(2)}, u32[]{:S(2)}) collective-permute-start(f32[1,1,24,64]{3,1,2,0:T(1,128)S(1)} %slice.546), channel_id=1, source_target_pairs={{1,0},{2,1},{3,2},{4,3},{5,4},{6,5},{7,6},{9,8},{10,9},{11,10},{12... | collective-permute-start | bytes 18440 | tf_op jit(solution)/shard_map/while/body/eval_jaxpr/ppermute | solution.py:19
  248.5 7.5 %collective-permute-start.8 = (f32[1,1,24,64]{3,2,1,0:T(8,128)S(1)}, f32[1,1,24,64]{3,2,1,0:T(8,128)S(1)}, u32[]{:S(2)}, u32[]{:S(2)}) collective-permute-start(f32[1,1,24,64]{3,2,1,0:T(8,128)S(1)} %bitcast.499), channel_id=1, source_target_pairs={{0,1},{1,2},{2,3},{3,4},{4,5},{5,6},{6,7},{8,9},{9,10},{10,11},{11... | collective-permute-start | bytes 18440 | tf_op jit(solution)/shard_map/while/body/eval_jaxpr/ppermute | solution.py:17
  257.8 9.9 %collective-permute-start = (bf16[1,1,32,64]{3,2,1,0:T(8,128)(2,1)S(1)}, bf16[1,1,32,64]{3,2,1,0:T(8,128)(2,1)S(1)}, u32[]{:S(2)}, u32[]{:S(2)}) collective-permute-start(bf16[1,1,32,64]{3,2,1,0:T(8,128)(2,1)S(1)} %get-tuple-element.1604), channel_id=1, source_target_pairs={{0,1},{1,2},{2,3},{3,4},{4,5},{5,6},{6,7},{8,9},{9,10},{10,11},{11... | collective-permute-start | bytes 12296 | tf_op jit(solution)/shard_map/while/body/eval_jaxpr/ppermute | solution.py:17
  261.6 6.3 %collective-permute-start.1 = (bf16[1,1,32,64]{3,2,1,0:T(8,128)(2,1)S(1)}, bf16[1,1,32,64]{3,2,1,0:T(8,128)(2,1)S(1)}, u32[]{:S(2)}, u32[]{:S(2)}) collective-permute-start(bf16[1,1,32,64]{3,2,1,0:T(8,128)(2,1)S(1)} %get-tuple-element.1605), channel_id=1, source_target_pairs={{1,0},{2,1},{3,2},{4,3},{5,4},{6,5},{7,6},{9,8},{10,9},{11,10},{12... | collective-permute-start | bytes 12296 | tf_op jit(solution)/shard_map/while/body/eval_jaxpr/ppermute | solution.py:19
  274.3 12.9 %collective-permute-start.2 = (bf16[1,1,32,64]{3,2,1,0:T(8,128)(2,1)S(1)}, bf16[1,1,32,64]{3,2,1,0:T(8,128)(2,1)S(1)}, u32[]{:S(2)}, u32[]{:S(2)}) collective-permute-start(bf16[1,1,32,64]{3,2,1,0:T(8,128)(2,1)S(1)} %get-tuple-element.1607), channel_id=1, source_target_pairs={{0,1},{1,2},{2,3},{3,4},{4,5},{5,6},{6,7},{8,9},{9,10},{10,11},{11... | collective-permute-start | bytes 12296 | tf_op jit(solution)/shard_map/while/body/eval_jaxpr/ppermute | solution.py:17
  278.0 11.1 %collective-permute-start.3 = (bf16[1,1,32,64]{3,2,1,0:T(8,128)(2,1)S(1)}, bf16[1,1,32,64]{3,2,1,0:T(8,128)(2,1)S(1)}, u32[]{:S(2)}, u32[]{:S(2)}) collective-permute-start(bf16[1,1,32,64]{3,2,1,0:T(8,128)(2,1)S(1)} %get-tuple-element.1609), channel_id=1, source_target_pairs={{0,1},{1,2},{2,3},{3,4},{4,5},{5,6},{6,7},{8,9},{9,10},{10,11},{11... | collective-permute-start | bytes 12296 | tf_op jit(solution)/shard_map/while/body/eval_jaxpr/ppermute | solution.py:17
  279.9 9.2 %collective-permute-start.4 = (bf16[1,1,32,64]{3,2,1,0:T(8,128)(2,1)S(1)}, bf16[1,1,32,64]{3,2,1,0:T(8,128)(2,1)S(1)}, u32[]{:S(2)}, u32[]{:S(2)}) collective-permute-start(bf16[1,1,32,64]{3,2,1,0:T(8,128)(2,1)S(1)} %get-tuple-element.1611), channel_id=1, source_target_pairs={{0,1},{1,2},{2,3},{3,4},{4,5},{5,6},{6,7},{8,9},{9,10},{10,11},{11... | collective-permute-start | bytes 12296 | tf_op jit(solution)/shard_map/while/body/eval_jaxpr/ppermute | solution.py:17
  283.3 6.2 %collective-permute-start.10 = (bf16[1,1,32,64]{3,2,1,0:T(8,128)(2,1)S(1)}, bf16[1,1,32,64]{3,2,1,0:T(8,128)(2,1)S(1)}, u32[]{:S(2)}, u32[]{:S(2)}) collective-permute-start(bf16[1,1,32,64]{3,2,1,0:T(8,128)(2,1)S(1)} %get-tuple-element.1624), channel_id=1, source_target_pairs={{1,0},{2,1},{3,2},{4,3},{5,4},{6,5},{7,6},{9,8},{10,9},{11,10},{12... | collective-permute-start | bytes 12296 | tf_op jit(solution)/shard_map/while/body/eval_jaxpr/ppermute | solution.py:19
  285.2 7.3 %collective-permute-start.9 = (bf16[1,1,32,64]{3,2,1,0:T(8,128)(2,1)S(1)}, bf16[1,1,32,64]{3,2,1,0:T(8,128)(2,1)S(1)}, u32[]{:S(2)}, u32[]{:S(2)}) collective-permute-start(bf16[1,1,32,64]{3,2,1,0:T(8,128)(2,1)S(1)} %get-tuple-element.1622), channel_id=1, source_target_pairs={{1,0},{2,1},{3,2},{4,3},{5,4},{6,5},{7,6},{9,8},{10,9},{11,10},{12... | collective-permute-start | bytes 12296 | tf_op jit(solution)/shard_map/while/body/eval_jaxpr/ppermute | solution.py:19
  287.2 8.3 %collective-permute-start.5 = (bf16[1,1,32,64]{3,2,1,0:T(8,128)(2,1)S(1)}, bf16[1,1,32,64]{3,2,1,0:T(8,128)(2,1)S(1)}, u32[]{:S(2)}, u32[]{:S(2)}) collective-permute-start(bf16[1,1,32,64]{3,2,1,0:T(8,128)(2,1)S(1)} %get-tuple-element.1613), channel_id=1, source_target_pairs={{1,0},{2,1},{3,2},{4,3},{5,4},{6,5},{7,6},{9,8},{10,9},{11,10},{12... | collective-permute-start | bytes 12296 | tf_op jit(solution)/shard_map/while/body/eval_jaxpr/ppermute | solution.py:19
  300.3 14.1 %collective-permute-start.6 = (bf16[1,64,32,64]{3,2,1,0:T(8,128)(2,1)S(1)}, bf16[1,64,32,64]{3,2,1,0:T(8,128)(2,1)S(1)}, u32[]{:S(2)}, u32[]{:S(2)}) collective-permute-start(bf16[1,64,32,64]{3,2,1,0:T(8,128)(2,1)S(1)} %fusion.298), channel_id=1, source_target_pairs={{0,8},{8,16},{16,24},{1,9},{9,17},{17,25},{2,10},{10,18},{18,26},{... | collective-permute-start | bytes 786440 | tf_op jit(solution)/shard_map/while/body/eval_jaxpr/ppermute | solution.py:29
  303.2 22.4 %copy-start.6 = (bf16[1,64,32,64]{3,2,1,0:T(8,128)(2,1)}, bf16[1,64,32,64]{3,2,1,0:T(8,128)(2,1)S(1)}, u32[]{:S(2)}) copy-start(bf16[1,64,32,64]{3,2,1,0:T(8,128)(2,1)S(1)} %fusion.301) | copy-start | bytes 786436 | tf_op jit(solution)/shard_map/while
  314.4 10.0 %copy-start.10 = (f32[9,64,64]{2,1,0:T(8,128)S(1)}, f32[9,64,64]{2,1,0:T(8,128)}, u32[]{:S(2)}) copy-start(f32[9,64,64]{2,1,0:T(8,128)} %copy-done.9) | copy-start | bytes 442372 | tf_op jit(solution)/shard_map/while
  315.8 8.9 %collective-permute-start.7 = (f32[1,1,24,64]{3,1,2,0:T(1,128)S(1)}, f32[1,1,24,64]{3,1,2,0:T(1,128)S(1)}, u32[]{:S(2)}, u32[]{:S(2)}) collective-permute-start(f32[1,1,24,64]{3,1,2,0:T(1,128)S(1)} %slice.546), channel_id=1, source_target_pairs={{1,0},{2,1},{3,2},{4,3},{5,4},{6,5},{7,6},{9,8},{10,9},{11,10},{12... | collective-permute-start | bytes 18440 | tf_op jit(solution)/shard_map/while/body/eval_jaxpr/ppermute | solution.py:19
  317.7 7.5 %collective-permute-start.8 = (f32[1,1,24,64]{3,2,1,0:T(8,128)S(1)}, f32[1,1,24,64]{3,2,1,0:T(8,128)S(1)}, u32[]{:S(2)}, u32[]{:S(2)}) collective-permute-start(f32[1,1,24,64]{3,2,1,0:T(8,128)S(1)} %bitcast.499), channel_id=1, source_target_pairs={{0,1},{1,2},{2,3},{3,4},{4,5},{5,6},{6,7},{8,9},{9,10},{10,11},{11... | collective-permute-start | bytes 18440 | tf_op jit(solution)/shard_map/while/body/eval_jaxpr/ppermute | solution.py:17
  (37 other events, 82.1 us)
Sparse Core Ops, SparseCore 0:
  326.2 53.9 all-reduce.4
where the time goes:
time: 395 us; the launch traced here: 389 us
  starting transfers between devices  136 us (34%)
  waiting for transfers between devices  86 us (22%)
  matrix products  43.2 us (11%)
  local copies, waits for them, and re-layouts  43 us (11%)
  other arithmetic  42.8 us (11%)
  between operations  23.6 us (6%)
  blocking collectives  11.5 us (3%)
    ppermute x22, starting transfers between devices, extended_2(): lax.ppermute(tail, axis, [(i, (i + 1) % count) for i in range(ends)])  84.7 us
    ppermute x4, waiting for transfers between devices, shifted_2(): return lax.ppermute(x, axis, pairs)  42.9 us
    ppermute x22, starting transfers between devices, extended_2(): lax.ppermute(head, axis, [((i + 1) % count, i) for i in range(ends)])  42.3 us
    psum x1, waiting for transfers between devices, local(): kernel_sum, bias_sum = lax.psum((final_state[2], final_state[3]), 'strip')  39.9 us
    dot_general x72, matrix products, weight_taps(): lax.dot_general(window, error, (((0, 1, 2), (0, 1, 2)), ((), ())), prefer...  22.9 us
    while x104, local copies, waits for them, and re-layouts  16.6 us
    conv_general_dilated x10, matrix products, conv_rows(): lax.conv_general_dilated(field_in, kernel, (1, 1), ((0, 0), (1, 1)), dime...  15 us
    psum x1, blocking collectives, local(): kernel_sum, bias_sum = lax.psum((final_state[2], final_state[3]), 'strip')  11.5 us
  transfers between devices with their start and end apart: 49, of which 10 were waited for; matrix products, arithmetic and copies ran while one was open for 14% of the time, Pallas kernels for 0%

commit v1 on v0

v1 whole, which is shorter than its diff:
```python
import functools
import math

import jax
import jax.numpy as jnp
import numpy as np
from jax import lax
from jax.experimental import pallas as pl
from jax.experimental.pallas import tpu as pltpu
from jax.sharding import PartitionSpec as P

LEAK = 0.05
LANES = 128
F32 = jnp.float32
BF16 = jnp.bfloat16
TAPS = 9
VMEM_BYTES = 56 * 1024 * 1024


def up_to(value, step):
    return -(-value // step) * step


class Level:
    def __init__(self, level, rows, cols):
        self.level = level
        self.rows = rows * 3**level // 4**level
        self.cols = cols * 3**level // 4**level
        self.pairs = -(-self.cols // 2)
        self.odd_pairs = -(-(self.cols + 1) // 2)

    def margin(self, error):
        self.error = error
        self.x_margin = error + 2
        self.x_rows = self.rows + 2 * (error + 2)
        self.hidden_rows = up_to(self.rows + 2 * (error + 1), 16)
        self.out_rows = up_to(self.rows + 2 * error, 16)
        self.in_rows = up_to(self.rows + 2 * (error - 1), 16)
        self.back_rows = up_to(self.rows + 2 * (error - 2), 16)
        self.own_rows = up_to(self.rows, 16)
        self.alloc = up_to(max(self.hidden_rows, self.x_margin + self.own_rows + 2) + 2, 8)


def levels_of(rows, cols, count):
    levels = [Level(s, rows, cols) for s in range(count)]
    levels[-1].margin(2)
    for s in range(count - 2, -1, -1):
        fine, coarse = levels[s], levels[s + 1]
        first = -coarse.error
        last = coarse.rows + coarse.error - 1
        low = 4 * (first // 3) + (-1, 1, 2)[first % 3]
        high = 4 * (last // 3) + (1, 2, 4)[last % 3]
        fine.margin(max(-low, high - fine.rows + 1) + 2)
        fine.k_first = first // 3
        fine.k_count = up_to(last // 3 - fine.k_first + 1, 8)
        fine.up_shift = -3 * fine.k_first - coarse.error
        start = fine.error - 2 + 4 * fine.k_first - 1
        fine.gu_row = max(0, -start)
        fine.gu_start = start + fine.gu_row
        assert fine.rows % 4 == 0
    return levels


def column_weights(fine, coarse):
    matrix = np.zeros((coarse, fine), np.float32)
    for x in range(fine):
        num = max((2 * x + 1) * coarse - fine, 0)
        low = num // (2 * fine)
        frac = np.float32(num - 2 * fine * low) / np.float32(2 * fine)
        matrix[low, x] += np.float32(1.0) - frac
        matrix[min(low + 1, coarse - 1), x] += frac
    return matrix


def lane_index(shape):
    return lax.broadcasted_iota(jnp.int32, shape, len(shape) - 1)


def half_swap(value):
    return pltpu.roll(value, LANES // 2, value.ndim - 1)


def twice(bias):
    return jnp.concatenate([bias, bias], axis=1)


def rounded(value):
    return value.astype(BF16).astype(F32)


def image_mask(level, base, count, strip, strips):
    row = lax.broadcasted_iota(jnp.int32, (1, count, LANES), 1) + base
    low = jnp.where(strip == 0, 0, -(10**6))
    high = jnp.where(strip == strips - 1, level.rows, 10**6)
    return (row >= low) & (row < high)


def odd_column_mask(level, first, count, mask):
    if first > 0 and 2 * (first + count - 1) < level.cols:
        return mask
    shape = (count, mask.shape[1], LANES)
    half = lax.broadcasted_iota(jnp.int32, shape, 2) // (LANES // 2)
    col = 2 * (first + lax.broadcasted_iota(jnp.int32, shape, 0)) - 1 + half
    return mask & (col >= 0) & (col < level.cols)


def conv(source, kernel, count, rows, chunk, emit):
    for first in range(0, count, chunk):
        size = min(chunk, count - first)
        parts = []
        for dy in range(3):
            block = source[first : first + size + 1, dy : dy + rows, :].astype(BF16)
            parts.append(block[:size].reshape(size * rows, LANES))
            parts.append(block[1:].reshape(size * rows, LANES))
        stacked = jnp.concatenate(parts, axis=1)
        result = jnp.dot(stacked, kernel[...], preferred_element_type=F32)
        emit(first, size, result.reshape(size, rows, LANES))


def kernel_terms(source, error, count, source_row, error_row, level):
    rows = level.own_rows
    err = error[0:count, error_row : error_row + rows, :]
    if rows != level.rows:
        row = lax.broadcasted_iota(jnp.int32, (1, rows, LANES), 1)
        err = jnp.where(row < level.rows, err, 0.0)
    total = jnp.sum(err, axis=(0, 1)).reshape(1, LANES)
    parts = []
    for dy in range(3):
        block = source[0 : count + 1, source_row + dy : source_row + dy + rows, :].astype(BF16)
        parts.append(block[:count].reshape(count * rows, LANES))
        parts.append(block[1:].reshape(count * rows, LANES))
    stacked = jnp.concatenate(parts, axis=1)
    product = lax.dot_general(
        err.astype(BF16).reshape(count * rows, LANES),
        stacked,
        (((0,), (0,)), ((), ())),
        preferred_element_type=F32,
    )
    return product, total


def pack_kernel_terms(out_ref, product, total, scale):
    half = LANES // 2
    by_tap = product.T * scale
    lane = lane_index((1, LANES))
    for dy in range(3):
        block = by_tap[dy * 2 * LANES : (dy + 1) * 2 * LANES]
        folded = block[: 3 * half] + half_swap(block)[half:]
        out_ref[dy * 96 : dy * 96 + 96, :] = jnp.where(lane < half, folded[:96], half_swap(folded[96:]))
    bias = (total + half_swap(total)) * scale
    out_ref[288:304, :] = jnp.broadcast_to(bias, (16, LANES))


def toeplitz(taps):
    half = LANES // 2
    zero = jnp.zeros((half, half), F32)
    rows = []
    for dy in range(3):
        for k in range(4):
            left = taps[dy * 3 + k] if k < 3 else zero
            right = taps[dy * 3 + k - 1] if k > 0 else zero
            rows.append(jnp.concatenate([left, right], axis=1))
    return jnp.concatenate(rows, axis=0)


def toeplitz_back(taps):
    half = LANES // 2
    zero = jnp.zeros((half, half), F32)
    columns = []
    for dy in range(3):
        for k in range(4):
            top = taps[(2 - dy) * 3 + 2 - k] if k < 3 else zero
            bottom = taps[(2 - dy) * 3 + 3 - k] if k > 0 else zero
            columns.append(jnp.concatenate([top, bottom], axis=0))
    pairs = [jnp.concatenate(columns[i : i + 2], axis=1).T for i in range(0, 12, 2)]
    return jnp.concatenate(pairs, axis=0)


def forward(level, xb, hb, kernels, bias, d_in, d_out, strip, strips, chunk, hidden_out=None):
    base = -(level.error + 1)
    mask = image_mask(level, base, level.hidden_rows, strip, strips)
    if level.alloc > level.hidden_rows:
        hb[0 : level.pairs + 1, level.hidden_rows : level.alloc, :] = jnp.zeros(
            (level.pairs + 1, level.alloc - level.hidden_rows, LANES), F32
        )
    if level.odd_pairs < level.pairs + 1:
        hb[level.odd_pairs : level.pairs + 1, 0 : level.alloc, :] = jnp.zeros(
            (level.pairs + 1 - level.odd_pairs, level.alloc, LANES), F32
        )
    bias_in, bias_out = bias[0:1], bias[1:2]

    def first_layer(first, size, value):
        pre = value + bias_in
        small = jnp.exp(-jnp.abs(pre))
        soft = jnp.maximum(pre, 0.0) + jnp.log(1.0 + small)
        act = LEAK * pre + (1.0 - LEAK) * soft
        keep = odd_column_mask(level, first, size, mask)
        hb[first : first + size, 0 : level.hidden_rows, :] = jnp.where(keep, rounded(act), 0.0)
        d_in[first : first + size, 0 : level.hidden_rows, :] = slope(pre)

    conv(xb, kernels[0], level.odd_pairs, level.hidden_rows, chunk, first_layer)

    def second_layer(first, size, value):
        d_out(first, size, slope(value + bias_out))

    conv(hb, kernels[1], level.pairs, level.out_rows, chunk, second_layer)


def slope(value):
    return LEAK + (1.0 - LEAK) * (0.5 + 0.5 * jnp.tanh(0.5 * value))


def backward(level, eo, ei, kernels, d_in, grad, grad_row, noise, gu, bi, strip, strips, chunk):
    mask_in = image_mask(level, -(level.error - 1), level.in_rows, strip, strips)
    if level.odd_pairs < level.pairs + 1:
        ei[level.odd_pairs : level.pairs + 1, 0 : level.alloc, :] = jnp.zeros(
            (level.pairs + 1 - level.odd_pairs, level.alloc, LANES), F32
        )

    def inner(first, size, value):
        keep = odd_column_mask(level, first, size, mask_in)
        part = d_in[first : first + size, 2 : 2 + level.in_rows, :]
        ei[first : first + size, 0 : level.in_rows, :] = jnp.where(keep, rounded(value * part), 0.0)

    conv(eo, kernels[1], level.odd_pairs, level.in_rows, chunk, inner)
    mask_back = image_mask(level, -(level.error - 2), level.back_rows, strip, strips)

    def outer(first, size, value):
        if noise is not None:
            bi[first : first + size, 0 : level.back_rows, :] = value
        if gu is not None:
            part = grad[first : first + size, grad_row + 2 : grad_row + 2 + level.back_rows, :]
            gu[first : first + size, level.gu_row : level.gu_row + level.back_rows, :] = jnp.where(mask_back, rounded(part + value), 0.0)

    conv(ei, kernels[0], level.pairs, level.back_rows, chunk, outer)
    if noise is not None:
        total_rows = noise.shape[0]
        row = lax.broadcasted_iota(jnp.int32, (level.own_rows, LANES), 0)
        lane = lane_index((level.own_rows, LANES))
        for p in range(noise.shape[1] // LANES):
            at = slice(p * LANES, (p + 1) * LANES)
            if p < level.pairs:
                part = bi[p, level.error - 2 : level.error - 2 + level.own_rows, :]
                if level.own_rows != level.rows:
                    part = jnp.where(row < level.rows, part, 0.0)
                if 2 * p + 1 >= level.cols:
                    part = jnp.where(lane < LANES // 2, part, 0.0)
                noise[0 : level.own_rows, at] = part.astype(BF16)
                if level.own_rows < total_rows:
                    noise[level.own_rows : total_rows, at] = jnp.zeros((total_rows - level.own_rows, LANES), BF16)
            else:
                noise[:, at] = jnp.zeros((total_rows, LANES), BF16)


def coarsen(fine, coarse, gu, rc, emit, strip, strips):
    count = fine.k_count
    start = fine.gu_start
    for p in range(fine.pairs):
        f = [gu[p, pl.ds(start + a, count, stride=4), :] for a in range(6)]
        rc[p, pl.ds(0, count, stride=3), :] = 0.125 * f[0] + 0.875 * f[1] + 0.375 * f[2]
        rc[p, pl.ds(1, count, stride=3), :] = 0.625 * f[2] + 0.625 * f[3]
        rc[p, pl.ds(2, count, stride=3), :] = 0.375 * f[3] + 0.875 * f[4] + 0.125 * f[5]
    top = -3 * fine.k_first
    low = top + coarse.rows - 1
    on_top = jnp.where(strip == 0, 1.0, 0.0).astype(F32)
    on_low = jnp.where(strip == strips - 1, 1.0, 0.0).astype(F32)
    all_pairs = slice(0, fine.pairs)
    rc[all_pairs, top : top + 1, :] = rc[all_pairs, top : top + 1, :] + on_top * rc[all_pairs, top - 1 : top, :]
    rc[all_pairs, low : low + 1, :] = rc[all_pairs, low : low + 1, :] + on_low * rc[all_pairs, low + 1 : low + 2, :]
    matrix = column_weights(fine.cols, coarse.cols)
    matrix = np.pad(matrix, ((0, 2 * coarse.pairs - coarse.cols), (0, 2 * fine.pairs - fine.cols)))
    lane = lane_index((1, LANES))

    def weights(low_lanes, high_lanes):
        return jnp.where(lane < LANES // 2, np.float32(low_lanes), np.float32(high_lanes))

    for m in range(coarse.pairs):
        total = None
        for q in range(fine.pairs):
            same = (matrix[2 * m, 2 * q], matrix[2 * m + 1, 2 * q + 1])
            cross = (matrix[2 * m, 2 * q + 1], matrix[2 * m + 1, 2 * q])
            value = rc[q, 0 : 3 * count, :] if any(same) or any(cross) else None
            for pair, moved in ((same, False), (cross, True)):
                if any(pair):
                    term = (half_swap(value) if moved else value) * weights(*pair)
                    total = term if total is None else total + term
        emit(m, total)


def fill_input(level, xb, act, top, low, tmp, payload_rows):
    margin = level.x_margin
    zero = jnp.zeros((level.alloc, LANES), F32)
    xb[0, 0 : level.alloc, :] = zero
    xb[level.pairs + 1, 0 : level.alloc, :] = zero
    lane = lane_index((1, LANES))
    for p in range(level.pairs):
        at = slice(p * LANES, (p + 1) * LANES)
        upper, own, lower = top(at), act[0 : level.own_rows, at].astype(F32), low(at)
        if 2 * p + 1 >= level.cols:
            upper, own, lower = (jnp.where(lane < LANES // 2, v, 0.0) for v in (upper, own, lower))
        end = margin + level.rows
        if end + margin < level.alloc:
            xb[p + 1, end + margin : level.alloc, :] = jnp.zeros((level.alloc - end - margin, LANES), F32)
        tmp[0, 0:32, :] = upper
        tmp[1, 0:32, :] = lower
        xb[p + 1, 0:margin, :] = tmp[0, payload_rows - margin : payload_rows, :]
        xb[p + 1, margin : margin + level.own_rows, :] = own
        xb[p + 1, end : end + margin, :] = tmp[1, 0:margin, :]
        after = up_to(end + margin, 1)
        if margin + level.own_rows > after:
            xb[p + 1, after : margin + level.own_rows, :] = jnp.zeros((margin + level.own_rows - after, LANES), F32)


def flat_to_pairs(level, flat, xb):
    zero = jnp.zeros((level.alloc, LANES), F32)
    xb[0, 0 : level.alloc, :] = zero
    xb[level.pairs + 1, 0 : level.alloc, :] = zero
    for p in range(level.pairs):
        xb[p + 1, 0 : level.x_rows, :] = flat[p * level.x_rows : (p + 1) * level.x_rows, :]
        if level.alloc > level.x_rows:
            xb[p + 1, level.x_rows : level.alloc, :] = jnp.zeros((level.alloc - level.x_rows, LANES), F32)


def call(body, out_shape, scratch, operands, flops, nbytes):
    return pl.pallas_call(
        body,
        out_shape=out_shape,
        in_specs=[pl.BlockSpec(memory_space=pltpu.VMEM)] * len(operands),
        out_specs=[pl.BlockSpec(memory_space=pltpu.VMEM)] * len(out_shape),
        scratch_shapes=scratch,
        compiler_params=pltpu.CompilerParams(vmem_limit_bytes=VMEM_BYTES),
        cost_estimate=pl.CostEstimate(flops=flops, bytes_accessed=nbytes, transcendentals=0),
    )(*operands)


def sds(shape, dtype):
    return jax.ShapeDtypeStruct(shape, dtype)


def buffer(level, extra):
    return pltpu.VMEM((level.pairs + extra, level.alloc, LANES), F32)


def local(strips, sections, cotangent, activations, weights, biases):
    row_count, flat_width = activations.shape[2:]
    channels = weights.shape[-1]
    cols = flat_width // channels
    assert 2 * channels == LANES and sections == 4 and cotangent.shape[0] == 1
    levels = levels_of(row_count, cols, sections)
    fine, second, third, last = levels
    x_margin, g_margin = fine.x_margin, fine.error
    payload = up_to(x_margin + g_margin, 16)
    pair_count = fine.pairs
    cot = cotangent[0]
    act = activations[0, 0]
    taps = weights.reshape(2 * TAPS, channels, channels)
    bias = biases[0]
    chunk = 4

    def ids():
        return lax.axis_index("section"), lax.axis_index("strip")

    def halo_body(act_ref, cot_ref, swap_ref, cross_ref, xs, cs, ts):
        section, strip = ids()
        odd = lax.rem(strip, 2) == 1
        live = jnp.int32(fine.rows)
        for level in levels[1:]:
            live = jnp.where(section == level.level, level.rows, live)
        for p in range(pair_count):
            at = slice(p * LANES, (p + 1) * LANES)
            xs[p, :, :] = act_ref[:, at].astype(F32)
            cs[p, :, :] = cot_ref[:, at].astype(F32)
            ts[0, p, 0:x_margin, :] = xs[p, 0:x_margin, :]
            ts[0, p, x_margin : x_margin + g_margin, :] = cs[p, 0:g_margin, :]
            ts[1, p, 0:x_margin, :] = xs[p, pl.ds(live - x_margin, x_margin), :]
            ts[1, p, x_margin : x_margin + g_margin, :] = cs[p, row_count - g_margin : row_count, :]
            upper = ts[0, p, 0:payload, :]
            lower = ts[1, p, 0:payload, :]
            swap_ref[:, at] = jnp.where(odd, upper, lower).astype(BF16)
            cross_ref[:, at] = jnp.where(odd, lower, upper).astype(BF16)

    halo_shape = sds((payload, flat_width), BF16)
    to_swap, to_cross = call(
        halo_body,
        [halo_shape, halo_shape],
        [
            pltpu.VMEM((pair_count, row_count, LANES), F32),
            pltpu.VMEM((pair_count, row_count, LANES), F32),
            pltpu.VMEM((2, pair_count, payload, LANES), F32),
        ],
        [act, cot],
        10**6,
        10**6,
    )
    swap_pairs = [(i, i ^ 1) for i in range(strips)]
    cross_pairs = [(i, i + 1) for i in range(1, strips - 1, 2)] + [(i + 1, i) for i in range(1, strips - 1, 2)]
    from_cross = lax.ppermute(to_cross, "strip", cross_pairs)
    from_swap = lax.ppermute(to_swap, "strip", swap_pairs)

    def expand(tap_list, forward_ref, back_ref):
        for c in range(2):
            chosen = tap_list[c * TAPS : (c + 1) * TAPS]
            forward_ref[c, :, :] = toeplitz(chosen).astype(BF16)
            back_ref[c, :, :] = toeplitz_back(chosen).astype(BF16)

    def matrix_body(taps_ref, forward_ref, back_ref, packed_ref):
        values = [taps_ref[t].astype(F32) for t in range(2 * TAPS)]
        expand(values, forward_ref, back_ref)
        half = channels // 2
        for t in range(2 * TAPS):
            packed_ref[t * half : (t + 1) * half, :] = jnp.concatenate(
                [values[t][:half], values[t][half:]], axis=1
            ).astype(BF16)

    matrix_shape = sds((2, 6 * LANES, LANES), BF16)
    packed_rows = TAPS * channels
    fwd_own, back_own, packed_own = call(
        matrix_body,
        [matrix_shape, matrix_shape, sds((packed_rows, LANES), BF16)],
        [],
        [taps],
        10**6,
        10**6,
    )

    g_rows = second.rows + 2 * second.error
    g_flat = up_to(second.pairs * g_rows, 16)
    x_flat = up_to(max(second.pairs * second.x_rows, third.pairs * third.x_rows), 16)
    g_flat = max(g_flat, 16)
    ship_rows = max(x_flat + packed_rows, g_flat) + 16

    def halo_readers(swap_ref, cross_ref, strip):
        odd = lax.rem(strip, 2) == 1

        def top(at):
            return jnp.where(odd, swap_ref[:, at].astype(F32), cross_ref[:, at].astype(F32))

        def low(at):
            return jnp.where(odd, cross_ref[:, at].astype(F32), swap_ref[:, at].astype(F32))

        return top, low

    def chain_body(
        act_ref, cot_ref, swap_ref, cross_ref, fwd_ref, back_ref, packed_ref, bias_ref,
        hop_ref, ship_ref, noise_ref, hid_ref, ein_ref, eout_ref,
        xb, hb, db, gb, eo, ei, bi, gu, rc, flat, tmp, bias_tmp,
    ):
        section, strip = ids()
        top, low = halo_readers(swap_ref, cross_ref, strip)

        @pl.when(section == 0)
        def _():
            level = fine
            fill_input(level, xb, act_ref, top, low, tmp, x_margin)
            zero = jnp.zeros((level.alloc, LANES), F32)
            eo[0, 0 : level.alloc, :] = zero
            eo[level.pairs + 1, 0 : level.alloc, :] = zero
            for p in range(level.pairs):
                at = slice(p * LANES, (p + 1) * LANES)
                tmp[0, 0:payload, :] = top(at)
                tmp[1, 0:payload, :] = low(at)
                gb[p, 0:g_margin, :] = tmp[0, x_margin : x_margin + g_margin, :]
                gb[p, g_margin : g_margin + row_count, :] = cot_ref[:, at].astype(F32)
                gb[p, g_margin + row_count : 2 * g_margin + row_count, :] = tmp[
                    1, x_margin : x_margin + g_margin, :
                ]
            mask_out = image_mask(level, -level.error, level.out_rows, strip, strips)

            def error(first, size, value):
                part = gb[first : first + size, 0 : level.out_rows, :]
                eo[first + 1 : first + 1 + size, 0 : level.out_rows, :] = jnp.where(
                    mask_out, rounded(part * value), 0.0
                )

            forward(
                level, xb, hb, [fwd_ref.at[0], fwd_ref.at[1]], twice(bias_ref[...]), db, error, strip, strips, chunk
            )
            backward(
                level, eo, ei, [back_ref.at[0], back_ref.at[1]], db, gb, 0, noise_ref, gu, bi, strip, strips, chunk
            )

            def emit(m, rows):
                flat[m * g_rows : (m + 1) * g_rows, :] = rows[0:g_rows]

            coarsen(fine, second, gu, rc, emit, strip, strips)
            value = flat[0:g_flat, :].astype(BF16)
            hop_ref[...] = value
            ship_ref[0:g_flat, :] = value
            rows = level.rows
            for p in range(level.pairs + 1):
                hid_ref[p, :, :] = hb[p, level.error : level.error + rows + 16, :].astype(BF16)
                ein_ref[p, :, :] = ei[p, level.error - 1 : level.error - 1 + rows, :].astype(BF16)
                if p < level.pairs:
                    eout_ref[p, :, :] = eo[p + 1, level.error : level.error + rows, :].astype(BF16)

        for level in (second, third):

            @pl.when(section == level.level)
            def _(level=level):
                fill_input(level, xb, act_ref, top, low, tmp, x_margin)
                for p in range(level.pairs):
                    flat[p * level.x_rows : (p + 1) * level.x_rows, :] = xb[p + 1, 0 : level.x_rows, :]
                used = up_to(level.pairs * level.x_rows, 16)
                ship_ref[0:used, :] = flat[0:used, :].astype(BF16)
                ship_ref[x_flat : x_flat + packed_rows, :] = packed_ref[...]
                rest = twice(bias_ref[...])
                for term in range(3):
                    part = rounded(rest)
                    bias_tmp[2 * term : 2 * term + 2, :] = part
                    rest = rest - part
                bias_tmp[6:16, :] = jnp.zeros((10, LANES), F32)
                ship_ref[x_flat + packed_rows : ship_rows, :] = bias_tmp[...].astype(BF16)

    hop_shape = sds((g_flat, LANES), BF16)
    ship_shape = sds((ship_rows, LANES), BF16)
    hop, ship, noise_first, hid_first, ein_first, eout_first = call(
        chain_body,
        [
            hop_shape,
            ship_shape,
            sds((row_count, flat_width), BF16),
            sds((fine.pairs + 1, row_count + 16, LANES), BF16),
            sds((fine.pairs + 1, row_count, LANES), BF16),
            sds((fine.pairs, row_count, LANES), BF16),
        ],
        [
            buffer(fine, 2),
            buffer(fine, 1),
            buffer(fine, 1),
            buffer(fine, 0),
            buffer(fine, 2),
            buffer(fine, 1),
            buffer(fine, 0),
            buffer(fine, 0),
            pltpu.VMEM((fine.pairs, 3 * fine.k_count, LANES), F32),
            pltpu.VMEM((up_to(max(g_flat, x_flat), 8) + 16, LANES), F32),
            pltpu.VMEM((2, max(payload, 32), LANES), F32),
            pltpu.VMEM((16, LANES), F32),
        ],
        [act, cot, from_swap, from_cross, fwd_own, back_own, packed_own, bias],
        3 * 10**9,
        4 * 10**6,
    )

    def across(value, pairs):
        return lax.ppermute(value, "section", pairs)

    got_hop = across(hop, [(0, 3)])
    got_far = across(ship, [(0, 2), (1, 3)])
    got_near = across(ship, [(0, 1), (1, 2), (2, 3)])

    def forward_body(
        act_ref, swap_ref, cross_ref, fwd_ref, back_ref, bias_ref, far_ref, near_ref,
        din1, dout1, din2, dout2, din3, dout3, back1, back2, hid_ref, xown_ref,
        xb, hb, flat, fwd_tmp, tmp,
    ):
        section, strip = ids()
        top, low = halo_readers(swap_ref, cross_ref, strip)
        slots = {1: (din1, dout1, back1), 2: (din2, dout2, back2), 3: (din3, dout3, None)}

        def run(level, kernels, bias_rows):
            d_in, d_out, _ = slots[level.level]

            def store(first, size, value):
                d_out[first : first + size, 0 : level.out_rows, :] = value

            forward(level, xb, hb, kernels, bias_rows, d_in, store, strip, strips, chunk)

        def own(level):
            fill_input(level, xb, act_ref, top, low, tmp, x_margin)
            run(level, [fwd_ref.at[0], fwd_ref.at[1]], twice(bias_ref[...]))
            hid_ref[0 : level.pairs + 1, 0 : level.alloc, :] = hb[0 : level.pairs + 1, 0 : level.alloc, :]
            xown_ref[0 : level.pairs + 2, 0 : level.alloc, :] = xb[0 : level.pairs + 2, 0 : level.alloc, :]
            back = slots[level.level][2]
            if back is not None:
                back[...] = back_ref[...]

        def shipped(level, source):
            half = channels // 2
            values = []
            for t in range(2 * TAPS):
                pack = source[x_flat + t * half : x_flat + (t + 1) * half, :].astype(F32)
                values.append(jnp.concatenate([pack[:, :channels], pack[:, channels:]], axis=0))
            expand(values, fwd_tmp, slots[level.level][2])
            used = up_to(level.pairs * level.x_rows, 16)
            flat[0:used, :] = source[0:used, :].astype(F32)
            flat_to_pairs(level, flat, xb)
            terms = source[x_flat + packed_rows : ship_rows, :].astype(F32)
            run(level, [fwd_tmp.at[0], fwd_tmp.at[1]], terms[0:2] + terms[2:4] + terms[4:6])

        @pl.when(section == 1)
        def _():
            own(second)

        @pl.when(section == 2)
        def _():
            own(third)
            shipped(second, near_ref)

        @pl.when(section == 3)
        def _():
            own(last)
            shipped(second, far_ref)
            shipped(third, near_ref)

    def field(level, extra):
        return sds((level.pairs + extra, level.alloc, LANES), F32)

    outs = call(
        forward_body,
        [
            field(second, 1), field(second, 0),
            field(third, 1), field(third, 0),
            field(last, 1), field(last, 0),
            matrix_shape, matrix_shape,
            field(second, 1), field(second, 2),
        ],
        [
            buffer(second, 2),
            buffer(second, 1),
            pltpu.VMEM((x_flat + 16, LANES), F32),
            pltpu.VMEM((2, 6 * LANES, LANES), BF16),
            pltpu.VMEM((2, max(payload, 32), LANES), F32),
        ],
        [act, from_swap, from_cross, fwd_own, back_own, bias, got_far, got_near],
        2 * 10**9,
        4 * 10**6,
    )
    din1, dout1, din2, dout2, din3, dout3, back1, back2, hid_own, x_own = outs

    grad_rows = up_to(TAPS * channels // 2 + 1, 16)

    def backward_body(
        act_ref, swap_ref, cross_ref, noise0, hid0, ein0, eout0,
        hop_ref, far_ref, near_ref,
        din1, dout1, din2, dout2, din3, dout3, back1, back2, back3, hid_ref, x_ref,
        noise_ref, keep_ref, send_ref,
        xb, hb, gb, eo, ei, bi, gu, rc, flat, tmp, pair_out,
    ):
        section, strip = ids()
        odd = lax.rem(strip, 2) == 1
        slots = {1: (din1, dout1, back1), 2: (din2, dout2, back2), 3: (din3, dout3, back3)}

        def gradients(level, source, hidden, err_in, err_out, rows_at):
            scale = np.float32(1.0 / math.sqrt(strips * level.rows * level.cols))
            first = kernel_terms(source, err_in, level.odd_pairs, rows_at[2], rows_at[0], level)
            pack_kernel_terms(pair_out.at[0], *first, scale)
            then = kernel_terms(hidden, err_out, level.pairs, rows_at[3], rows_at[1], level)
            pack_kernel_terms(pair_out.at[1], *then, scale)

        def step(level, grad_row, keep):
            d_in, d_out, back = slots[level.level]
            mask = image_mask(level, -level.error, level.out_rows, strip, strips)
            zero = jnp.zeros((level.alloc, LANES), F32)
            eo[0, 0 : level.alloc, :] = zero
            eo[level.pairs + 1, 0 : level.alloc, :] = zero
            for p in range(level.pairs):
                part = gb[p, grad_row : grad_row + level.out_rows, :] * d_out[p, 0 : level.out_rows, :]
                eo[p + 1, 0 : level.out_rows, :] = jnp.where(mask[0], rounded(part), 0.0)
            backward(
                level, eo, ei, [back.at[0], back.at[1]], d_in, gb, grad_row,
                noise_ref if keep else None, None if keep else gu, bi, strip, strips, chunk,
            )

        def take(source):
            flat[0:g_flat, :] = source[0:g_flat, :].astype(F32)
            for p in range(second.pairs):
                gb[p, 0:g_rows, :] = flat[p * g_rows : (p + 1) * g_rows, :]

        def down(upper, lower):
            def emit(m, rows):
                gb[m, 0 : 3 * upper.k_count, :] = rounded(rows)

            coarsen(upper, lower, gu, rc, emit, strip, strips)

        def finish(level):
            gradients(
                level, x_ref, hid_ref, ei, eo.at[1 : 1 + level.pairs],
                (level.error - 1, level.error, level.error + 1, level.error),
            )

        @pl.when(section == 0)
        def _():
            noise_ref[...] = noise0[...]
            top, low = halo_readers(swap_ref, cross_ref, strip)
            fill_input(fine, xb, act_ref, top, low, tmp, x_margin)
            rows = fine.rows
            for p in range(fine.pairs + 1):
                hb[p, 0 : rows + 16, :] = hid0[p, :, :].astype(F32)
                ei[p, 0:rows, :] = ein0[p, :, :].astype(F32)
                if p < fine.pairs:
                    eo[p, 0:rows, :] = eout0[p, :, :].astype(F32)
            gradients(fine, xb, hb, ei, eo, (0, 0, fine.error + 1, 0))

        @pl.when(section == 1)
        def _():
            take(near_ref)
            step(second, 0, True)
            finish(second)

        @pl.when(section == 2)
        def _():
            take(far_ref)
            step(second, 0, False)
            down(second, third)
            step(third, second.up_shift, True)
            finish(third)

        @pl.when(section == 3)
        def _():
            take(hop_ref)
            step(second, 0, False)
            down(second, third)
            step(third, second.up_shift, False)
            down(third, last)
            step(last, third.up_shift, True)
            finish(last)

        first, then = pair_out[0], pair_out[1]
        keep_ref[...] = jnp.where(odd, then, first)
        send_ref[...] = jnp.where(odd, first, then)

    half_shape = sds((grad_rows, LANES), F32)
    noise, keep, send = call(
        backward_body,
        [sds((row_count, flat_width), BF16), half_shape, half_shape],
        [
            buffer(fine, 2),
            buffer(fine, 1),
            buffer(fine, 0),
            buffer(fine, 2),
            buffer(fine, 1),
            buffer(fine, 0),
            buffer(fine, 0),
            pltpu.VMEM((second.pairs, 3 * second.k_count, LANES), F32),
            pltpu.VMEM((g_flat + 16, LANES), F32),
            pltpu.VMEM((2, max(payload, 32), LANES), F32),
            pltpu.VMEM((2, grad_rows, LANES), F32),
        ],
        [
            act, from_swap, from_cross, noise_first, hid_first, ein_first, eout_first,
            got_hop, got_far, got_near,
            din1, dout1, din2, dout2, din3, dout3, back1, back2, back_own, hid_own, x_own,
        ],
        3 * 10**9,
        6 * 10**6,
    )

    total = keep + lax.ppermute(send, "strip", swap_pairs)
    hop_size = 2
    while hop_size < strips:
        mine = lax.reduce_precision(total, 8, 7)
        other = lax.ppermute(mine.astype(BF16), "strip", [(i, i ^ hop_size) for i in range(strips)])
        total = mine + other.astype(F32)
        hop_size *= 2
    other = lax.ppermute(total, "strip", swap_pairs)

    def final_body(mine_ref, other_ref, kernel_ref, bias_ref):
        _, strip = ids()
        odd = lax.rem(strip, 2) == 1
        half = channels
        for c in range(2):
            if c == 0:
                value = jnp.where(odd, other_ref[...], mine_ref[...])
            else:
                value = jnp.where(odd, mine_ref[...], other_ref[...])
            swapped = half_swap(value)
            for dy in range(3):
                kernel_ref[c, dy * 192 : dy * 192 + 96, :] = value[dy * 96 : dy * 96 + 96, :half]
                kernel_ref[c, dy * 192 + 96 : dy * 192 + 192, :] = swapped[dy * 96 : dy * 96 + 96, :half]
            bias_ref[c : c + 1, :] = value[288:289, :half]

    kernel_sum, bias_sum = call(
        final_body,
        [sds((2, TAPS * channels, channels), F32), sds((2, channels), F32)],
        [],
        [total, other],
        10**6,
        10**6,
    )
    return (
        noise[None, None],
        kernel_sum.reshape(1, 2, 3, 3, channels, channels),
        bias_sum[None],
    )


def solution(mesh):
    strips = mesh.shape["strip"]
    sections = mesh.shape["section"]
    return jax.shard_map(
        functools.partial(local, strips, sections),
        mesh=mesh,
        in_specs=(
            P(None, "strip", None),
            P("section", None, "strip", None),
            P("section", None, None, None, None, None),
            P("section", None, None),
        ),
        out_specs=(
            P("section", None, "strip", None),
            P("section", None, None, None, None, None),
            P("section", None, None),
        ),
        check_vma=False,
    )
```

time: 395 us -> 64.7 us (0.16); the launches traced: 389 us -> 64.4 us
  starting transfers between devices: 136 us -> 18.4 us
  waiting for transfers between devices: 86 us -> 21.2 us
  matrix products: 43.2 us -> 0 us
  other arithmetic: 42.8 us -> 1.08 us
  local copies, waits for them, and re-layouts: 43 us -> 2.75 us
  between operations: 23.6 us -> 0.71 us
  Pallas kernels: 0 us -> 20.2 us
  blocking collectives: 11.5 us -> 0 us
    ppermute x48 -> x9, starting transfers between devices: 136 us -> 18.4 us  [the longest x2 6.93 us: local(): lax.ppermute(mine.astype(BF16), 'strip', [(i, i ^ hop_size) for i in rang...]
    psum x1 -> x0, waiting for transfers between devices: 39.9 us -> none  [local(): kernel_sum, bias_sum = lax.psum((final_state[2], final_state[3]), 'strip')]
    dot_general x80 -> x0, matrix products: 28.2 us -> none  [the longest x72 22.9 us: weight_taps(): lax.dot_general(window, error, (((0, 1, 2), (0, 1, 2)), ((), ())), prefer...]
    ppermute x48 -> x9, waiting for transfers between devices: 46.1 us -> 21.2 us  [the longest x3 13.2 us: across(): return lax.ppermute(value, 'section', pairs)]
    pallas_call x0 -> x6, Pallas kernels: none -> 20.2 us  [call(): pl.pallas_call(body, out_shape=out_shape, in_specs=[pl.BlockSpec(memory_s...]
    while x104 -> x0, local copies, waits for them, and re-layouts: 16.6 us -> none
    conv_general_dilated x10 -> x0, matrix products: 15 us -> none  [conv_rows(): lax.conv_general_dilated(field_in, kernel, (1, 1), ((0, 0), (1, 1)), dime...]
    psum x1 -> x0, blocking collectives: 11.5 us -> none  [local(): kernel_sum, bias_sum = lax.psum((final_state[2], final_state[3]), 'strip')]
  transfers between devices with their start and end apart: 49 -> 9, of which waited for: 10 -> 7; matrix products, arithmetic and copies ran while one was open for 14% -> 0% of each run, Pallas kernels for 0% -> 11%
where the time goes in v1:
time: 64.7 us; the launch traced here: 64.4 us
  waiting for transfers between devices  21.2 us (33%)
  Pallas kernels  20.2 us (31%)
  starting transfers between devices  18.4 us (28%)
  local copies, waits for them, and re-layouts  2.75 us (4%)
  other arithmetic  1.08 us (2%)
  between operations  0.71 us (1%)
    pallas_call x6, Pallas kernels, call(): pl.pallas_call(body, out_shape=out_shape, in_specs=[pl.BlockSpec(memory_s...  20.2 us
    ppermute x3, waiting for transfers between devices, across(): return lax.ppermute(value, 'section', pairs)  13.2 us
    ppermute x2, starting transfers between devices, local(): lax.ppermute(mine.astype(BF16), 'strip', [(i, i ^ hop_size) for i in rang...  6.93 us
    ppermute x3, starting transfers between devices, across(): return lax.ppermute(value, 'section', pairs)  4.91 us
    ppermute x2, waiting for transfers between devices, local(): lax.ppermute(mine.astype(BF16), 'strip', [(i, i ^ hop_size) for i in rang...  4.42 us
    ppermute x1, starting transfers between devices, local(): from_cross = lax.ppermute(to_cross, 'strip', cross_pairs)  3.08 us
    unnamed x16, local copies, waits for them, and re-layouts  2.75 us
    ppermute x1, starting transfers between devices, local(): other = lax.ppermute(total, 'strip', swap_pairs)  2.46 us
  transfers between devices with their start and end apart: 9, of which 7 were waited for; matrix products, arithmetic and copies ran while one was open for 0% of the time, Pallas kernels for 11%

profile of v1, /device:TPU:5, one launch (start us, length us, event | category | flops | bytes accessed | tf_op | source)
XLA Modules:
  0.0 64.4 jit_solution(5903321318596464651)
XLA Ops:
  0.6 1.9 %shard_map.67 = (bf16[32,2048]{1,0:T(8,128)(2,1)}, bf16[32,2048]{1,0:T(8,128)(2,1)}) custom-call(bf16[64,2048]{1,0:T(8,128)(2,1)} %bitcast.10, bf16[64,2048]{1,0:T(8,128)(2,1)} %bitcast.8), custom_call_target="tpu_custom_call" | custom-call | flops 1000000 | bytes 1000000 | tf_op jit(solution)/shard_map/pallas_call | solution.py:325
  2.5 0.7 %collective-permute-start = (bf16[32,2048]{1,0:T(8,128)(2,1)}, bf16[32,2048]{1,0:T(8,128)(2,1)S(1)}, u32[]{:S(2)}, u32[]{:S(2)}) collective-permute-start(bf16[32,2048]{1,0:T(8,128)(2,1)} %get-tuple-element.29), channel_id=1, source_target_pairs={{0,1},{1,0},{2,3},{3,2},{4,5},{5,4},{6,7},{7,6},{8,9},{9,8},{10,11... | collective-permute-start | bytes 393224 | tf_op jit(solution)/shard_map/ppermute | solution.py:398
  3.2 3.1 %collective-permute-start.1 = (bf16[32,2048]{1,0:T(8,128)(2,1)}, bf16[32,2048]{1,0:T(8,128)(2,1)S(1)}, u32[]{:S(2)}, u32[]{:S(2)}) collective-permute-start(bf16[32,2048]{1,0:T(8,128)(2,1)} %get-tuple-element.30), channel_id=1, source_target_pairs={{1,2},{3,4},{5,6},{2,1},{4,3},{6,5},{9,10},{11,12},{13,14},{10,9},... | collective-permute-start | bytes 393224 | tf_op jit(solution)/shard_map/ppermute | solution.py:397
  6.3 2.1 %shard_map.68 = (bf16[2,768,128]{2,1,0:T(8,128)(2,1)}, bf16[2,768,128]{2,1,0:T(8,128)(2,1)}, bf16[576,128]{1,0:T(8,128)(2,1)}) custom-call(bf16[18,64,64]{2,1,0:T(8,128)(2,1)} %bitcast.7), custom_call_target="tpu_custom_call" | custom-call | flops 1000000 | bytes 1000000 | tf_op jit(solution)/shard_map/pallas_call | solution.py:325
  8.4 0.0 collective-permute-done.swap_ref
  8.4 0.0 copy-start.6
  8.4 1.3 %collective-permute-done.1.cross_ref = bf16[32,2048]{1,0:T(8,128)(2,1)S(1)} collective-permute-done((bf16[32,2048]{1,0:T(8,128)(2,1)}, bf16[32,2048]{1,0:T(8,128)(2,1)S(1)}, u32[]{:S(2)}, u32[]{:S(2)}) %collective-permute-start.1) | collective-permute-done | bytes 131104 | tf_op jit(solution)/shard_map/ppermute | solution.py:397
  9.7 0.0 copy-start.7
  9.7 0.0 copy-done.6
  9.7 0.6 %copy-done.7 = bf16[32,2048]{1,0:T(8,128)(2,1)} copy-done((bf16[32,2048]{1,0:T(8,128)(2,1)}, bf16[32,2048]{1,0:T(8,128)(2,1)S(1)}, u32[]{:S(2)}) %copy-start.7) | copy-done | bytes 131096
  10.3 2.8 %shard_map.69 = (bf16[800,128]{1,0:T(8,128)(2,1)}, bf16[1440,128]{1,0:T(8,128)(2,1)}, bf16[64,2048]{1,0:T(8,128)(2,1)}, bf16[17,80,128]{2,1,0:T(8,128)(2,1)}, bf...) custom-call(bf16[64,2048]{1,0:T(8,128)(2,1)} %bitcast.11, bf16[64,2048]{1,0:T(8,128)(2,1)} %bitcast.9, ...), custom_call_target="tpu_custom_call" | custom-call | flops 3000000000 | bytes 4000000 | tf_op jit(solution)/shard_map/pallas_call | solution.py:325
  13.1 2.9 %collective-permute-start.4 = (bf16[1440,128]{1,0:T(8,128)(2,1)}, bf16[1440,128]{1,0:T(8,128)(2,1)S(1)}, u32[]{:S(2)}, u32[]{:S(2)}) collective-permute-start(bf16[1440,128]{1,0:T(8,128)(2,1)} %get-tuple-element.39), channel_id=1, source_target_pairs={{0,8},{8,16},{16,24},{1,9},{9,17},{17,25},{2,10},{10,18},{18,26},{... | collective-permute-start | bytes 1105928 | tf_op jit(solution)/shard_map/ppermute | solution.py:546
  16.1 1.3 %collective-permute-start.3 = (bf16[1440,128]{1,0:T(8,128)(2,1)}, bf16[1440,128]{1,0:T(8,128)(2,1)S(1)}, u32[]{:S(2)}, u32[]{:S(2)}) collective-permute-start(bf16[1440,128]{1,0:T(8,128)(2,1)} %get-tuple-element.39), channel_id=1, source_target_pairs={{0,16},{8,24},{1,17},{9,25},{2,18},{10,26},{3,19},{11,27},{4,20},{... | collective-permute-start | bytes 1105928 | tf_op jit(solution)/shard_map/ppermute | solution.py:546
  17.4 0.7 %collective-permute-start.2 = (bf16[800,128]{1,0:T(8,128)(2,1)}, bf16[800,128]{1,0:T(8,128)(2,1)S(1)}, u32[]{:S(2)}, u32[]{:S(2)}) collective-permute-start(bf16[800,128]{1,0:T(8,128)(2,1)} %get-tuple-element.38), channel_id=1, source_target_pairs={{0,24},{1,25},{2,26},{3,27},{4,28},{5,29},{6,30},{7,31}} | collective-permute-start | bytes 614408 | tf_op jit(solution)/shard_map/ppermute | solution.py:546
  18.0 5.2 %collective-permute-done.4.near_ref = bf16[1440,128]{1,0:T(8,128)(2,1)S(1)} collective-permute-done((bf16[1440,128]{1,0:T(8,128)(2,1)}, bf16[1440,128]{1,0:T(8,128)(2,1)S(1)}, u32[]{:S(2)}, u32[]{:S(2)}) %collective-permute-start.4) | collective-permute-done | bytes 368672 | tf_op jit(solution)/shard_map/ppermute | solution.py:546
  23.3 0.0 copy-start.3
  23.3 8.0 %collective-permute-done.3.far_ref = bf16[1440,128]{1,0:T(8,128)(2,1)S(1)} collective-permute-done((bf16[1440,128]{1,0:T(8,128)(2,1)}, bf16[1440,128]{1,0:T(8,128)(2,1)S(1)}, u32[]{:S(2)}, u32[]{:S(2)}) %collective-permute-start.3) | collective-permute-done | bytes 368672 | tf_op jit(solution)/shard_map/ppermute | solution.py:546
  31.3 0.0 copy-done.3
  31.3 0.0 copy-start.4
  31.3 0.8 %copy-done.4 = bf16[1440,128]{1,0:T(8,128)(2,1)} copy-done((bf16[1440,128]{1,0:T(8,128)(2,1)}, bf16[1440,128]{1,0:T(8,128)(2,1)S(1)}, u32[]{:S(2)}) %copy-start.4) | copy-done | bytes 368664
  32.0 5.3 %shard_map.70 = (f32[13,88,128]{2,1,0:T(8,128)}, f32[12,88,128]{2,1,0:T(8,128)}, f32[10,64,128]{2,1,0:T(8,128)}, f32[9,64,128]{2,1,0:T(8,128)}, f32[8,56,128]{2,...) custom-call(bf16[64,2048]{1,0:T(8,128)(2,1)} %bitcast.12, ...), custom_call_target="tpu_custom_call" | custom-call | flops 2000000000 | bytes 4000000 | tf_op jit(solution)/shard_map/pallas_call | solution.py:325
  37.3 0.0 collective-permute-done.2.hop_ref
  37.3 0.0 copy-start.5
  37.4 0.7 %copy-done.5 = bf16[800,128]{1,0:T(8,128)(2,1)} copy-done((bf16[800,128]{1,0:T(8,128)(2,1)}, bf16[800,128]{1,0:T(8,128)(2,1)S(1)}, u32[]{:S(2)}) %copy-start.5) | copy-done | bytes 204824
  38.0 6.2 %shard_map.71 = (bf16[64,2048]{1,0:T(8,128)(2,1)}, f32[304,128]{1,0:T(8,128)}, f32[304,128]{1,0:T(8,128)}) custom-call(bf16[64,2048]{1,0:T(8,128)(2,1)} %bitcast.13, bf16[32,2048]{1,0:T(8,128)(2,1)} %copy-done.6, bf16[32,2048]{1,0:T(8,128)(2,1)} %copy-done.7, bf16[64,2048]{1,0:T(8,128)(2,1)} %get-tuple-element.34.noise0, ...), custom_call_target="tpu_custom_call" | custom-call | flops 3000000000 | bytes 6000000 | tf_op jit(solution)/shard_map/pallas_call | solution.py:325
  44.2 0.4 collective-permute-start.5
  44.6 1.2 %collective-permute-done.5 = f32[304,128]{1,0:T(8,128)S(1)} collective-permute-done((f32[304,128]{1,0:T(8,128)}, f32[304,128]{1,0:T(8,128)S(1)}, u32[]{:S(2)}, u32[]{:S(2)}) %collective-permute-start.5) | collective-permute-done | bytes 155680 | tf_op jit(solution)/shard_map/ppermute | solution.py:749
  45.8 0.0 copy-start
  45.8 1.0 %fusion.1 = bf16[304,128]{1,0:T(8,128)(2,1)S(1)} fusion(f32[304,128]{1,0:T(8,128)} %get-tuple-element.51, f32[304,128]{1,0:T(8,128)S(1)} %collective-permute-done.5), kind=kLoop, calls=%fused_computation.4 | loop fusion | flops 116736 | bytes 389120 | tf_op jit(solution)/shard_map/convert_element_type | solution.py:753
  46.8 4.7 %collective-permute-start.6 = (bf16[304,128]{1,0:T(8,128)(2,1)S(1)}, bf16[304,128]{1,0:T(8,128)(2,1)S(1)}, u32[]{:S(2)}, u32[]{:S(2)}) collective-permute-start(bf16[304,128]{1,0:T(8,128)(2,1)S(1)} %fusion.1), channel_id=1, source_target_pairs={{0,2},{1,3},{2,0},{3,1},{4,6},{5,7},{6,4},{7,5},{8,10},{9,11},{10,... | collective-permute-start | bytes 233480 | tf_op jit(solution)/shard_map/ppermute | solution.py:753
  51.5 2.4 %collective-permute-done.6 = bf16[304,128]{1,0:T(8,128)(2,1)S(1)} collective-permute-done((bf16[304,128]{1,0:T(8,128)(2,1)S(1)}, bf16[304,128]{1,0:T(8,128)(2,1)S(1)}, u32[]{:S(2)}, u32[]{:S(2)}) %collective-permute-start.6) | collective-permute-done | bytes 77856 | tf_op jit(solution)/shard_map/ppermute | solution.py:753
  54.0 0.0 copy-done
  54.0 2.2 %collective-permute-start.7 = (bf16[304,128]{1,0:T(8,128)(2,1)S(1)}, bf16[304,128]{1,0:T(8,128)(2,1)S(1)}, u32[]{:S(2)}, u32[]{:S(2)}) collective-permute-start(bf16[304,128]{1,0:T(8,128)(2,1)S(1)} %fusion), channel_id=1, source_target_pairs={{0,4},{1,5},{2,6},{3,7},{4,0},{5,1},{6,2},{7,3},{8,12},{9,13},{10,... | collective-permute-start | bytes 233480 | tf_op jit(solution)/shard_map/ppermute | solution.py:753
  56.2 2.0 %collective-permute-done.7 = bf16[304,128]{1,0:T(8,128)(2,1)S(1)} collective-permute-done((bf16[304,128]{1,0:T(8,128)(2,1)S(1)}, bf16[304,128]{1,0:T(8,128)(2,1)S(1)}, u32[]{:S(2)}, u32[]{:S(2)}) %collective-permute-start.7) | collective-permute-done | bytes 77856 | tf_op jit(solution)/shard_map/ppermute | solution.py:753
  58.3 0.0 copy-start.1
  58.3 2.5 %collective-permute-start.8 = (f32[304,128]{1,0:T(8,128)S(1)}, f32[304,128]{1,0:T(8,128)S(1)}, u32[]{:S(2)}, u32[]{:S(2)}) collective-permute-start(f32[304,128]{1,0:T(8,128)S(1)} %convert_add_fusion.mine_ref), channel_id=1, source_target_pairs={{0,1},{1,0},{2,3},{3,2},{4,5},{5,4},{6,7},{7,6},{8,9},{9,8},{10,11... | collective-permute-start | bytes 466952 | tf_op jit(solution)/shard_map/ppermute | solution.py:756
  60.7 1.0 %collective-permute-done.8.other_ref = f32[304,128]{1,0:T(8,128)S(1)} collective-permute-done((f32[304,128]{1,0:T(8,128)S(1)}, f32[304,128]{1,0:T(8,128)S(1)}, u32[]{:S(2)}, u32[]{:S(2)}) %collective-permute-start.8) | collective-permute-done | bytes 155680 | tf_op jit(solution)/shard_map/ppermute | solution.py:756
  61.8 0.0 copy-done.1
  61.8 0.0 copy-start.2
  61.8 0.7 %copy-done.2 = f32[304,128]{1,0:T(8,128)} copy-done((f32[304,128]{1,0:T(8,128)}, f32[304,128]{1,0:T(8,128)S(1)}, u32[]{:S(2)}) %copy-start.2) | copy-done | bytes 155672
  62.4 2.0 %shard_map.72 = (f32[2,576,64]{2,1,0:T(8,128)}, f32[2,64]{1,0:T(2,128)}) custom-call(f32[304,128]{1,0:T(8,128)} %copy-done.1, f32[304,128]{1,0:T(8,128)} %copy-done.2), custom_call_target="tpu_custom_call" | custom-call | flops 1000000 | bytes 1000000 | tf_op jit(solution)/shard_map/pallas_call | solution.py:325
  (2 shorter events, 0.1 us)
Async XLA Ops:
  2.5 5.8 %collective-permute-start = (bf16[32,2048]{1,0:T(8,128)(2,1)}, bf16[32,2048]{1,0:T(8,128)(2,1)S(1)}, u32[]{:S(2)}, u32[]{:S(2)}) collective-permute-start(bf16[32,2048]{1,0:T(8,128)(2,1)} %get-tuple-element.29), channel_id=1, source_target_pairs={{0,1},{1,0},{2,3},{3,2},{4,5},{5,4},{6,7},{7,6},{8,9},{9,8},{10,11... | collective-permute-start | bytes 393224 | tf_op jit(solution)/shard_map/ppermute | solution.py:398
  3.2 6.5 %collective-permute-start.1 = (bf16[32,2048]{1,0:T(8,128)(2,1)}, bf16[32,2048]{1,0:T(8,128)(2,1)S(1)}, u32[]{:S(2)}, u32[]{:S(2)}) collective-permute-start(bf16[32,2048]{1,0:T(8,128)(2,1)} %get-tuple-element.30), channel_id=1, source_target_pairs={{1,2},{3,4},{5,6},{2,1},{4,3},{6,5},{9,10},{11,12},{13,14},{10,9},... | collective-permute-start | bytes 393224 | tf_op jit(solution)/shard_map/ppermute | solution.py:397
  8.4 1.3 %copy-start.6 = (bf16[32,2048]{1,0:T(8,128)(2,1)}, bf16[32,2048]{1,0:T(8,128)(2,1)S(1)}, u32[]{:S(2)}) copy-start(bf16[32,2048]{1,0:T(8,128)(2,1)S(1)} %collective-permute-done.swap_ref) | copy-start | bytes 393220
  9.7 0.7 %copy-start.7 = (bf16[32,2048]{1,0:T(8,128)(2,1)}, bf16[32,2048]{1,0:T(8,128)(2,1)S(1)}, u32[]{:S(2)}) copy-start(bf16[32,2048]{1,0:T(8,128)(2,1)S(1)} %collective-permute-done.1.cross_ref) | copy-start | bytes 393220
  13.1 10.2 %collective-permute-start.4 = (bf16[1440,128]{1,0:T(8,128)(2,1)}, bf16[1440,128]{1,0:T(8,128)(2,1)S(1)}, u32[]{:S(2)}, u32[]{:S(2)}) collective-permute-start(bf16[1440,128]{1,0:T(8,128)(2,1)} %get-tuple-element.39), channel_id=1, source_target_pairs={{0,8},{8,16},{16,24},{1,9},{9,17},{17,25},{2,10},{10,18},{18,26},{... | collective-permute-start | bytes 1105928 | tf_op jit(solution)/shard_map/ppermute | solution.py:546
  16.1 15.2 %collective-permute-start.3 = (bf16[1440,128]{1,0:T(8,128)(2,1)}, bf16[1440,128]{1,0:T(8,128)(2,1)S(1)}, u32[]{:S(2)}, u32[]{:S(2)}) collective-permute-start(bf16[1440,128]{1,0:T(8,128)(2,1)} %get-tuple-element.39), channel_id=1, source_target_pairs={{0,16},{8,24},{1,17},{9,25},{2,18},{10,26},{3,19},{11,27},{4,20},{... | collective-permute-start | bytes 1105928 | tf_op jit(solution)/shard_map/ppermute | solution.py:546
  17.4 20.0 %collective-permute-start.2 = (bf16[800,128]{1,0:T(8,128)(2,1)}, bf16[800,128]{1,0:T(8,128)(2,1)S(1)}, u32[]{:S(2)}, u32[]{:S(2)}) collective-permute-start(bf16[800,128]{1,0:T(8,128)(2,1)} %get-tuple-element.38), channel_id=1, source_target_pairs={{0,24},{1,25},{2,26},{3,27},{4,28},{5,29},{6,30},{7,31}} | collective-permute-start | bytes 614408 | tf_op jit(solution)/shard_map/ppermute | solution.py:546
  23.3 8.0 %copy-start.3 = (bf16[1440,128]{1,0:T(8,128)(2,1)}, bf16[1440,128]{1,0:T(8,128)(2,1)S(1)}, u32[]{:S(2)}) copy-start(bf16[1440,128]{1,0:T(8,128)(2,1)S(1)} %collective-permute-done.4.near_ref) | copy-start | bytes 1105924
  31.3 0.8 %copy-start.4 = (bf16[1440,128]{1,0:T(8,128)(2,1)}, bf16[1440,128]{1,0:T(8,128)(2,1)S(1)}, u32[]{:S(2)}) copy-start(bf16[1440,128]{1,0:T(8,128)(2,1)S(1)} %collective-permute-done.3.far_ref) | copy-start | bytes 1105924
  37.3 0.7 %copy-start.5 = (bf16[800,128]{1,0:T(8,128)(2,1)}, bf16[800,128]{1,0:T(8,128)(2,1)S(1)}, u32[]{:S(2)}) copy-start(bf16[800,128]{1,0:T(8,128)(2,1)S(1)} %collective-permute-done.2.hop_ref) | copy-start | bytes 614404
  44.2 1.6 %collective-permute-start.5 = (f32[304,128]{1,0:T(8,128)}, f32[304,128]{1,0:T(8,128)S(1)}, u32[]{:S(2)}, u32[]{:S(2)}) collective-permute-start(f32[304,128]{1,0:T(8,128)} %get-tuple-element.52), channel_id=1, source_target_pairs={{0,1},{1,0},{2,3},{3,2},{4,5},{5,4},{6,7},{7,6},{8,9},{9,8},{10,11... | collective-permute-start | bytes 466952 | tf_op jit(solution)/shard_map/ppermute | solution.py:749
  45.8 8.2 %copy-start = (f32[304,128]{1,0:T(8,128)S(1)}, f32[304,128]{1,0:T(8,128)}, u32[]{:S(2)}) copy-start(f32[304,128]{1,0:T(8,128)} %get-tuple-element.51) | copy-start | bytes 466948
  46.8 7.1 %collective-permute-start.6 = (bf16[304,128]{1,0:T(8,128)(2,1)S(1)}, bf16[304,128]{1,0:T(8,128)(2,1)S(1)}, u32[]{:S(2)}, u32[]{:S(2)}) collective-permute-start(bf16[304,128]{1,0:T(8,128)(2,1)S(1)} %fusion.1), channel_id=1, source_target_pairs={{0,2},{1,3},{2,0},{3,1},{4,6},{5,7},{6,4},{7,5},{8,10},{9,11},{10,... | collective-permute-start | bytes 233480 | tf_op jit(solution)/shard_map/ppermute | solution.py:753
  54.0 4.2 %collective-permute-start.7 = (bf16[304,128]{1,0:T(8,128)(2,1)S(1)}, bf16[304,128]{1,0:T(8,128)(2,1)S(1)}, u32[]{:S(2)}, u32[]{:S(2)}) collective-permute-start(bf16[304,128]{1,0:T(8,128)(2,1)S(1)} %fusion), channel_id=1, source_target_pairs={{0,4},{1,5},{2,6},{3,7},{4,0},{5,1},{6,2},{7,3},{8,12},{9,13},{10,... | collective-permute-start | bytes 233480 | tf_op jit(solution)/shard_map/ppermute | solution.py:753
  58.3 3.5 %copy-start.1 = (f32[304,128]{1,0:T(8,128)}, f32[304,128]{1,0:T(8,128)S(1)}, u32[]{:S(2)}) copy-start(f32[304,128]{1,0:T(8,128)S(1)} %convert_add_fusion.mine_ref) | copy-start | bytes 466948
  58.3 3.5 %collective-permute-start.8 = (f32[304,128]{1,0:T(8,128)S(1)}, f32[304,128]{1,0:T(8,128)S(1)}, u32[]{:S(2)}, u32[]{:S(2)}) collective-permute-start(f32[304,128]{1,0:T(8,128)S(1)} %convert_add_fusion.mine_ref), channel_id=1, source_target_pairs={{0,1},{1,0},{2,3},{3,2},{4,5},{5,4},{6,7},{7,6},{8,9},{9,8},{10,11... | collective-permute-start | bytes 466952 | tf_op jit(solution)/shard_map/ppermute | solution.py:756
  61.8 0.7 %copy-start.2 = (f32[304,128]{1,0:T(8,128)}, f32[304,128]{1,0:T(8,128)S(1)}, u32[]{:S(2)}) copy-start(f32[304,128]{1,0:T(8,128)S(1)} %collective-permute-done.8.other_ref) | copy-start | bytes 466948

commit v2 on v1

--- a/solution.py
+++ b/solution.py
@@ -14,7 +14,7 @@
 F32 = jnp.float32
 BF16 = jnp.bfloat16
 TAPS = 9
-VMEM_BYTES = 56 * 1024 * 1024
+VMEM_BYTES = 24 * 1024 * 1024
 
 
 def up_to(value, step):
@@ -321,7 +321,9 @@
             xb[p + 1, level.x_rows : level.alloc, :] = jnp.zeros((level.alloc - level.x_rows, LANES), F32)
 
 
-def call(body, out_shape, scratch, operands, flops, nbytes):
+def call(body, out_shape, scratch, operands, flops, nbytes, final=()):
+    operands = [pltpu.with_memory_space_constraint(x, pltpu.VMEM) for x in operands]
+    out_shape = [s if i in final else pltpu.VMEM(s.shape, s.dtype) for i, s in enumerate(out_shape)]
     return pl.pallas_call(
         body,
         out_shape=out_shape,
@@ -744,6 +746,7 @@
         ],
         3 * 10**9,
         6 * 10**6,
+        final=(0,),
     )
 
     total = keep + lax.ppermute(send, "strip", swap_pairs)
@@ -777,6 +780,7 @@
         [total, other],
         10**6,
         10**6,
+        final=(0, 1),
     )
     return (
         noise[None, None],

time: 64.7 us -> 51.2 us (0.79)
  Pallas kernels: 20.2 us -> 6.64 us
  starting transfers between devices: 18.4 us -> 19.7 us
  other arithmetic: 1.08 us -> 0.11 us
    pallas_call x6, Pallas kernels: 20.2 us -> 6.64 us  [call(): pl.pallas_call(body, out_shape=out_shape, in_specs=[pl.BlockSpec(memory_s...]
    ppermute x3, waiting for transfers between devices: 13.2 us -> 11.6 us  [across(): return lax.ppermute(value, 'section', pairs)]
    ppermute x1, waiting for transfers between devices: 1.32 us -> 2.83 us  [local(): from_cross = lax.ppermute(to_cross, 'strip', cross_pairs)]
    ppermute x2, starting transfers between devices: 6.93 us -> 8.38 us  [local(): lax.ppermute(mine.astype(BF16), 'strip', [(i, i ^ hop_size) for i in rang...]
    convert_element_type x2, other arithmetic: 1.04 us -> 0.06 us  [local(): mine.astype(BF16)]
    unnamed x16 -> x10, local copies, waits for them, and re-layouts: 2.75 us -> 2.62 us
  transfers between devices with their start and end apart: 9 -> 9, of which waited for: 7 -> 7; matrix products, arithmetic and copies ran while one was open for 0% -> 0% of each run, Pallas kernels for 11% -> 4%
where the time goes in v2:
time: 51.2 us; the launch traced here: 51 us
  waiting for transfers between devices  21.2 us (41%)
  starting transfers between devices  19.7 us (38%)
  Pallas kernels  6.64 us (13%)
  local copies, waits for them, and re-layouts  2.62 us (5%)
  between operations  0.75 us (1%)
    ppermute x3, waiting for transfers between devices, across(): return lax.ppermute(value, 'section', pairs)  11.6 us
    ppermute x2, starting transfers between devices, local(): lax.ppermute(mine.astype(BF16), 'strip', [(i, i ^ hop_size) for i in rang...  8.38 us
    pallas_call x6, Pallas kernels, call(): pl.pallas_call(body, out_shape=out_shape, in_specs=[pl.BlockSpec(memory_s...  6.64 us
    ppermute x3, starting transfers between devices, across(): return lax.ppermute(value, 'section', pairs)  4.92 us
    ppermute x2, waiting for transfers between devices, local(): lax.ppermute(mine.astype(BF16), 'strip', [(i, i ^ hop_size) for i in rang...  4.41 us
    ppermute x1, starting transfers between devices, local(): from_cross = lax.ppermute(to_cross, 'strip', cross_pairs)  3.1 us
    ppermute x1, waiting for transfers between devices, local(): from_cross = lax.ppermute(to_cross, 'strip', cross_pairs)  2.83 us
    unnamed x10, local copies, waits for them, and re-layouts  2.62 us
  transfers between devices with their start and end apart: 9, of which 7 were waited for; matrix products, arithmetic and copies ran while one was open for 0% of the time, Pallas kernels for 4%

profile of v2, /device:TPU:5, one launch (start us, length us, event | category | flops | bytes accessed | tf_op | source)
XLA Modules:
  0.0 51.0 jit_solution(214904207906077548)
XLA Ops:
  0.6 0.0 copy-start
  0.6 0.0 copy-start.1
  0.7 1.0 %copy-done.1 = bf16[1,64,2048]{2,1,0:T(8,128)(2,1)S(1)} copy-done((bf16[1,64,2048]{2,1,0:T(8,128)(2,1)S(1)}, bf16[1,64,2048]{2,1,0:T(8,128)(2,1)}, u32[]{:S(2)}) %copy-start.1) | copy-done | bytes 262168
  1.6 0.0 copy-start.3
  1.6 0.9 %copy-done.3 = bf16[1,1,64,2048]{3,2,1,0:T(8,128)(2,1)S(1)} copy-done((bf16[1,1,64,2048]{3,2,1,0:T(8,128)(2,1)S(1)}, bf16[1,1,64,2048]{3,2,1,0:T(8,128)(2,1)}, u32[]{:S(2)}) %copy-start.3) | copy-done | bytes 262168
  2.6 0.2 shard_map.67
  2.8 0.0 copy-start.2
  2.8 0.7 %collective-permute-start = (bf16[32,2048]{1,0:T(8,128)(2,1)S(1)}, bf16[32,2048]{1,0:T(8,128)(2,1)S(1)}, u32[]{:S(2)}, u32[]{:S(2)}) collective-permute-start(bf16[32,2048]{1,0:T(8,128)(2,1)S(1)} %get-tuple-element.29), channel_id=1, source_target_pairs={{0,1},{1,0},{2,3},{3,2},{4,5},{5,4},{6,7},{7,6},{8,9},{9,8},{10,11... | collective-permute-start | bytes 393224 | tf_op jit(solution)/shard_map/ppermute | solution.py:400
  3.5 3.1 %collective-permute-start.1 = (bf16[32,2048]{1,0:T(8,128)(2,1)S(1)}, bf16[32,2048]{1,0:T(8,128)(2,1)S(1)}, u32[]{:S(2)}, u32[]{:S(2)}) collective-permute-start(bf16[32,2048]{1,0:T(8,128)(2,1)S(1)} %get-tuple-element.30), channel_id=1, source_target_pairs={{1,2},{3,4},{5,6},{2,1},{4,3},{6,5},{9,10},{11,12},{13,14},{10,9},... | collective-permute-start | bytes 393224 | tf_op jit(solution)/shard_map/ppermute | solution.py:399
  6.6 0.0 copy-done
  6.6 0.3 shard_map.68
  6.9 0.0 collective-permute-done.swap_ref
  6.9 2.8 %collective-permute-done.1.cross_ref = bf16[32,2048]{1,0:T(8,128)(2,1)S(1)} collective-permute-done((bf16[32,2048]{1,0:T(8,128)(2,1)S(1)}, bf16[32,2048]{1,0:T(8,128)(2,1)S(1)}, u32[]{:S(2)}, u32[]{:S(2)}) %collective-permute-start.1) | collective-permute-done | bytes 131104 | tf_op jit(solution)/shard_map/ppermute | solution.py:399
  9.8 0.0 copy-start.4
  9.8 0.0 copy-done.2
  9.8 0.7 %copy-done.4 = f32[1,2,64]{2,1,0:T(2,128)S(1)} copy-done((f32[1,2,64]{2,1,0:T(2,128)S(1)}, f32[1,2,64]{2,1,0:T(2,128)}, u32[]{:S(2)}) %copy-start.4) | copy-done | bytes 536
  10.5 0.2 shard_map.69
  10.6 3.0 %collective-permute-start.4 = (bf16[1440,128]{1,0:T(8,128)(2,1)S(1)}, bf16[1440,128]{1,0:T(8,128)(2,1)S(1)}, u32[]{:S(2)}, u32[]{:S(2)}) collective-permute-start(bf16[1440,128]{1,0:T(8,128)(2,1)S(1)} %get-tuple-element.39), channel_id=1, source_target_pairs={{0,8},{8,16},{16,24},{1,9},{9,17},{17,25},{2,10},{10,18},{18,26},{... | collective-permute-start | bytes 1105928 | tf_op jit(solution)/shard_map/ppermute | solution.py:548
  13.6 1.3 %collective-permute-start.3 = (bf16[1440,128]{1,0:T(8,128)(2,1)S(1)}, bf16[1440,128]{1,0:T(8,128)(2,1)S(1)}, u32[]{:S(2)}, u32[]{:S(2)}) collective-permute-start(bf16[1440,128]{1,0:T(8,128)(2,1)S(1)} %get-tuple-element.39), channel_id=1, source_target_pairs={{0,16},{8,24},{1,17},{9,25},{2,18},{10,26},{3,19},{11,27},{4,20},{... | collective-permute-start | bytes 1105928 | tf_op jit(solution)/shard_map/ppermute | solution.py:548
  14.9 0.7 %collective-permute-start.2 = (bf16[800,128]{1,0:T(8,128)(2,1)S(1)}, bf16[800,128]{1,0:T(8,128)(2,1)S(1)}, u32[]{:S(2)}, u32[]{:S(2)}) collective-permute-start(bf16[800,128]{1,0:T(8,128)(2,1)S(1)} %get-tuple-element.38), channel_id=1, source_target_pairs={{0,24},{1,25},{2,26},{3,27},{4,28},{5,29},{6,30},{7,31}} | collective-permute-start | bytes 614408 | tf_op jit(solution)/shard_map/ppermute | solution.py:548
  15.6 4.3 %collective-permute-done.4.near_ref = bf16[1440,128]{1,0:T(8,128)(2,1)S(1)} collective-permute-done((bf16[1440,128]{1,0:T(8,128)(2,1)S(1)}, bf16[1440,128]{1,0:T(8,128)(2,1)S(1)}, u32[]{:S(2)}, u32[]{:S(2)}) %collective-permute-start.4) | collective-permute-done | bytes 368672 | tf_op jit(solution)/shard_map/ppermute | solution.py:548
  19.8 7.3 %collective-permute-done.3.far_ref = bf16[1440,128]{1,0:T(8,128)(2,1)S(1)} collective-permute-done((bf16[1440,128]{1,0:T(8,128)(2,1)S(1)}, bf16[1440,128]{1,0:T(8,128)(2,1)S(1)}, u32[]{:S(2)}, u32[]{:S(2)}) %collective-permute-start.3) | collective-permute-done | bytes 368672 | tf_op jit(solution)/shard_map/ppermute | solution.py:548
  27.2 1.8 %shard_map.70 = (f32[13,88,128]{2,1,0:T(8,128)S(1)}, f32[12,88,128]{2,1,0:T(8,128)S(1)}, f32[10,64,128]{2,1,0:T(8,128)S(1)}, f32[9,64,128]{2,1,0:T(8,128)S(1)}, ...) custom-call(bf16[64,2048]{1,0:T(8,128)(2,1)S(1)} %bitcast.12, ...), custom_call_target="tpu_custom_call" | custom-call | flops 2000000000 | bytes 4000000 | tf_op jit(solution)/shard_map/pallas_call | solution.py:327
  29.0 0.0 collective-permute-done.2.hop_ref
  29.0 3.2 %shard_map.71 = (bf16[64,2048]{1,0:T(8,128)(2,1)}, f32[304,128]{1,0:T(8,128)S(1)}, f32[304,128]{1,0:T(8,128)S(1)}) custom-call(bf16[64,2048]{1,0:T(8,128)(2,1)S(1)} %bitcast.13, bf16[32,2048]{1,0:T(8,128)(2,1)S(1)} %collective-permute-done.swap_ref, bf16[32,2048]{1,0:T(8,128)(2,1)S(1)} %collective-permute-done.1.cross_ref, ...), custom_call_target="tpu_custom_call" | custom-call | flops 3000000000 | bytes 6000000 | tf_op jit(solution)/shard_map/pallas_call | solution.py:327
  32.2 0.1 collective-permute-start.5
  32.3 1.3 %collective-permute-done.5 = f32[304,128]{1,0:T(8,128)S(1)} collective-permute-done((f32[304,128]{1,0:T(8,128)S(1)}, f32[304,128]{1,0:T(8,128)S(1)}, u32[]{:S(2)}, u32[]{:S(2)}) %collective-permute-start.5) | collective-permute-done | bytes 155680 | tf_op jit(solution)/shard_map/ppermute | solution.py:752
  33.6 6.1 %collective-permute-start.6 = (bf16[304,128]{1,0:T(8,128)(2,1)S(1)}, bf16[304,128]{1,0:T(8,128)(2,1)S(1)}, u32[]{:S(2)}, u32[]{:S(2)}) collective-permute-start(bf16[304,128]{1,0:T(8,128)(2,1)S(1)} %fusion.1), channel_id=1, source_target_pairs={{0,2},{1,3},{2,0},{3,1},{4,6},{5,7},{6,4},{7,5},{8,10},{9,11},{10,... | collective-permute-start | bytes 233480 | tf_op jit(solution)/shard_map/ppermute | solution.py:756
  39.8 2.4 %collective-permute-done.6 = bf16[304,128]{1,0:T(8,128)(2,1)S(1)} collective-permute-done((bf16[304,128]{1,0:T(8,128)(2,1)S(1)}, bf16[304,128]{1,0:T(8,128)(2,1)S(1)}, u32[]{:S(2)}, u32[]{:S(2)}) %collective-permute-start.6) | collective-permute-done | bytes 77856 | tf_op jit(solution)/shard_map/ppermute | solution.py:756
  42.2 2.2 %collective-permute-start.7 = (bf16[304,128]{1,0:T(8,128)(2,1)S(1)}, bf16[304,128]{1,0:T(8,128)(2,1)S(1)}, u32[]{:S(2)}, u32[]{:S(2)}) collective-permute-start(bf16[304,128]{1,0:T(8,128)(2,1)S(1)} %fusion), channel_id=1, source_target_pairs={{0,4},{1,5},{2,6},{3,7},{4,0},{5,1},{6,2},{7,3},{8,12},{9,13},{10,... | collective-permute-start | bytes 233480 | tf_op jit(solution)/shard_map/ppermute | solution.py:756
  44.5 2.0 %collective-permute-done.7 = bf16[304,128]{1,0:T(8,128)(2,1)S(1)} collective-permute-done((bf16[304,128]{1,0:T(8,128)(2,1)S(1)}, bf16[304,128]{1,0:T(8,128)(2,1)S(1)}, u32[]{:S(2)}, u32[]{:S(2)}) %collective-permute-start.7) | collective-permute-done | bytes 77856 | tf_op jit(solution)/shard_map/ppermute | solution.py:756
  46.5 2.5 %collective-permute-start.8 = (f32[304,128]{1,0:T(8,128)S(1)}, f32[304,128]{1,0:T(8,128)S(1)}, u32[]{:S(2)}, u32[]{:S(2)}) collective-permute-start(f32[304,128]{1,0:T(8,128)S(1)} %convert_add_fusion.mine_ref), channel_id=1, source_target_pairs={{0,1},{1,0},{2,3},{3,2},{4,5},{5,4},{6,7},{7,6},{8,9},{9,8},{10,11... | collective-permute-start | bytes 466952 | tf_op jit(solution)/shard_map/ppermute | solution.py:759
  49.0 1.0 %collective-permute-done.8.other_ref = f32[304,128]{1,0:T(8,128)S(1)} collective-permute-done((f32[304,128]{1,0:T(8,128)S(1)}, f32[304,128]{1,0:T(8,128)S(1)}, u32[]{:S(2)}, u32[]{:S(2)}) %collective-permute-start.8) | collective-permute-done | bytes 155680 | tf_op jit(solution)/shard_map/ppermute | solution.py:759
  50.0 1.0 %shard_map.72 = (f32[2,576,64]{2,1,0:T(8,128)}, f32[2,64]{1,0:T(2,128)}) custom-call(f32[304,128]{1,0:T(8,128)S(1)} %convert_add_fusion.mine_ref, f32[304,128]{1,0:T(8,128)S(1)} %collective-permute-done.8.other_ref), custom_call_target="tpu_custom_call" | custom-call | flops 1000000 | bytes 1000000 | tf_op jit(solution)/shard_map/pallas_call | solution.py:327
  (3 shorter events, 0.1 us)
Async XLA Ops:
  0.6 6.0 %copy-start = (bf16[1,2,3,3,64,64]{5,4,3,2,1,0:T(8,128)(2,1)S(1)}, bf16[1,2,3,3,64,64]{5,4,3,2,1,0:T(8,128)(2,1)}, u32[]{:S(2)}) copy-start(bf16[1,2,3,3,64,64]{5,4,3,2,1,0:T(8,128)(2,1)} %param.6) | copy-start | bytes 442372
  0.6 1.0 %copy-start.1 = (bf16[1,64,2048]{2,1,0:T(8,128)(2,1)S(1)}, bf16[1,64,2048]{2,1,0:T(8,128)(2,1)}, u32[]{:S(2)}) copy-start(bf16[1,64,2048]{2,1,0:T(8,128)(2,1)} %param.4) | copy-start | bytes 786436
  1.6 0.9 %copy-start.3 = (bf16[1,1,64,2048]{3,2,1,0:T(8,128)(2,1)S(1)}, bf16[1,1,64,2048]{3,2,1,0:T(8,128)(2,1)}, u32[]{:S(2)}) copy-start(bf16[1,1,64,2048]{3,2,1,0:T(8,128)(2,1)} %param.5) | copy-start | bytes 786436
  2.8 7.0 %copy-start.2 = (bf16[1,64,2048]{2,1,0:T(8,128)(2,1)S(1)}, bf16[1,64,2048]{2,1,0:T(8,128)(2,1)}, u32[]{:S(2)}) copy-start(bf16[1,64,2048]{2,1,0:T(8,128)(2,1)} %param.4) | copy-start | bytes 786436
  2.8 4.2 %collective-permute-start = (bf16[32,2048]{1,0:T(8,128)(2,1)S(1)}, bf16[32,2048]{1,0:T(8,128)(2,1)S(1)}, u32[]{:S(2)}, u32[]{:S(2)}) collective-permute-start(bf16[32,2048]{1,0:T(8,128)(2,1)S(1)} %get-tuple-element.29), channel_id=1, source_target_pairs={{0,1},{1,0},{2,3},{3,2},{4,5},{5,4},{6,7},{7,6},{8,9},{9,8},{10,11... | collective-permute-start | bytes 393224 | tf_op jit(solution)/shard_map/ppermute | solution.py:400
  3.5 6.3 %collective-permute-start.1 = (bf16[32,2048]{1,0:T(8,128)(2,1)S(1)}, bf16[32,2048]{1,0:T(8,128)(2,1)S(1)}, u32[]{:S(2)}, u32[]{:S(2)}) collective-permute-start(bf16[32,2048]{1,0:T(8,128)(2,1)S(1)} %get-tuple-element.30), channel_id=1, source_target_pairs={{1,2},{3,4},{5,6},{2,1},{4,3},{6,5},{9,10},{11,12},{13,14},{10,9},... | collective-permute-start | bytes 393224 | tf_op jit(solution)/shard_map/ppermute | solution.py:399
  9.8 0.7 %copy-start.4 = (f32[1,2,64]{2,1,0:T(2,128)S(1)}, f32[1,2,64]{2,1,0:T(2,128)}, u32[]{:S(2)}) copy-start(f32[1,2,64]{2,1,0:T(2,128)} %param.7) | copy-start | bytes 1540
  10.6 9.2 %collective-permute-start.4 = (bf16[1440,128]{1,0:T(8,128)(2,1)S(1)}, bf16[1440,128]{1,0:T(8,128)(2,1)S(1)}, u32[]{:S(2)}, u32[]{:S(2)}) collective-permute-start(bf16[1440,128]{1,0:T(8,128)(2,1)S(1)} %get-tuple-element.39), channel_id=1, source_target_pairs={{0,8},{8,16},{16,24},{1,9},{9,17},{17,25},{2,10},{10,18},{18,26},{... | collective-permute-start | bytes 1105928 | tf_op jit(solution)/shard_map/ppermute | solution.py:548
  13.6 13.6 %collective-permute-start.3 = (bf16[1440,128]{1,0:T(8,128)(2,1)S(1)}, bf16[1440,128]{1,0:T(8,128)(2,1)S(1)}, u32[]{:S(2)}, u32[]{:S(2)}) collective-permute-start(bf16[1440,128]{1,0:T(8,128)(2,1)S(1)} %get-tuple-element.39), channel_id=1, source_target_pairs={{0,16},{8,24},{1,17},{9,25},{2,18},{10,26},{3,19},{11,27},{4,20},{... | collective-permute-start | bytes 1105928 | tf_op jit(solution)/shard_map/ppermute | solution.py:548
  14.9 14.1 %collective-permute-start.2 = (bf16[800,128]{1,0:T(8,128)(2,1)S(1)}, bf16[800,128]{1,0:T(8,128)(2,1)S(1)}, u32[]{:S(2)}, u32[]{:S(2)}) collective-permute-start(bf16[800,128]{1,0:T(8,128)(2,1)S(1)} %get-tuple-element.38), channel_id=1, source_target_pairs={{0,24},{1,25},{2,26},{3,27},{4,28},{5,29},{6,30},{7,31}} | collective-permute-start | bytes 614408 | tf_op jit(solution)/shard_map/ppermute | solution.py:548
  32.2 1.4 %collective-permute-start.5 = (f32[304,128]{1,0:T(8,128)S(1)}, f32[304,128]{1,0:T(8,128)S(1)}, u32[]{:S(2)}, u32[]{:S(2)}) collective-permute-start(f32[304,128]{1,0:T(8,128)S(1)} %get-tuple-element.52), channel_id=1, source_target_pairs={{0,1},{1,0},{2,3},{3,2},{4,5},{5,4},{6,7},{7,6},{8,9},{9,8},{10,11... | collective-permute-start | bytes 466952 | tf_op jit(solution)/shard_map/ppermute | solution.py:752
  33.6 8.6 %collective-permute-start.6 = (bf16[304,128]{1,0:T(8,128)(2,1)S(1)}, bf16[304,128]{1,0:T(8,128)(2,1)S(1)}, u32[]{:S(2)}, u32[]{:S(2)}) collective-permute-start(bf16[304,128]{1,0:T(8,128)(2,1)S(1)} %fusion.1), channel_id=1, source_target_pairs={{0,2},{1,3},{2,0},{3,1},{4,6},{5,7},{6,4},{7,5},{8,10},{9,11},{10,... | collective-permute-start | bytes 233480 | tf_op jit(solution)/shard_map/ppermute | solution.py:756
  42.2 4.2 %collective-permute-start.7 = (bf16[304,128]{1,0:T(8,128)(2,1)S(1)}, bf16[304,128]{1,0:T(8,128)(2,1)S(1)}, u32[]{:S(2)}, u32[]{:S(2)}) collective-permute-start(bf16[304,128]{1,0:T(8,128)(2,1)S(1)} %fusion), channel_id=1, source_target_pairs={{0,4},{1,5},{2,6},{3,7},{4,0},{5,1},{6,2},{7,3},{8,12},{9,13},{10,... | collective-permute-start | bytes 233480 | tf_op jit(solution)/shard_map/ppermute | solution.py:756
  46.5 3.5 %collective-permute-start.8 = (f32[304,128]{1,0:T(8,128)S(1)}, f32[304,128]{1,0:T(8,128)S(1)}, u32[]{:S(2)}, u32[]{:S(2)}) collective-permute-start(f32[304,128]{1,0:T(8,128)S(1)} %convert_add_fusion.mine_ref), channel_id=1, source_target_pairs={{0,1},{1,0},{2,3},{3,2},{4,5},{5,4},{6,7},{7,6},{8,9},{9,8},{10,11... | collective-permute-start | bytes 466952 | tf_op jit(solution)/shard_map/ppermute | solution.py:759

commit v3 on v2

v3 whole, which is shorter than its diff:
```python
import functools
import math

import jax
import jax.numpy as jnp
import numpy as np
from jax import lax
from jax.experimental import pallas as pl
from jax.experimental.pallas import tpu as pltpu
from jax.sharding import PartitionSpec as P

LEAK = 0.05
LANES = 128
F32 = jnp.float32
BF16 = jnp.bfloat16
TAPS = 9
VMEM_BYTES = 24 * 1024 * 1024


def up_to(value, step):
    return -(-value // step) * step


class Level:
    def __init__(self, level, rows, cols):
        self.level = level
        self.rows = rows * 3**level // 4**level
        self.cols = cols * 3**level // 4**level
        self.pairs = -(-self.cols // 2)
        self.odd_pairs = -(-(self.cols + 1) // 2)

    def margin(self, error):
        self.error = error
        self.x_margin = error + 2
        self.x_rows = self.rows + 2 * (error + 2)
        self.hidden_rows = up_to(self.rows + 2 * (error + 1), 16)
        self.out_rows = up_to(self.rows + 2 * error, 16)
        self.in_rows = up_to(self.rows + 2 * (error - 1), 16)
        self.back_rows = up_to(self.rows + 2 * (error - 2), 16)
        self.own_rows = up_to(self.rows, 16)
        self.alloc = up_to(max(self.hidden_rows, self.x_margin + self.own_rows + 2) + 2, 8)


def levels_of(rows, cols, count):
    levels = [Level(s, rows, cols) for s in range(count)]
    levels[-1].margin(2)
    for s in range(count - 2, -1, -1):
        fine, coarse = levels[s], levels[s + 1]
        first = -coarse.error
        last = coarse.rows + coarse.error - 1
        low = 4 * (first // 3) + (-1, 1, 2)[first % 3]
        high = 4 * (last // 3) + (1, 2, 4)[last % 3]
        fine.margin(max(-low, high - fine.rows + 1) + 2)
        fine.k_first = first // 3
        fine.k_count = up_to(last // 3 - fine.k_first + 1, 8)
        fine.up_shift = -3 * fine.k_first - coarse.error
        start = fine.error - 2 + 4 * fine.k_first - 1
        fine.gu_row = max(0, -start)
        fine.gu_start = start + fine.gu_row
        assert fine.rows % 4 == 0
    return levels


def column_weights(fine, coarse):
    matrix = np.zeros((coarse, fine), np.float32)
    for x in range(fine):
        num = max((2 * x + 1) * coarse - fine, 0)
        low = num // (2 * fine)
        frac = np.float32(num - 2 * fine * low) / np.float32(2 * fine)
        matrix[low, x] += np.float32(1.0) - frac
        matrix[min(low + 1, coarse - 1), x] += frac
    return matrix


def lane_index(shape):
    return lax.broadcasted_iota(jnp.int32, shape, len(shape) - 1)


def half_swap(value):
    return pltpu.roll(value, LANES // 2, value.ndim - 1)


def twice(bias):
    return jnp.concatenate([bias, bias], axis=1)


def rounded(value):
    return value.astype(BF16).astype(F32)


def image_mask(level, base, count, strip, strips):
    row = lax.broadcasted_iota(jnp.int32, (1, count, LANES), 1) + base
    low = jnp.where(strip == 0, 0, -(10**6))
    high = jnp.where(strip == strips - 1, level.rows, 10**6)
    return (row >= low) & (row < high)


def odd_column_mask(level, first, count, mask):
    if first > 0 and 2 * (first + count - 1) < level.cols:
        return mask
    shape = (count, mask.shape[1], LANES)
    half = lax.broadcasted_iota(jnp.int32, shape, 2) // (LANES // 2)
    col = 2 * (first + lax.broadcasted_iota(jnp.int32, shape, 0)) - 1 + half
    return mask & (col >= 0) & (col < level.cols)


def conv(source, kernel, count, segments, chunk, emit):
    total = sum(rows for _, rows in segments)
    for first in range(0, count, chunk):
        size = min(chunk, count - first)
        parts = []
        for dy in range(3):
            blocks = [source[first : first + size + 1, a + dy : a + dy + rows, :] for a, rows in segments]
            block = blocks[0] if len(blocks) == 1 else jnp.concatenate(blocks, axis=1)
            block = block.astype(BF16)
            parts.append(block[:size].reshape(size * total, LANES))
            parts.append(block[1:].reshape(size * total, LANES))
        stacked = jnp.concatenate(parts, axis=1)
        result = jnp.dot(stacked, kernel[...], preferred_element_type=F32).reshape(size, total, LANES)
        at = 0
        for a, rows in segments:
            emit(first, size, a, rows, result[:, at : at + rows])
            at += rows


def kernel_terms(source, error, count, source_row, error_row, level):
    rows = level.own_rows
    err = error[0:count, error_row : error_row + rows, :]
    if rows != level.rows:
        row = lax.broadcasted_iota(jnp.int32, (1, rows, LANES), 1)
        err = jnp.where(row < level.rows, err, 0.0)
    total = jnp.sum(err, axis=(0, 1)).reshape(1, LANES)
    parts = []
    for dy in range(3):
        block = source[0 : count + 1, source_row + dy : source_row + dy + rows, :].astype(BF16)
        parts.append(block[:count].reshape(count * rows, LANES))
        parts.append(block[1:].reshape(count * rows, LANES))
    stacked = jnp.concatenate(parts, axis=1)
    product = lax.dot_general(
        err.astype(BF16).reshape(count * rows, LANES),
        stacked,
        (((0,), (0,)), ((), ())),
        preferred_element_type=F32,
    )
    return product, total


def pack_kernel_terms(out_ref, product, total, scale):
    half = LANES // 2
    by_tap = product.T * scale
    lane = lane_index((1, LANES))
    for dy in range(3):
        block = by_tap[dy * 2 * LANES : (dy + 1) * 2 * LANES]
        folded = block[: 3 * half] + half_swap(block)[half:]
        out_ref[dy * 96 : dy * 96 + 96, :] = jnp.where(lane < half, folded[:96], half_swap(folded[96:]))
    bias = (total + half_swap(total)) * scale
    out_ref[288:304, :] = jnp.broadcast_to(bias, (16, LANES))


def toeplitz(taps):
    half = LANES // 2
    zero = jnp.zeros((half, half), F32)
    rows = []
    for dy in range(3):
        for k in range(4):
            left = taps[dy * 3 + k] if k < 3 else zero
            right = taps[dy * 3 + k - 1] if k > 0 else zero
            rows.append(jnp.concatenate([left, right], axis=1))
    return jnp.concatenate(rows, axis=0)


def toeplitz_back(taps):
    half = LANES // 2
    zero = jnp.zeros((half, half), F32)
    columns = []
    for dy in range(3):
        for k in range(4):
            top = taps[(2 - dy) * 3 + 2 - k] if k < 3 else zero
            bottom = taps[(2 - dy) * 3 + 3 - k] if k > 0 else zero
            columns.append(jnp.concatenate([top, bottom], axis=0))
    pairs = [jnp.concatenate(columns[i : i + 2], axis=1).T for i in range(0, 12, 2)]
    return jnp.concatenate(pairs, axis=0)


def zero_tail(ref, level, rows):
    if level.alloc > rows:
        ref[0 : level.pairs + 1, rows : level.alloc, :] = jnp.zeros((level.pairs + 1, level.alloc - rows, LANES), F32)
    if level.odd_pairs < level.pairs + 1:
        ref[level.odd_pairs : level.pairs + 1, 0 : level.alloc, :] = jnp.zeros(
            (level.pairs + 1 - level.odd_pairs, level.alloc, LANES), F32
        )


def zero_edges(ref, level):
    zero = jnp.zeros((level.alloc, LANES), F32)
    ref[0, 0 : level.alloc, :] = zero
    ref[level.pairs + 1, 0 : level.alloc, :] = zero


def slope(value):
    return LEAK + (1.0 - LEAK) * (0.5 + 0.5 * jnp.tanh(0.5 * value))


def forward(level, xb, hb, kernels, bias, d_in, d_out, place, chunk, hidden_parts=None, out_parts=None):
    strip, strips = place
    bias_in, bias_out = bias[0:1], bias[1:2]

    def first_layer(first, size, a, rows, value):
        mask = image_mask(level, a - (level.error + 1), rows, strip, strips)
        pre = value + bias_in
        small = jnp.exp(-jnp.abs(pre))
        soft = jnp.maximum(pre, 0.0) + jnp.log(1.0 + small)
        act = LEAK * pre + (1.0 - LEAK) * soft
        keep = odd_column_mask(level, first, size, mask)
        hb[first : first + size, a : a + rows, :] = jnp.where(keep, rounded(act), 0.0)
        d_in[first : first + size, a : a + rows, :] = slope(pre)

    conv(xb, kernels[0], level.odd_pairs, hidden_parts or [(0, level.hidden_rows)], chunk, first_layer)

    def second_layer(first, size, a, rows, value):
        d_out(first, size, a, rows, slope(value + bias_out))

    conv(hb, kernels[1], level.pairs, out_parts or [(0, level.out_rows)], chunk, second_layer)


def backward(level, eo, ei, kernels, d_in, grad, grad_row, bi, gu, place, chunk, in_parts=None, back_parts=None):
    strip, strips = place

    def inner(first, size, a, rows, value):
        mask = image_mask(level, a - (level.error - 1), rows, strip, strips)
        keep = odd_column_mask(level, first, size, mask)
        part = d_in[first : first + size, 2 + a : 2 + a + rows, :]
        ei[first : first + size, a : a + rows, :] = jnp.where(keep, rounded(value * part), 0.0)

    conv(eo, kernels[1], level.odd_pairs, in_parts or [(0, level.in_rows)], chunk, inner)

    def outer(first, size, a, rows, value):
        if bi is not None:
            bi[first : first + size, a : a + rows, :] = value
        if gu is not None:
            mask = image_mask(level, a - (level.error - 2), rows, strip, strips)
            part = grad[first : first + size, grad_row + 2 + a : grad_row + 2 + a + rows, :]
            at = level.gu_row + a
            gu[first : first + size, at : at + rows, :] = jnp.where(mask, rounded(part + value), 0.0)

    conv(ei, kernels[0], level.pairs, back_parts or [(0, level.back_rows)], chunk, outer)


def write_noise(level, bi, noise):
    total_rows = noise.shape[0]
    row = lax.broadcasted_iota(jnp.int32, (level.own_rows, LANES), 0)
    lane = lane_index((level.own_rows, LANES))
    for p in range(noise.shape[1] // LANES):
        at = slice(p * LANES, (p + 1) * LANES)
        if p < level.pairs:
            part = bi[p, level.error - 2 : level.error - 2 + level.own_rows, :]
            if level.own_rows != level.rows:
                part = jnp.where(row < level.rows, part, 0.0)
            if 2 * p + 1 >= level.cols:
                part = jnp.where(lane < LANES // 2, part, 0.0)
            noise[0 : level.own_rows, at] = part.astype(BF16)
            if level.own_rows < total_rows:
                noise[level.own_rows : total_rows, at] = jnp.zeros((total_rows - level.own_rows, LANES), BF16)
        else:
            noise[:, at] = jnp.zeros((total_rows, LANES), BF16)


def coarsen(fine, coarse, gu, rc, ranges, spans, emit, place, edges=True):
    strip, strips = place
    for k, count in ranges:
        start = fine.gu_start + 4 * (k - fine.k_first)
        at = 3 * (k - fine.k_first)
        for p in range(fine.pairs):
            f = [gu[p, pl.ds(start + a, count, stride=4), :] for a in range(6)]
            rc[p, pl.ds(at, count, stride=3), :] = 0.125 * f[0] + 0.875 * f[1] + 0.375 * f[2]
            rc[p, pl.ds(at + 1, count, stride=3), :] = 0.625 * f[2] + 0.625 * f[3]
            rc[p, pl.ds(at + 2, count, stride=3), :] = 0.375 * f[3] + 0.875 * f[4] + 0.125 * f[5]
    if edges:
        top = -3 * fine.k_first
        low = top + coarse.rows - 1
        on_top = jnp.where(strip == 0, 1.0, 0.0).astype(F32)
        on_low = jnp.where(strip == strips - 1, 1.0, 0.0).astype(F32)
        every = slice(0, fine.pairs)
        rc[every, top : top + 1, :] = rc[every, top : top + 1, :] + on_top * rc[every, top - 1 : top, :]
        rc[every, low : low + 1, :] = rc[every, low : low + 1, :] + on_low * rc[every, low + 1 : low + 2, :]
    matrix = column_weights(fine.cols, coarse.cols)
    matrix = np.pad(matrix, ((0, 2 * coarse.pairs - coarse.cols), (0, 2 * fine.pairs - fine.cols)))
    lane = lane_index((1, LANES))

    def weights(low_lanes, high_lanes):
        return jnp.where(lane < LANES // 2, np.float32(low_lanes), np.float32(high_lanes))

    for span, (row, rows) in enumerate(spans):
        at = row - 3 * fine.k_first
        for m in range(coarse.pairs):
            total = None
            for q in range(fine.pairs):
                same = (matrix[2 * m, 2 * q], matrix[2 * m + 1, 2 * q + 1])
                cross = (matrix[2 * m, 2 * q + 1], matrix[2 * m + 1, 2 * q])
                value = rc[q, at : at + rows, :] if any(same) or any(cross) else None
                for pair, moved in ((same, False), (cross, True)):
                    if any(pair):
                        term = (half_swap(value) if moved else value) * weights(*pair)
                        total = term if total is None else total + term
            emit(m, span, total)


def own_input(level, xb, act):
    zero_edges(xb, level)
    lane = lane_index((1, LANES))
    for p in range(level.pairs):
        own = act[0 : level.own_rows, p * LANES : (p + 1) * LANES].astype(F32)
        if 2 * p + 1 >= level.cols:
            own = jnp.where(lane < LANES // 2, own, 0.0)
        xb[p + 1, level.x_margin : level.x_margin + level.own_rows, :] = own


def zero_after(level, xb):
    end = level.x_rows
    if end < level.alloc:
        xb[1 : level.pairs + 1, end : level.alloc, :] = jnp.zeros((level.pairs, level.alloc - end, LANES), F32)


def halo_input(level, xb, top, low, tmp, payload_rows):
    margin = level.x_margin
    end = margin + level.rows
    lane = lane_index((1, LANES))
    for p in range(level.pairs):
        at = slice(p * LANES, (p + 1) * LANES)
        upper, lower = top(at), low(at)
        if 2 * p + 1 >= level.cols:
            upper, lower = (jnp.where(lane < LANES // 2, v, 0.0) for v in (upper, lower))
        tmp[0, 0 : upper.shape[0], :] = upper
        tmp[1, 0 : lower.shape[0], :] = lower
        xb[p + 1, 0:margin, :] = tmp[0, payload_rows - margin : payload_rows, :]
        xb[p + 1, end : end + margin, :] = tmp[1, 0:margin, :]
    zero_after(level, xb)


def shipped_input(level, xb, own):
    zero_edges(xb, level)
    for p in range(level.pairs):
        xb[p + 1, 0 : level.x_rows, :] = own[p * level.x_rows : (p + 1) * level.x_rows, :]
    zero_after(level, xb)


def call(body, out_shape, scratch, operands, final=(), outside=(), aliases=None, flops=1000):
    operands = [
        pltpu.with_memory_space_constraint(x, pltpu.HBM if i in outside else pltpu.VMEM)
        for i, x in enumerate(operands)
    ]
    out_shape = [s if i in final else pltpu.VMEM(s.shape, s.dtype) for i, s in enumerate(out_shape)]
    return pl.pallas_call(
        body,
        out_shape=out_shape,
        in_specs=[pl.BlockSpec(memory_space=pltpu.VMEM)] * len(operands),
        out_specs=[pl.BlockSpec(memory_space=pltpu.VMEM)] * len(out_shape),
        scratch_shapes=scratch,
        input_output_aliases=aliases or {},
        compiler_params=pltpu.CompilerParams(vmem_limit_bytes=VMEM_BYTES),
        cost_estimate=pl.CostEstimate(flops=flops, bytes_accessed=1000, transcendentals=0),
    )(*operands)


def sds(shape, dtype):
    return jax.ShapeDtypeStruct(shape, dtype)


def field(level, extra):
    return sds((level.pairs + extra, level.alloc, LANES), F32)


def buffer(level, extra):
    return pltpu.VMEM((level.pairs + extra, level.alloc, LANES), F32)


def local(strips, sections, cotangent, activations, weights, biases):
    row_count, flat_width = activations.shape[2:]
    channels = weights.shape[-1]
    half = channels // 2
    cols = flat_width // channels
    assert 2 * channels == LANES and sections == 4 and cotangent.shape[0] == 1
    levels = levels_of(row_count, cols, sections)
    fine, second, third, last = levels
    x_margin, g_margin = fine.x_margin, fine.error
    payload = up_to(x_margin + g_margin, 16)
    pair_count = fine.pairs
    chunk = 4

    def place():
        return lax.axis_index("strip"), strips

    def is_odd():
        return lax.rem(lax.axis_index("strip"), 2) == 1

    packed_rows = TAPS * channels
    own_flat = up_to(third.pairs * third.x_rows, 16)
    ship_rows = own_flat + packed_rows + 16

    def halo_body(
        act_hbm, cot_hbm, bias_hbm, act_ref, cot_ref, both_ref, swap_ref, cross_ref, xs, cs, ts
    ):
        both_ref[0:2, :] = twice(bias_hbm[...])
        section = lax.axis_index("section")
        odd = is_odd()

        live = jnp.int32(fine.rows)
        for level in levels[1:]:
            live = jnp.where(section == level.level, level.rows, live)
        for p in range(pair_count):
            at = slice(p * LANES, (p + 1) * LANES)
            act_ref[:, at] = act_hbm[:, at]
            cot_ref[:, at] = cot_hbm[:, at]
            xs[p, :, :] = act_hbm[:, at].astype(F32)
            cs[p, :, :] = cot_hbm[:, at].astype(F32)
            ts[0, p, 0:x_margin, :] = xs[p, 0:x_margin, :]
            ts[0, p, x_margin : x_margin + g_margin, :] = cs[p, 0:g_margin, :]
            ts[1, p, 0:x_margin, :] = xs[p, pl.ds(live - x_margin, x_margin), :]
            ts[1, p, x_margin : x_margin + g_margin, :] = cs[p, row_count - g_margin : row_count, :]
            upper = ts[0, p, 0:payload, :]
            lower = ts[1, p, 0:payload, :]
            swap_ref[:, at] = jnp.where(odd, upper, lower).astype(BF16)
            cross_ref[:, at] = jnp.where(odd, lower, upper).astype(BF16)

    strip_shape = sds((row_count, flat_width), BF16)
    halo_shape = sds((payload, flat_width), BF16)
    taps = weights.reshape(2 * TAPS, channels, channels)
    act, cot, bias_own, to_swap, to_cross = call(
        halo_body,
        [
            strip_shape, strip_shape, sds((8, LANES), F32), halo_shape, halo_shape,
        ],
        [
            pltpu.VMEM((pair_count, row_count, LANES), F32),
            pltpu.VMEM((pair_count, row_count, LANES), F32),
            pltpu.VMEM((2, pair_count, payload, LANES), F32),
        ],
        [activations[0, 0], cotangent[0], biases[0]],
        outside=(0, 1, 2),
    )
    swap_pairs = [(i, i ^ 1) for i in range(strips)]
    cross_pairs = [(i, i + 1) for i in range(1, strips - 1, 2)] + [(i + 1, i) for i in range(1, strips - 1, 2)]
    from_cross = lax.ppermute(to_cross, "strip", cross_pairs)
    from_swap = lax.ppermute(to_swap, "strip", swap_pairs)


    def expand(tap_list, forward_ref, back_ref):
        for c in range(2):
            chosen = tap_list[c * TAPS : (c + 1) * TAPS]
            forward_ref[c, :, :] = toeplitz(chosen).astype(BF16)
            back_ref[c, :, :] = toeplitz_back(chosen).astype(BF16)

    def matrix_body(taps_ref, bias_ref, forward_ref, back_ref):
        expand([taps_ref[t].astype(F32) for t in range(2 * TAPS)], forward_ref, back_ref)

    matrix_shape = sds((2, 6 * LANES, LANES), BF16)
    fwd_own, back_own = call(matrix_body, [matrix_shape, matrix_shape], [], [taps, bias_own])

    def across(value, pairs):
        return lax.ppermute(value, "section", pairs)

    def ends(count):
        return [(0, 24), (count - 24, 24)]

    inside = [(16, row_count)]
    assert fine.error == 15 and fine.hidden_rows == row_count + 32 == fine.back_rows
    g_in = (4, second.rows - 8)
    g_end = second.error + g_in[0]
    in_rows = up_to(second.pairs * g_in[1], 16)
    rim_rows = up_to(second.pairs * 2 * g_end, 16)

    def error_of(level, gb, eo, mask_place):
        def error(first, size, a, rows, value):
            mask = image_mask(level, a - level.error, rows, *mask_place)
            part = gb[first : first + size, a : a + rows, :]
            eo[first + 1 : first + 1 + size, a : a + rows, :] = jnp.where(mask, rounded(part * value), 0.0)

        return error

    def inside_body(
        act_ref, cot_ref, fwd_ref, back_ref, bias_ref, hop_ref, xb, hb, db, gb, eo, ei, bi, gu, rc, flat,
    ):
        section = lax.axis_index("section")

        @pl.when(section == 0)
        def _():
            level = fine
            own_input(level, xb, act_ref)
            zero_after(level, xb)
            zero_edges(eo, level)
            zero_tail(hb, level, level.hidden_rows)
            zero_tail(ei, level, level.alloc)
            for p in range(level.pairs):
                gb[p, g_margin : g_margin + row_count, :] = cot_ref[:, p * LANES : (p + 1) * LANES].astype(F32)
            forward(
                level, xb, hb, [fwd_ref.at[0], fwd_ref.at[1]], bias_ref, db, error_of(level, gb, eo, place()),
                place(), chunk, inside, inside,
            )
            backward(
                level, eo, ei, [back_ref.at[0], back_ref.at[1]], db, gb, 0, bi, gu, place(), chunk, inside, inside
            )

            def emit(m, span, rows):
                flat[m * g_in[1] : (m + 1) * g_in[1], :] = rows

            coarsen(fine, second, gu, rc, [(0, 16)], [g_in], emit, place(), edges=False)
            hop_ref[...] = flat[0:in_rows, :].astype(BF16)

    coarse_buffer = pltpu.VMEM((fine.pairs, 3 * fine.k_count + 8, LANES), F32)
    state_shapes = [
        field(fine, 2), field(fine, 1), field(fine, 1), field(fine, 0),
        field(fine, 2), field(fine, 1), field(fine, 0), field(fine, 0),
    ]
    hop_in, *state = call(
        inside_body,
        [sds((in_rows, LANES), BF16), *state_shapes],
        [coarse_buffer, pltpu.VMEM((in_rows + 16, LANES), F32)],
        [act, cot, fwd_own, back_own, bias_own],
    )
    in_near = across(hop_in, [(0, 1)])

    def halo_readers(swap_ref, cross_ref):
        odd = is_odd()

        def top(at):
            return jnp.where(odd, swap_ref[:, at].astype(F32), cross_ref[:, at].astype(F32))

        def low(at):
            return jnp.where(odd, cross_ref[:, at].astype(F32), swap_ref[:, at].astype(F32))

        return top, low

    def rim_body(
        swap_ref, cross_ref, fwd_ref, back_ref, bias_ref, xi, hi, di, gi, oi, ii, bii, ui,
        rim_ref, noise_ref, xb, hb, db, gb, eo, ei, bi, gu, rc, flat, tmp,
    ):
        section = lax.axis_index("section")
        top, low = halo_readers(swap_ref, cross_ref)

        @pl.when(section == 0)
        def _():
            level = fine
            halo_input(level, xb, top, low, tmp, x_margin)
            for p in range(level.pairs):
                at = slice(p * LANES, (p + 1) * LANES)
                tmp[0, 0:payload, :] = top(at)
                tmp[1, 0:payload, :] = low(at)
                gb[p, 0:g_margin, :] = tmp[0, x_margin : x_margin + g_margin, :]
                gb[p, g_margin + row_count : 2 * g_margin + row_count, :] = tmp[
                    1, x_margin : x_margin + g_margin, :
                ]
            parts = ends(level.hidden_rows)
            forward(
                level, xb, hb, [fwd_ref.at[0], fwd_ref.at[1]], bias_ref, db, error_of(level, gb, eo, place()),
                place(), chunk, parts, parts,
            )
            backward(
                level, eo, ei, [back_ref.at[0], back_ref.at[1]], db, gb, 0, bi, gu, place(), chunk, parts, parts
            )

            def emit(m, span, rows):
                at = m * 2 * g_end + span * g_end
                flat[at : at + g_end, :] = rows[0:g_end]

            last_k = (second.rows + second.error) // 3
            coarsen(
                fine, second, gu, rc,
                [(fine.k_first, 8), (last_k - 7, 8)],
                [(-second.error, up_to(g_end, 8)), (g_in[0] + g_in[1], up_to(g_end, 8))],
                emit, place(),
            )
            rim_ref[...] = flat[0:rim_rows, :].astype(BF16)
            write_noise(level, bi, noise_ref)

    tmp_buffer = pltpu.VMEM((2, payload, LANES), F32)
    rim, noise_first, *state = call(
        rim_body,
        [sds((rim_rows, LANES), BF16), strip_shape, *state_shapes],
        [coarse_buffer, pltpu.VMEM((rim_rows + 32, LANES), F32), tmp_buffer],
        [from_swap, from_cross, fwd_own, back_own, bias_own, *state],
        aliases={5 + i: 2 + i for i in range(len(state_shapes))},
        flops=2 * 10**9,
    )
    rim_near = across(rim, [(0, 1)])

    def ship_body(act_ref, swap_ref, cross_ref, taps_ref, both_ref, rim_ref, ship_ref, tmp, flat, bias_tmp):
        top, low = halo_readers(swap_ref, cross_ref)

        @pl.when(lax.axis_index("section") == 2)
        def _():
            level = third
            margin = level.x_margin
            for p in range(level.pairs):
                at = slice(p * LANES, (p + 1) * LANES)
                tmp[0, 0:payload, :] = top(at)
                tmp[1, 0:payload, :] = low(at)
                to = p * level.x_rows
                end = to + margin + level.rows
                flat[to : to + margin, :] = tmp[0, x_margin - margin : x_margin, :]
                flat[to + margin : to + margin + level.own_rows, :] = act_ref[0 : level.own_rows, at].astype(F32)
                flat[end : end + margin, :] = tmp[1, 0:margin, :]
            ship_ref[0:own_flat, :] = flat[0:own_flat, :].astype(BF16)
            for t in range(2 * TAPS):
                at = own_flat + t * half
                value = taps_ref[t].astype(F32)
                ship_ref[at : at + half, :] = jnp.concatenate([value[:half], value[half:]], axis=1).astype(BF16)
            rest = both_ref[0:2, :]
            for term in range(3):
                part = rounded(rest)
                bias_tmp[2 * term : 2 * term + 2, :] = part
                rest = rest - part
            bias_tmp[6:16, :] = jnp.zeros((10, LANES), F32)
            ship_ref[own_flat + packed_rows : ship_rows, :] = bias_tmp[...].astype(BF16)

    (ship,) = call(
        ship_body,
        [sds((ship_rows, LANES), BF16)],
        [tmp_buffer, pltpu.VMEM((own_flat + 32, LANES), F32), pltpu.VMEM((16, LANES), F32)],
        [act, from_swap, from_cross, taps, bias_own, rim],
    )
    shipped = across(ship, [(2, 3)])

    grad_rows = up_to(packed_rows // 2 + 1, 16)

    def gradients(level, source, hidden, err_in, err_out, rows_at, pair_out):
        scale = np.float32(1.0 / math.sqrt(strips * level.rows * level.cols))
        first = kernel_terms(source, err_in, level.odd_pairs, rows_at[2], rows_at[0], level)
        pack_kernel_terms(pair_out.at[0], *first, scale)
        then = kernel_terms(hidden, err_out, level.pairs, rows_at[3], rows_at[1], level)
        pack_kernel_terms(pair_out.at[1], *then, scale)

    def finish(level, source, hidden, ei, eo, pair_out):
        at = (level.error - 1, level.error, level.error + 1, level.error)
        gradients(level, source, hidden, ei, eo.at[1 : 1 + level.pairs], at, pair_out)

    def store_in(level, d_out):
        def store(first, size, a, rows, value):
            d_out[first : first + size, a : a + rows, :] = value

        return store

    def beside_body(
        act_ref, swap_ref, cross_ref, fwd_ref, bias_ref, x0, h0, o0, i0,
        din_ref, dout_ref, hid_ref, x_ref, pair_ref, tmp,
    ):
        section = lax.axis_index("section")
        top, low = halo_readers(swap_ref, cross_ref)

        @pl.when(section == 0)
        def _():
            finish(fine, x0, h0, i0, o0, pair_ref)

        for level in levels[1:]:

            @pl.when(section == level.level)
            def _(level=level):
                own_input(level, x_ref, act_ref)
                halo_input(level, x_ref, top, low, tmp, x_margin)
                zero_tail(hid_ref, level, level.hidden_rows)
                forward(
                    level, x_ref, hid_ref, [fwd_ref.at[0], fwd_ref.at[1]], bias_ref, din_ref,
                    store_in(level, dout_ref), place(), chunk,
                )

    pair_shape = sds((2, grad_rows, LANES), F32)
    din_own, dout_own, hid_own, x_own, pair_first = call(
        beside_body,
        [field(second, 1), field(second, 0), field(second, 1), field(second, 2), pair_shape],
        [tmp_buffer],
        [act, from_swap, from_cross, fwd_own, bias_own, state[0], state[1], state[4], state[5]],
    )

    def step(level, gb, grad_row, d_in, d_out, back, eo, ei, bi, gu):
        mask = image_mask(level, -level.error, level.out_rows, *place())
        zero_edges(eo, level)
        zero_tail(ei, level, level.alloc)
        for p in range(level.pairs):
            part = gb[p, grad_row : grad_row + level.out_rows, :] * d_out[p, 0 : level.out_rows, :]
            eo[p + 1, 0 : level.out_rows, :] = jnp.where(mask[0], rounded(part), 0.0)
        backward(level, eo, ei, [back.at[0], back.at[1]], d_in, gb, grad_row, bi, gu, place(), chunk)

    third_rows = third.rows + 2 * third.error
    third_flat = up_to(third.pairs * third_rows, 16)

    def hand_down(upper, lower, gu, rc, gb):
        def emit(m, span, value):
            gb[m, 0 : 3 * upper.k_count, :] = rounded(value)

        coarsen(
            upper, lower, gu, rc, [(upper.k_first, upper.k_count)], [(3 * upper.k_first, 3 * upper.k_count)],
            emit, place(),
        )

    def second_body(
        in_ref, rim_ref, din_o, dout_o, back_o, third_ref, eo, ei, bi, gb, gu, rc, mid, rims, flat
    ):
        @pl.when(lax.axis_index("section") == 1)
        def _():
            mid[...] = in_ref[...].astype(F32)
            rims[...] = rim_ref[...].astype(F32)
            low = g_end + g_in[1]
            for p in range(second.pairs):
                at = p * 2 * g_end
                gb[p, 0:g_end, :] = rims[at : at + g_end, :]
                gb[p, g_end:low, :] = mid[p * g_in[1] : (p + 1) * g_in[1], :]
                gb[p, low : low + g_end, :] = rims[at + g_end : at + 2 * g_end, :]
            step(second, gb, 0, din_o, dout_o, back_o, eo, ei, bi, gu)
            hand_down(second, third, gu, rc, gb)
            at = second.up_shift
            for p in range(third.pairs):
                flat[p * third_rows : (p + 1) * third_rows, :] = gb[p, at : at + third_rows, :]
            third_ref[...] = flat[0:third_flat, :].astype(BF16)

    coarse_tmp = pltpu.VMEM((second.pairs, 3 * second.k_count + 8, LANES), F32)
    third_grad, eo_own, ei_own, bi_own = call(
        second_body,
        [sds((third_flat, LANES), BF16), field(second, 2), field(second, 1), field(second, 0)],
        [
            buffer(second, 0),
            buffer(fine, 0),
            coarse_tmp,
            pltpu.VMEM((in_rows, LANES), F32),
            pltpu.VMEM((rim_rows, LANES), F32),
            pltpu.VMEM((third_flat + 16, LANES), F32),
        ],
        [in_near, rim_near, din_own, dout_own, back_own],
        flops=4 * 10**9,
    )
    third_to_last = across(third_grad, [(1, 3)])
    third_to_own = across(third_grad, [(1, 2)])

    def shipped_body(ship_ref, own_ref, din_s, dout_s, back_s, fwd_s, xb, hb, own):
        @pl.when(lax.axis_index("section") == 3)
        def _():
            level = third
            values = []
            for t in range(2 * TAPS):
                pack = ship_ref[own_flat + t * half : own_flat + (t + 1) * half, :].astype(F32)
                values.append(jnp.concatenate([pack[:, :channels], pack[:, channels:]], axis=0))
            expand(values, fwd_s, back_s)
            terms = ship_ref[own_flat + packed_rows : ship_rows, :].astype(F32)
            bias = terms[0:2] + terms[2:4] + terms[4:6]
            own[0:own_flat, :] = ship_ref[0:own_flat, :].astype(F32)
            shipped_input(level, xb, own)
            zero_tail(hb, level, level.hidden_rows)
            forward(level, xb, hb, [fwd_s.at[0], fwd_s.at[1]], bias, din_s, store_in(level, dout_s), place(), chunk)

    din_s, dout_s, back_s = call(
        shipped_body,
        [field(third, 1), field(third, 0), matrix_shape],
        [
            pltpu.VMEM((2, 6 * LANES, LANES), BF16),
            buffer(third, 2),
            buffer(third, 1),
            pltpu.VMEM((own_flat + 16, LANES), F32),
        ],
        [shipped, third_to_own],
    )

    def last_body(
        pair0, own_ref, last_ref, din_o, dout_o, hid_o, x_o, back_o, din_s, dout_s, back_s, eo_o, ei_o,
        keep_ref, send_ref, bi, pair_out, gb, eo, ei, gu, rc, flat,
    ):
        section = lax.axis_index("section")
        odd = is_odd()

        def take(source):
            flat[...] = source[...].astype(F32)
            for p in range(third.pairs):
                gb[p, 0:third_rows, :] = flat[p * third_rows : (p + 1) * third_rows, :]

        @pl.when(section == 0)
        def _():
            pair_out[...] = pair0[...]

        @pl.when(section == 1)
        def _():
            finish(second, x_o, hid_o, ei_o, eo_o, pair_out)

        @pl.when(section == 2)
        def _():
            take(own_ref)
            step(third, gb, 0, din_o, dout_o, back_o, eo, ei, bi, None)
            finish(third, x_o, hid_o, ei, eo, pair_out)

        @pl.when(section == 3)
        def _():
            take(last_ref)
            step(third, gb, 0, din_s, dout_s, back_s, eo, ei, None, gu)
            hand_down(third, last, gu, rc, gb)
            step(last, gb, third.up_shift, din_o, dout_o, back_o, eo, ei, bi, None)
            finish(last, x_o, hid_o, ei, eo, pair_out)

        first, then = pair_out[0], pair_out[1]
        keep_ref[...] = jnp.where(odd, then, first)
        send_ref[...] = jnp.where(odd, first, then)

    half_shape = sds((grad_rows, LANES), F32)
    keep, send, bi_last = call(
        last_body,
        [half_shape, half_shape, field(third, 0)],
        [
            pltpu.VMEM((2, grad_rows, LANES), F32),
            buffer(third, 0),
            buffer(third, 2),
            buffer(third, 1),
            buffer(fine, 0),
            coarse_tmp,
            pltpu.VMEM((third_flat, LANES), F32),
        ],
        [
            pair_first, third_to_own, third_to_last, din_own, dout_own, hid_own, x_own, back_own,
            din_s, dout_s, back_s, eo_own, ei_own,
        ],
    )

    total = keep + lax.ppermute(send, "strip", swap_pairs)
    hop_size = 2
    while hop_size < strips:
        mine = lax.reduce_precision(total, 8, 7)
        other = lax.ppermute(mine.astype(BF16), "strip", [(i, i ^ hop_size) for i in range(strips)])
        total = mine + other.astype(F32)
        hop_size *= 2
    other = lax.ppermute(total, "strip", swap_pairs)

    def noise_body(noise0, bi_o, bi_l, noise_ref):
        section = lax.axis_index("section")

        @pl.when(section == 0)
        def _():
            noise_ref[...] = noise0[...]

        for level, source in ((second, bi_o), (third, bi_l), (last, bi_l)):

            @pl.when(section == level.level)
            def _(level=level, source=source):
                write_noise(level, source, noise_ref)

    (noise,) = call(noise_body, [strip_shape], [], [noise_first, bi_own, bi_last], final=(0,))

    def final_body(mine_ref, other_ref, kernel_ref, bias_ref):
        odd = is_odd()
        for c in range(2):
            if c == 0:
                value = jnp.where(odd, other_ref[...], mine_ref[...])
            else:
                value = jnp.where(odd, mine_ref[...], other_ref[...])
            swapped = half_swap(value)
            for dy in range(3):
                kernel_ref[c, dy * 192 : dy * 192 + 96, :] = value[dy * 96 : dy * 96 + 96, :channels]
                kernel_ref[c, dy * 192 + 96 : dy * 192 + 192, :] = swapped[dy * 96 : dy * 96 + 96, :channels]
            bias_ref[c : c + 1, :] = value[288:289, :channels]

    kernel_sum, bias_sum = call(
        final_body,
        [sds((2, TAPS * channels, channels), F32), sds((2, channels), F32)],
        [],
        [total, other],
        final=(0, 1),
    )
    return (
        noise[None, None],
        kernel_sum.reshape(1, 2, 3, 3, channels, channels),
        bias_sum[None],
    )


def solution(mesh):
    strips = mesh.shape["strip"]
    sections = mesh.shape["section"]
    return jax.shard_map(
        functools.partial(local, strips, sections),
        mesh=mesh,
        in_specs=(
            P(None, "strip", None),
            P("section", None, "strip", None),
            P("section", None, None, None, None, None),
            P("section", None, None),
        ),
        out_specs=(
            P("section", None, "strip", None),
            P("section", None, None, None, None, None),
            P("section", None, None),
        ),
        check_vma=False,
    )
```

time: 51.2 us -> 39 us (0.76)
  the two profiles are of different devices: /device:TPU:5 before, /device:TPU:7 now
where the time goes in v3:
time: 39 us; the launch traced here: 38.8 us
  starting transfers between devices  16.4 us (42%)
  waiting for transfers between devices  14.8 us (38%)
  Pallas kernels  6.63 us (17%)
  between operations  0.8 us (2%)
    ppermute x5, waiting for transfers between devices, across(): return lax.ppermute(value, 'section', pairs)  6.77 us
    pallas_call x11, Pallas kernels, call(): pl.pallas_call(body, out_shape=out_shape, in_specs=[pl.BlockSpec(memory_s...  6.63 us
    ppermute x2, starting transfers between devices, local(): lax.ppermute(mine.astype(BF16), 'strip', [(i, i ^ hop_size) for i in rang...  5.47 us
    ppermute x5, starting transfers between devices, across(): return lax.ppermute(value, 'section', pairs)  4.57 us
    ppermute x2, waiting for transfers between devices, local(): lax.ppermute(mine.astype(BF16), 'strip', [(i, i ^ hop_size) for i in rang...  4.28 us
    ppermute x1, starting transfers between devices, local(): from_cross = lax.ppermute(to_cross, 'strip', cross_pairs)  3.1 us
    ppermute x1, starting transfers between devices, local(): other = lax.ppermute(total, 'strip', swap_pairs)  2.46 us
    ppermute x1, waiting for transfers between devices, local(): from_cross = lax.ppermute(to_cross, 'strip', cross_pairs)  2.12 us
  transfers between devices with their start and end apart: 11, of which 7 were waited for; matrix products, arithmetic and copies ran while one was open for 0% of the time, Pallas kernels for 7%

profile of v3, /device:TPU:7, one launch (start us, length us, event | category | flops | bytes accessed | tf_op | source)
XLA Modules:
  0.0 38.8 jit_solution(14177726092859737400)
XLA Ops:
  0.6 0.0 copy-start
  0.6 1.3 %shard_map.67 = (bf16[64,2048]{1,0:T(8,128)(2,1)S(1)}, bf16[64,2048]{1,0:T(8,128)(2,1)S(1)}, f32[8,128]{1,0:T(8,128)S(1)}, bf16[32,2048]{1,0:T(8,128)(2,1)S(1)}, bf16[32,2048]{1,0:T(8,128)(2,1)S(1)}) custom-call(bf16[64,2048]{1,0:T(8,128)(2,1)} %bitcast.9, bf16[64,2048]{1,0:T(8,128)(2,1)} %bitcast.10, f32[2,64]{1,0:T(2,128)} %bitcast.12), custom_call_target="tpu_custom_call" | custom-call | flops 1000 | bytes 1000 | tf_op jit(solution)/shard_map/pallas_call | solution.py:353
  2.0 0.7 %collective-permute-start = (bf16[32,2048]{1,0:T(8,128)(2,1)S(1)}, bf16[32,2048]{1,0:T(8,128)(2,1)S(1)}, u32[]{:S(2)}, u32[]{:S(2)}) collective-permute-start(bf16[32,2048]{1,0:T(8,128)(2,1)S(1)} %get-tuple-element.42), channel_id=1, source_target_pairs={{0,1},{1,0},{2,3},{3,2},{4,5},{5,4},{6,7},{7,6},{8,9},{9,8},{10,11... | collective-permute-start | bytes 393224 | tf_op jit(solution)/shard_map/ppermute | solution.py:444
  2.7 3.1 %collective-permute-start.1 = (bf16[32,2048]{1,0:T(8,128)(2,1)S(1)}, bf16[32,2048]{1,0:T(8,128)(2,1)S(1)}, u32[]{:S(2)}, u32[]{:S(2)}) collective-permute-start(bf16[32,2048]{1,0:T(8,128)(2,1)S(1)} %get-tuple-element.43), channel_id=1, source_target_pairs={{1,2},{3,4},{5,6},{2,1},{4,3},{6,5},{9,10},{11,12},{13,14},{10,9},... | collective-permute-start | bytes 393224 | tf_op jit(solution)/shard_map/ppermute | solution.py:443
  5.8 0.0 copy-done
  5.8 0.3 shard_map.68
  6.2 0.7 %collective-permute-start.2 = (bf16[480,128]{1,0:T(8,128)(2,1)S(1)}, bf16[480,128]{1,0:T(8,128)(2,1)S(1)}, u32[]{:S(2)}, u32[]{:S(2)}) collective-permute-start(bf16[480,128]{1,0:T(8,128)(2,1)S(1)} %get-tuple-element.58), channel_id=1, source_target_pairs={{0,8},{1,9},{2,10},{3,11},{4,12},{5,13},{6,14},{7,15}} | collective-permute-start | bytes 368648 | tf_op jit(solution)/shard_map/ppermute | solution.py:460
  6.8 0.0 collective-permute-done.swap_ref
  6.9 2.1 %collective-permute-done.1.cross_ref = bf16[32,2048]{1,0:T(8,128)(2,1)S(1)} collective-permute-done((bf16[32,2048]{1,0:T(8,128)(2,1)S(1)}, bf16[32,2048]{1,0:T(8,128)(2,1)S(1)}, u32[]{:S(2)}, u32[]{:S(2)}) %collective-permute-start.1) | collective-permute-done | bytes 131104 | tf_op jit(solution)/shard_map/ppermute | solution.py:443
  9.0 0.7 %collective-permute-start.3 = (bf16[320,128]{1,0:T(8,128)(2,1)S(1)}, bf16[320,128]{1,0:T(8,128)(2,1)S(1)}, u32[]{:S(2)}, u32[]{:S(2)}) collective-permute-start(bf16[320,128]{1,0:T(8,128)(2,1)S(1)} %get-tuple-element.59.rim_ref), channel_id=1, source_target_pairs={{0,8},{1,9},{2,10},{3,11},{4,12},{5,13},{6,14},{7,15}} | collective-permute-start | bytes 245768 | tf_op jit(solution)/shard_map/ppermute | solution.py:460
  9.7 1.3 %collective-permute-start.6 = (bf16[1056,128]{1,0:T(8,128)(2,1)S(1)}, bf16[1056,128]{1,0:T(8,128)(2,1)S(1)}, u32[]{:S(2)}, u32[]{:S(2)}) collective-permute-start(bf16[1056,128]{1,0:T(8,128)(2,1)S(1)} %shard_map.73), channel_id=1, source_target_pairs={{16,24},{17,25},{18,26},{19,27},{20,28},{21,29},{22,30},{23,31}} | collective-permute-start | bytes 811016 | tf_op jit(solution)/shard_map/ppermute | solution.py:460
  11.0 0.6 %shard_map.71 = (f32[13,88,128]{2,1,0:T(8,128)S(1)}, f32[12,88,128]{2,1,0:T(8,128)S(1)}, f32[13,88,128]{2,1,0:T(8,128)S(1)}, f32[14,88,128]{2,1,0:T(8,128)S(1)}, f32[2,304,128]{2,1,0:T(8,128)S(1)}) custom-call(bf16[64,2048]{1,0:T(8,128)(2,1)S(1)} %get-tuple-element.47.act_ref, bf16[32,2048]{1,0:T(8,128)(2,1)S(1)} %collective-permute-done.swap_ref, ...), custom_call_target="tpu_custom_call" | custom-call | flops 1000 | bytes 1000 | tf_op jit(solution)/shard_map/pallas_call | solution.py:353
  11.6 0.0 collective-permute-done.2.in_ref
  11.6 0.0 collective-permute-done.3.rim_ref
  11.6 0.7 %collective-permute-start.4 = (bf16[416,128]{1,0:T(8,128)(2,1)S(1)}, bf16[416,128]{1,0:T(8,128)(2,1)S(1)}, u32[]{:S(2)}, u32[]{:S(2)}) collective-permute-start(bf16[416,128]{1,0:T(8,128)(2,1)S(1)} %get-tuple-element.68), channel_id=1, source_target_pairs={{8,16},{9,17},{10,18},{11,19},{12,20},{13,21},{14,22},{15,23}} | collective-permute-start | bytes 319496 | tf_op jit(solution)/shard_map/ppermute | solution.py:460
  12.3 1.3 %collective-permute-start.5 = (bf16[416,128]{1,0:T(8,128)(2,1)S(1)}, bf16[416,128]{1,0:T(8,128)(2,1)S(1)}, u32[]{:S(2)}, u32[]{:S(2)}) collective-permute-start(bf16[416,128]{1,0:T(8,128)(2,1)S(1)} %get-tuple-element.68), channel_id=1, source_target_pairs={{8,24},{9,25},{10,26},{11,27},{12,28},{13,29},{14,30},{15,31}} | collective-permute-start | bytes 319496 | tf_op jit(solution)/shard_map/ppermute | solution.py:460
  13.6 0.0 collective-permute-done.4.own_ref
  13.6 3.3 %collective-permute-done.6.ship_ref = bf16[1056,128]{1,0:T(8,128)(2,1)S(1)} collective-permute-done((bf16[1056,128]{1,0:T(8,128)(2,1)S(1)}, bf16[1056,128]{1,0:T(8,128)(2,1)S(1)}, u32[]{:S(2)}, u32[]{:S(2)}) %collective-permute-start.6) | collective-permute-done | bytes 270368 | tf_op jit(solution)/shard_map/ppermute | solution.py:460
  16.9 0.9 %shard_map.74 = (f32[10,64,128]{2,1,0:T(8,128)S(1)}, f32[9,64,128]{2,1,0:T(8,128)S(1)}, bf16[2,768,128]{2,1,0:T(8,128)(2,1)S(1)}) custom-call(bf16[1056,128]{1,0:T(8,128)(2,1)S(1)} %collective-permute-done.6.ship_ref, bf16[416,128]{1,0:T(8,128)(2,1)S(1)} %collective-permute-done.4.own_ref), custom_call_target="tpu_custom_call" | custom-call | flops 1000 | bytes 1000 | tf_op jit(solution)/shard_map/pallas_call | solution.py:353
  17.7 3.5 %collective-permute-done.5.last_ref = bf16[416,128]{1,0:T(8,128)(2,1)S(1)} collective-permute-done((bf16[416,128]{1,0:T(8,128)(2,1)S(1)}, bf16[416,128]{1,0:T(8,128)(2,1)S(1)}, u32[]{:S(2)}, u32[]{:S(2)}) %collective-permute-start.5) | collective-permute-done | bytes 106528 | tf_op jit(solution)/shard_map/ppermute | solution.py:460
  21.2 1.8 %shard_map.75 = (f32[304,128]{1,0:T(8,128)S(1)}, f32[304,128]{1,0:T(8,128)S(1)}, f32[9,64,128]{2,1,0:T(8,128)S(1)}) custom-call(f32[2,304,128]{2,1,0:T(8,128)S(1)} %get-tuple-element.67.pair0, bf16[416,128]{1,0:T(8,128)(2,1)S(1)} %collective-permute-done.4.own_ref, bf16[416,128]{1,0:T(8,128)(2,1)S(1)} %collective-permute-done.5.last_ref, ...), custom_call_target="tpu_custom_call" | custom-call | flops 1000 | bytes 1000 | tf_op jit(solution)/shard_map/pallas_call | solution.py:353
  23.0 0.1 collective-permute-start.7
  23.1 1.4 %collective-permute-done.7 = f32[304,128]{1,0:T(8,128)S(1)} collective-permute-done((f32[304,128]{1,0:T(8,128)S(1)}, f32[304,128]{1,0:T(8,128)S(1)}, u32[]{:S(2)}, u32[]{:S(2)}) %collective-permute-start.7) | collective-permute-done | bytes 155680 | tf_op jit(solution)/shard_map/ppermute | solution.py:817
  24.5 3.1 %collective-permute-start.8 = (bf16[304,128]{1,0:T(8,128)(2,1)S(1)}, bf16[304,128]{1,0:T(8,128)(2,1)S(1)}, u32[]{:S(2)}, u32[]{:S(2)}) collective-permute-start(bf16[304,128]{1,0:T(8,128)(2,1)S(1)} %fusion.1), channel_id=1, source_target_pairs={{0,2},{1,3},{2,0},{3,1},{4,6},{5,7},{6,4},{7,5},{8,10},{9,11},{10,... | collective-permute-start | bytes 233480 | tf_op jit(solution)/shard_map/ppermute | solution.py:821
  27.6 2.4 %collective-permute-done.8 = bf16[304,128]{1,0:T(8,128)(2,1)S(1)} collective-permute-done((bf16[304,128]{1,0:T(8,128)(2,1)S(1)}, bf16[304,128]{1,0:T(8,128)(2,1)S(1)}, u32[]{:S(2)}, u32[]{:S(2)}) %collective-permute-start.8) | collective-permute-done | bytes 77856 | tf_op jit(solution)/shard_map/ppermute | solution.py:821
  30.1 2.4 %collective-permute-start.9 = (bf16[304,128]{1,0:T(8,128)(2,1)S(1)}, bf16[304,128]{1,0:T(8,128)(2,1)S(1)}, u32[]{:S(2)}, u32[]{:S(2)}) collective-permute-start(bf16[304,128]{1,0:T(8,128)(2,1)S(1)} %fusion), channel_id=1, source_target_pairs={{0,4},{1,5},{2,6},{3,7},{4,0},{5,1},{6,2},{7,3},{8,12},{9,13},{10,... | collective-permute-start | bytes 233480 | tf_op jit(solution)/shard_map/ppermute | solution.py:821
  32.4 1.8 %collective-permute-done.9 = bf16[304,128]{1,0:T(8,128)(2,1)S(1)} collective-permute-done((bf16[304,128]{1,0:T(8,128)(2,1)S(1)}, bf16[304,128]{1,0:T(8,128)(2,1)S(1)}, u32[]{:S(2)}, u32[]{:S(2)}) %collective-permute-start.9) | collective-permute-done | bytes 77856 | tf_op jit(solution)/shard_map/ppermute | solution.py:821
  34.3 2.5 %collective-permute-start.10 = (f32[304,128]{1,0:T(8,128)S(1)}, f32[304,128]{1,0:T(8,128)S(1)}, u32[]{:S(2)}, u32[]{:S(2)}) collective-permute-start(f32[304,128]{1,0:T(8,128)S(1)} %convert_add_fusion.mine_ref), channel_id=1, source_target_pairs={{0,1},{1,0},{2,3},{3,2},{4,5},{5,4},{6,7},{7,6},{8,9},{9,8},{10,11... | collective-permute-start | bytes 466952 | tf_op jit(solution)/shard_map/ppermute | solution.py:824
  36.8 0.7 %shard_map.76 = bf16[64,2048]{1,0:T(8,128)(2,1)} custom-call(bf16[64,2048]{1,0:T(8,128)(2,1)S(1)} %get-tuple-element.57.noise0, f32[12,88,128]{2,1,0:T(8,128)S(1)} %get-tuple-element.66.bi_o, f32[9,64,128]{2,1,0:T(8,128)S(1)} %get-tuple-element.76.bi_l), custom_call_target="tpu_custom_call" | custom-call | flops 1000 | bytes 1000 | tf_op jit(solution)/shard_map/pallas_call | solution.py:353
  37.5 0.3 collective-permute-done.10.other_ref
  37.8 1.0 %shard_map.77 = (f32[2,576,64]{2,1,0:T(8,128)}, f32[2,64]{1,0:T(2,128)}) custom-call(f32[304,128]{1,0:T(8,128)S(1)} %convert_add_fusion.mine_ref, f32[304,128]{1,0:T(8,128)S(1)} %collective-permute-done.10.other_ref), custom_call_target="tpu_custom_call" | custom-call | flops 1000 | bytes 1000 | tf_op jit(solution)/shard_map/pallas_call | solution.py:353
  (7 shorter events, 0.2 us)
Async XLA Ops:
  0.6 5.2 %copy-start = (bf16[1,2,3,3,64,64]{5,4,3,2,1,0:T(8,128)(2,1)S(1)}, bf16[1,2,3,3,64,64]{5,4,3,2,1,0:T(8,128)(2,1)}, u32[]{:S(2)}) copy-start(bf16[1,2,3,3,64,64]{5,4,3,2,1,0:T(8,128)(2,1)} %param.6) | copy-start | bytes 442372
  2.0 4.9 %collective-permute-start = (bf16[32,2048]{1,0:T(8,128)(2,1)S(1)}, bf16[32,2048]{1,0:T(8,128)(2,1)S(1)}, u32[]{:S(2)}, u32[]{:S(2)}) collective-permute-start(bf16[32,2048]{1,0:T(8,128)(2,1)S(1)} %get-tuple-element.42), channel_id=1, source_target_pairs={{0,1},{1,0},{2,3},{3,2},{4,5},{5,4},{6,7},{7,6},{8,9},{9,8},{10,11... | collective-permute-start | bytes 393224 | tf_op jit(solution)/shard_map/ppermute | solution.py:444
  2.7 6.3 %collective-permute-start.1 = (bf16[32,2048]{1,0:T(8,128)(2,1)S(1)}, bf16[32,2048]{1,0:T(8,128)(2,1)S(1)}, u32[]{:S(2)}, u32[]{:S(2)}) collective-permute-start(bf16[32,2048]{1,0:T(8,128)(2,1)S(1)} %get-tuple-element.43), channel_id=1, source_target_pairs={{1,2},{3,4},{5,6},{2,1},{4,3},{6,5},{9,10},{11,12},{13,14},{10,9},... | collective-permute-start | bytes 393224 | tf_op jit(solution)/shard_map/ppermute | solution.py:443
  6.2 5.4 %collective-permute-start.2 = (bf16[480,128]{1,0:T(8,128)(2,1)S(1)}, bf16[480,128]{1,0:T(8,128)(2,1)S(1)}, u32[]{:S(2)}, u32[]{:S(2)}) collective-permute-start(bf16[480,128]{1,0:T(8,128)(2,1)S(1)} %get-tuple-element.58), channel_id=1, source_target_pairs={{0,8},{1,9},{2,10},{3,11},{4,12},{5,13},{6,14},{7,15}} | collective-permute-start | bytes 368648 | tf_op jit(solution)/shard_map/ppermute | solution.py:460
  9.0 2.6 %collective-permute-start.3 = (bf16[320,128]{1,0:T(8,128)(2,1)S(1)}, bf16[320,128]{1,0:T(8,128)(2,1)S(1)}, u32[]{:S(2)}, u32[]{:S(2)}) collective-permute-start(bf16[320,128]{1,0:T(8,128)(2,1)S(1)} %get-tuple-element.59.rim_ref), channel_id=1, source_target_pairs={{0,8},{1,9},{2,10},{3,11},{4,12},{5,13},{6,14},{7,15}} | collective-permute-start | bytes 245768 | tf_op jit(solution)/shard_map/ppermute | solution.py:460
  9.7 7.2 %collective-permute-start.6 = (bf16[1056,128]{1,0:T(8,128)(2,1)S(1)}, bf16[1056,128]{1,0:T(8,128)(2,1)S(1)}, u32[]{:S(2)}, u32[]{:S(2)}) collective-permute-start(bf16[1056,128]{1,0:T(8,128)(2,1)S(1)} %shard_map.73), channel_id=1, source_target_pairs={{16,24},{17,25},{18,26},{19,27},{20,28},{21,29},{22,30},{23,31}} | collective-permute-start | bytes 811016 | tf_op jit(solution)/shard_map/ppermute | solution.py:460
  11.6 2.0 %collective-permute-start.4 = (bf16[416,128]{1,0:T(8,128)(2,1)S(1)}, bf16[416,128]{1,0:T(8,128)(2,1)S(1)}, u32[]{:S(2)}, u32[]{:S(2)}) collective-permute-start(bf16[416,128]{1,0:T(8,128)(2,1)S(1)} %get-tuple-element.68), channel_id=1, source_target_pairs={{8,16},{9,17},{10,18},{11,19},{12,20},{13,21},{14,22},{15,23}} | collective-permute-start | bytes 319496 | tf_op jit(solution)/shard_map/ppermute | solution.py:460
  12.3 8.9 %collective-permute-start.5 = (bf16[416,128]{1,0:T(8,128)(2,1)S(1)}, bf16[416,128]{1,0:T(8,128)(2,1)S(1)}, u32[]{:S(2)}, u32[]{:S(2)}) collective-permute-start(bf16[416,128]{1,0:T(8,128)(2,1)S(1)} %get-tuple-element.68), channel_id=1, source_target_pairs={{8,24},{9,25},{10,26},{11,27},{12,28},{13,29},{14,30},{15,31}} | collective-permute-start | bytes 319496 | tf_op jit(solution)/shard_map/ppermute | solution.py:460
  23.0 1.4 %collective-permute-start.7 = (f32[304,128]{1,0:T(8,128)S(1)}, f32[304,128]{1,0:T(8,128)S(1)}, u32[]{:S(2)}, u32[]{:S(2)}) collective-permute-start(f32[304,128]{1,0:T(8,128)S(1)} %get-tuple-element.78), channel_id=1, source_target_pairs={{0,1},{1,0},{2,3},{3,2},{4,5},{5,4},{6,7},{7,6},{8,9},{9,8},{10,11... | collective-permute-start | bytes 466952 | tf_op jit(solution)/shard_map/ppermute | solution.py:817
  24.5 5.5 %collective-permute-start.8 = (bf16[304,128]{1,0:T(8,128)(2,1)S(1)}, bf16[304,128]{1,0:T(8,128)(2,1)S(1)}, u32[]{:S(2)}, u32[]{:S(2)}) collective-permute-start(bf16[304,128]{1,0:T(8,128)(2,1)S(1)} %fusion.1), channel_id=1, source_target_pairs={{0,2},{1,3},{2,0},{3,1},{4,6},{5,7},{6,4},{7,5},{8,10},{9,11},{10,... | collective-permute-start | bytes 233480 | tf_op jit(solution)/shard_map/ppermute | solution.py:821
  30.1 4.2 %collective-permute-start.9 = (bf16[304,128]{1,0:T(8,128)(2,1)S(1)}, bf16[304,128]{1,0:T(8,128)(2,1)S(1)}, u32[]{:S(2)}, u32[]{:S(2)}) collective-permute-start(bf16[304,128]{1,0:T(8,128)(2,1)S(1)} %fusion), channel_id=1, source_target_pairs={{0,4},{1,5},{2,6},{3,7},{4,0},{5,1},{6,2},{7,3},{8,12},{9,13},{10,... | collective-permute-start | bytes 233480 | tf_op jit(solution)/shard_map/ppermute | solution.py:821
  34.3 3.5 %collective-permute-start.10 = (f32[304,128]{1,0:T(8,128)S(1)}, f32[304,128]{1,0:T(8,128)S(1)}, u32[]{:S(2)}, u32[]{:S(2)}) collective-permute-start(f32[304,128]{1,0:T(8,128)S(1)} %convert_add_fusion.mine_ref), channel_id=1, source_target_pairs={{0,1},{1,0},{2,3},{3,2},{4,5},{5,4},{6,7},{7,6},{8,9},{9,8},{10,11... | collective-permute-start | bytes 466952 | tf_op jit(solution)/shard_map/ppermute | solution.py:824

commit v4 on v3

--- a/solution.py
+++ b/solution.py
@@ -33,12 +33,12 @@
         self.error = error
         self.x_margin = error + 2
         self.x_rows = self.rows + 2 * (error + 2)
-        self.hidden_rows = up_to(self.rows + 2 * (error + 1), 16)
-        self.out_rows = up_to(self.rows + 2 * error, 16)
-        self.in_rows = up_to(self.rows + 2 * (error - 1), 16)
-        self.back_rows = up_to(self.rows + 2 * (error - 2), 16)
+        self.hidden_rows = up_to(self.rows + 2 * (error + 1) + 2, 8) - 2
+        self.out_rows = up_to(self.rows + 2 * error + 2, 8) - 2
+        self.in_rows = up_to(self.rows + 2 * (error - 1) + 2, 8) - 2
+        self.back_rows = up_to(self.rows + 2 * (error - 2) + 2, 8) - 2
         self.own_rows = up_to(self.rows, 16)
-        self.alloc = up_to(max(self.hidden_rows, self.x_margin + self.own_rows + 2) + 2, 8)
+        self.alloc = up_to(max(self.hidden_rows + 2, self.x_margin + self.own_rows + 2), 8)
 
 
 def levels_of(rows, cols, count):
@@ -108,18 +108,19 @@
     total = sum(rows for _, rows in segments)
     for first in range(0, count, chunk):
         size = min(chunk, count - first)
-        parts = []
-        for dy in range(3):
-            blocks = [source[first : first + size + 1, a + dy : a + dy + rows, :] for a, rows in segments]
-            block = blocks[0] if len(blocks) == 1 else jnp.concatenate(blocks, axis=1)
-            block = block.astype(BF16)
-            parts.append(block[:size].reshape(size * total, LANES))
-            parts.append(block[1:].reshape(size * total, LANES))
-        stacked = jnp.concatenate(parts, axis=1)
-        result = jnp.dot(stacked, kernel[...], preferred_element_type=F32).reshape(size, total, LANES)
+        blocks = [source[first : first + size + 1, a : a + rows, :] for a, rows in segments]
+        block = blocks[0] if len(blocks) == 1 else jnp.concatenate(blocks, axis=1)
+        left = block[:size].reshape(size * total, LANES).astype(BF16)
+        right = block[1:].reshape(size * total, LANES).astype(BF16)
+        by_row = jnp.dot(jnp.concatenate([left, right], axis=1), kernel[...], preferred_element_type=F32)
+        result = by_row[:, :LANES]
+        for dy in (1, 2):
+            part = by_row[:, dy * LANES : (dy + 1) * LANES]
+            result = result + pltpu.roll(part, size * total - dy, 0)
+        result = result.reshape(size, total, LANES)
         at = 0
         for a, rows in segments:
-            emit(first, size, a, rows, result[:, at : at + rows])
+            emit(first, size, a, rows - 2, result[:, at : at + rows - 2])
             at += rows
 
 
@@ -160,26 +161,29 @@
 def toeplitz(taps):
     half = LANES // 2
     zero = jnp.zeros((half, half), F32)
-    rows = []
+    columns = []
     for dy in range(3):
+        rows = []
         for k in range(4):
             left = taps[dy * 3 + k] if k < 3 else zero
             right = taps[dy * 3 + k - 1] if k > 0 else zero
             rows.append(jnp.concatenate([left, right], axis=1))
-    return jnp.concatenate(rows, axis=0)
+        columns.append(jnp.concatenate(rows, axis=0))
+    return jnp.concatenate(columns, axis=1)
 
 
 def toeplitz_back(taps):
     half = LANES // 2
     zero = jnp.zeros((half, half), F32)
-    columns = []
+    by_row = []
     for dy in range(3):
+        columns = []
         for k in range(4):
             top = taps[(2 - dy) * 3 + 2 - k] if k < 3 else zero
             bottom = taps[(2 - dy) * 3 + 3 - k] if k > 0 else zero
             columns.append(jnp.concatenate([top, bottom], axis=0))
-    pairs = [jnp.concatenate(columns[i : i + 2], axis=1).T for i in range(0, 12, 2)]
-    return jnp.concatenate(pairs, axis=0)
+        by_row.append(jnp.concatenate([jnp.concatenate(columns[i : i + 2], axis=1).T for i in (0, 2)], axis=0))
+    return jnp.concatenate(by_row, axis=1)
 
 
 def zero_tail(ref, level, rows):
@@ -215,12 +219,12 @@
         hb[first : first + size, a : a + rows, :] = jnp.where(keep, rounded(act), 0.0)
         d_in[first : first + size, a : a + rows, :] = slope(pre)
 
-    conv(xb, kernels[0], level.odd_pairs, hidden_parts or [(0, level.hidden_rows)], chunk, first_layer)
+    conv(xb, kernels[0], level.odd_pairs, hidden_parts or [(0, level.hidden_rows + 2)], chunk, first_layer)
 
     def second_layer(first, size, a, rows, value):
         d_out(first, size, a, rows, slope(value + bias_out))
 
-    conv(hb, kernels[1], level.pairs, out_parts or [(0, level.out_rows)], chunk, second_layer)
+    conv(hb, kernels[1], level.pairs, out_parts or [(0, level.out_rows + 2)], chunk, second_layer)
 
 
 def backward(level, eo, ei, kernels, d_in, grad, grad_row, bi, gu, place, chunk, in_parts=None, back_parts=None):
@@ -232,7 +236,7 @@
         part = d_in[first : first + size, 2 + a : 2 + a + rows, :]
         ei[first : first + size, a : a + rows, :] = jnp.where(keep, rounded(value * part), 0.0)
 
-    conv(eo, kernels[1], level.odd_pairs, in_parts or [(0, level.in_rows)], chunk, inner)
+    conv(eo, kernels[1], level.odd_pairs, in_parts or [(0, level.in_rows + 2)], chunk, inner)
 
     def outer(first, size, a, rows, value):
         if bi is not None:
@@ -243,7 +247,7 @@
             at = level.gu_row + a
             gu[first : first + size, at : at + rows, :] = jnp.where(mask, rounded(part + value), 0.0)
 
-    conv(ei, kernels[0], level.pairs, back_parts or [(0, level.back_rows)], chunk, outer)
+    conv(ei, kernels[0], level.pairs, back_parts or [(0, level.back_rows + 2)], chunk, outer)
 
 
 def write_noise(level, bi, noise):
@@ -453,17 +457,15 @@
     def matrix_body(taps_ref, bias_ref, forward_ref, back_ref):
         expand([taps_ref[t].astype(F32) for t in range(2 * TAPS)], forward_ref, back_ref)
 
-    matrix_shape = sds((2, 6 * LANES, LANES), BF16)
+    matrix_shape = sds((2, 2 * LANES, 3 * LANES), BF16)
     fwd_own, back_own = call(matrix_body, [matrix_shape, matrix_shape], [], [taps, bias_own])
 
     def across(value, pairs):
         return lax.ppermute(value, "section", pairs)
 
-    def ends(count):
-        return [(0, 24), (count - 24, 24)]
-
-    inside = [(16, row_count)]
-    assert fine.error == 15 and fine.hidden_rows == row_count + 32 == fine.back_rows
+    inside = [[(17, row_count)], [(16, row_count)]]
+    ends = [[(0, 24), (row_count + 10, 24)], [(0, 24), (row_count + 8, 24)]]
+    assert fine.error == 15 and fine.x_margin == 17 and row_count >= 32
     g_in = (4, second.rows - 8)
     g_end = second.error + g_in[0]
     in_rows = up_to(second.pairs * g_in[1], 16)
@@ -494,10 +496,11 @@
                 gb[p, g_margin : g_margin + row_count, :] = cot_ref[:, p * LANES : (p + 1) * LANES].astype(F32)
             forward(
                 level, xb, hb, [fwd_ref.at[0], fwd_ref.at[1]], bias_ref, db, error_of(level, gb, eo, place()),
-                place(), chunk, inside, inside,
+                place(), chunk, *inside,
             )
             backward(
-                level, eo, ei, [back_ref.at[0], back_ref.at[1]], db, gb, 0, bi, gu, place(), chunk, inside, inside
+                level, eo, ei, [back_ref.at[0], back_ref.at[1]], db, gb, 0, bi, gu, place(), chunk,
+                inside[1], inside[1],
             )
 
             def emit(m, span, rows):
@@ -517,7 +520,7 @@
         [coarse_buffer, pltpu.VMEM((in_rows + 16, LANES), F32)],
         [act, cot, fwd_own, back_own, bias_own],
     )
-    in_near = across(hop_in, [(0, 1)])
+    in_near = across(hop_in, [(0, 1), (1, 3), (3, 2), (2, 0)])
 
     def halo_readers(swap_ref, cross_ref):
         odd = is_odd()
@@ -532,7 +535,7 @@
 
     def rim_body(
         swap_ref, cross_ref, fwd_ref, back_ref, bias_ref, xi, hi, di, gi, oi, ii, bii, ui,
-        rim_ref, noise_ref, xb, hb, db, gb, eo, ei, bi, gu, rc, flat, tmp,
+        rim_ref, xb, hb, db, gb, eo, ei, bi, gu, rc, flat, tmp,
     ):
         section = lax.axis_index("section")
         top, low = halo_readers(swap_ref, cross_ref)
@@ -540,22 +543,23 @@
         @pl.when(section == 0)
         def _():
             level = fine
-            halo_input(level, xb, top, low, tmp, x_margin)
+            end = x_margin + row_count
             for p in range(level.pairs):
                 at = slice(p * LANES, (p + 1) * LANES)
                 tmp[0, 0:payload, :] = top(at)
                 tmp[1, 0:payload, :] = low(at)
+                xb[p + 1, 0:x_margin, :] = tmp[0, 0:x_margin, :]
+                xb[p + 1, end : end + x_margin, :] = tmp[1, 0:x_margin, :]
                 gb[p, 0:g_margin, :] = tmp[0, x_margin : x_margin + g_margin, :]
                 gb[p, g_margin + row_count : 2 * g_margin + row_count, :] = tmp[
                     1, x_margin : x_margin + g_margin, :
                 ]
-            parts = ends(level.hidden_rows)
             forward(
                 level, xb, hb, [fwd_ref.at[0], fwd_ref.at[1]], bias_ref, db, error_of(level, gb, eo, place()),
-                place(), chunk, parts, parts,
+                place(), chunk, ends[0], ends[0],
             )
             backward(
-                level, eo, ei, [back_ref.at[0], back_ref.at[1]], db, gb, 0, bi, gu, place(), chunk, parts, parts
+                level, eo, ei, [back_ref.at[0], back_ref.at[1]], db, gb, 0, bi, gu, place(), chunk, ends[1], ends[1]
             )
 
             def emit(m, span, rows):
@@ -570,18 +574,17 @@
                 emit, place(),
             )
             rim_ref[...] = flat[0:rim_rows, :].astype(BF16)
-            write_noise(level, bi, noise_ref)
 
     tmp_buffer = pltpu.VMEM((2, payload, LANES), F32)
-    rim, noise_first, *state = call(
+    rim, *state = call(
         rim_body,
-        [sds((rim_rows, LANES), BF16), strip_shape, *state_shapes],
+        [sds((rim_rows, LANES), BF16), *state_shapes],
         [coarse_buffer, pltpu.VMEM((rim_rows + 32, LANES), F32), tmp_buffer],
         [from_swap, from_cross, fwd_own, back_own, bias_own, *state],
-        aliases={5 + i: 2 + i for i in range(len(state_shapes))},
+        aliases={5 + i: 1 + i for i in range(len(state_shapes))},
         flops=2 * 10**9,
     )
-    rim_near = across(rim, [(0, 1)])
+    rim_near = across(rim, [(0, 1), (1, 3), (3, 2), (2, 0)])
 
     def ship_body(act_ref, swap_ref, cross_ref, taps_ref, both_ref, rim_ref, ship_ref, tmp, flat, bias_tmp):
         top, low = halo_readers(swap_ref, cross_ref)
@@ -726,7 +729,7 @@
         [in_near, rim_near, din_own, dout_own, back_own],
         flops=4 * 10**9,
     )
-    third_to_last = across(third_grad, [(1, 3)])
+    third_to_last = across(third_grad, [(1, 3), (3, 2), (2, 0), (0, 1)])
     third_to_own = across(third_grad, [(1, 2)])
 
     def shipped_body(ship_ref, own_ref, din_s, dout_s, back_s, fwd_s, xb, hb, own):
@@ -749,7 +752,7 @@
         shipped_body,
         [field(third, 1), field(third, 0), matrix_shape],
         [
-            pltpu.VMEM((2, 6 * LANES, LANES), BF16),
+            pltpu.VMEM((2, 2 * LANES, 3 * LANES), BF16),
             buffer(third, 2),
             buffer(third, 1),
             pltpu.VMEM((own_flat + 16, LANES), F32),
@@ -815,28 +818,28 @@
     )
 
     total = keep + lax.ppermute(send, "strip", swap_pairs)
-    hop_size = 2
-    while hop_size < strips:
+    step = 2
+    while step < strips:
         mine = lax.reduce_precision(total, 8, 7)
-        other = lax.ppermute(mine.astype(BF16), "strip", [(i, i ^ hop_size) for i in range(strips)])
-        total = mine + other.astype(F32)
-        hop_size *= 2
+        small = mine.astype(BF16)
+        offsets = (step, 2 * step, 3 * step) if 2 * step < strips else (step,)
+        got = [lax.ppermute(small, "strip", [(i, i ^ o) for i in range(strips)]).astype(F32) for o in offsets]
+        total = mine + got[0]
+        if len(got) == 3:
+            total = total + (got[1] + got[2])
+        step *= len(got) + 1
     other = lax.ppermute(total, "strip", swap_pairs)
 
-    def noise_body(noise0, bi_o, bi_l, noise_ref):
+    def noise_body(bi_f, bi_o, bi_l, noise_ref):
         section = lax.axis_index("section")
 
-        @pl.when(section == 0)
-        def _():
-            noise_ref[...] = noise0[...]
-
-        for level, source in ((second, bi_o), (third, bi_l), (last, bi_l)):
+        for level, source in ((fine, bi_f), (second, bi_o), (third, bi_l), (last, bi_l)):
 
             @pl.when(section == level.level)
             def _(level=level, source=source):
                 write_noise(level, source, noise_ref)
 
-    (noise,) = call(noise_body, [strip_shape], [], [noise_first, bi_own, bi_last], final=(0,))
+    (noise,) = call(noise_body, [strip_shape], [], [state[6], bi_own, bi_last], final=(0,))
 
     def final_body(mine_ref, other_ref, kernel_ref, bias_ref):
         odd = is_odd()

time: 39 us -> 37.6 us (0.964)
  the two profiles are of different devices: /device:TPU:7 before, /device:TPU:5 now
where the time goes in v4:
time: 37.6 us; the launch traced here: 37.2 us
  starting transfers between devices  16.5 us (44%)
  waiting for transfers between devices  14.3 us (38%)
  Pallas kernels  5.57 us (15%)
  between operations  0.77 us (2%)
    ppermute x5, starting transfers between devices, across(): return lax.ppermute(value, 'section', pairs)  6.88 us
    ppermute x3, waiting for transfers between devices, local(): lax.ppermute(small, 'strip', [(i, i ^ o) for i in range(strips)])  6.84 us
    pallas_call x11, Pallas kernels, call(): pl.pallas_call(body, out_shape=out_shape, in_specs=[pl.BlockSpec(memory_s...  5.57 us
    ppermute x5, waiting for transfers between devices, across(): return lax.ppermute(value, 'section', pairs)  4.99 us
    ppermute x3, starting transfers between devices, local(): lax.ppermute(small, 'strip', [(i, i ^ o) for i in range(strips)])  4.82 us
    ppermute x1, starting transfers between devices, local(): from_cross = lax.ppermute(to_cross, 'strip', cross_pairs)  3.1 us
    ppermute x1, waiting for transfers between devices, local(): total = keep + lax.ppermute(send, 'strip', swap_pairs)  1.37 us
    ppermute x1, starting transfers between devices, local(): other = lax.ppermute(total, 'strip', swap_pairs)  0.85 us
  transfers between devices with their start and end apart: 12, of which 6 were waited for; matrix products, arithmetic and copies ran while one was open for 0% of the time, Pallas kernels for 5%

profile of v4, /device:TPU:5, one launch (start us, length us, event | category | flops | bytes accessed | tf_op | source)
XLA Modules:
  0.0 37.2 jit_solution(13563277423873721632)
XLA Ops:
  0.6 0.0 copy-start
  0.6 1.3 %shard_map.67 = (bf16[64,2048]{1,0:T(8,128)(2,1)S(1)}, bf16[64,2048]{1,0:T(8,128)(2,1)S(1)}, f32[8,128]{1,0:T(8,128)S(1)}, bf16[32,2048]{1,0:T(8,128)(2,1)S(1)}, bf16[32,2048]{1,0:T(8,128)(2,1)S(1)}) custom-call(bf16[64,2048]{1,0:T(8,128)(2,1)} %bitcast.10, bf16[64,2048]{1,0:T(8,128)(2,1)} %bitcast.11, f32[2,64]{1,0:T(2,128)} %bitcast.12), custom_call_target="tpu_custom_call" | custom-call | flops 1000 | bytes 1000 | tf_op jit(solution)/shard_map/pallas_call | solution.py:357
  2.0 0.7 %collective-permute-start = (bf16[32,2048]{1,0:T(8,128)(2,1)S(1)}, bf16[32,2048]{1,0:T(8,128)(2,1)S(1)}, u32[]{:S(2)}, u32[]{:S(2)}) collective-permute-start(bf16[32,2048]{1,0:T(8,128)(2,1)S(1)} %get-tuple-element.42), channel_id=1, source_target_pairs={{0,1},{1,0},{2,3},{3,2},{4,5},{5,4},{6,7},{7,6},{8,9},{9,8},{10,11... | collective-permute-start | bytes 393224 | tf_op jit(solution)/shard_map/ppermute | solution.py:448
  2.7 3.1 %collective-permute-start.1 = (bf16[32,2048]{1,0:T(8,128)(2,1)S(1)}, bf16[32,2048]{1,0:T(8,128)(2,1)S(1)}, u32[]{:S(2)}, u32[]{:S(2)}) collective-permute-start(bf16[32,2048]{1,0:T(8,128)(2,1)S(1)} %get-tuple-element.43), channel_id=1, source_target_pairs={{1,2},{3,4},{5,6},{2,1},{4,3},{6,5},{9,10},{11,12},{13,14},{10,9},... | collective-permute-start | bytes 393224 | tf_op jit(solution)/shard_map/ppermute | solution.py:447
  5.8 0.0 copy-done
  5.8 0.3 shard_map.68
  6.2 2.3 %collective-permute-start.2 = (bf16[480,128]{1,0:T(8,128)(2,1)S(1)}, bf16[480,128]{1,0:T(8,128)(2,1)S(1)}, u32[]{:S(2)}, u32[]{:S(2)}) collective-permute-start(bf16[480,128]{1,0:T(8,128)(2,1)S(1)} %get-tuple-element.58), channel_id=1, source_target_pairs={{0,8},{8,24},{24,16},{16,0},{1,9},{9,25},{25,17},{17,1},{2,10},{10... | collective-permute-start | bytes 368648 | tf_op jit(solution)/shard_map/ppermute | solution.py:464
  8.5 0.0 collective-permute-done.swap_ref
  8.5 0.8 %collective-permute-done.1.cross_ref = bf16[32,2048]{1,0:T(8,128)(2,1)S(1)} collective-permute-done((bf16[32,2048]{1,0:T(8,128)(2,1)S(1)}, bf16[32,2048]{1,0:T(8,128)(2,1)S(1)}, u32[]{:S(2)}, u32[]{:S(2)}) %collective-permute-start.1) | collective-permute-done | bytes 131104 | tf_op jit(solution)/shard_map/ppermute | solution.py:447
  9.3 1.5 %collective-permute-start.3 = (bf16[320,128]{1,0:T(8,128)(2,1)S(1)}, bf16[320,128]{1,0:T(8,128)(2,1)S(1)}, u32[]{:S(2)}, u32[]{:S(2)}) collective-permute-start(bf16[320,128]{1,0:T(8,128)(2,1)S(1)} %get-tuple-element.59.rim_ref), channel_id=1, source_target_pairs={{0,8},{8,24},{24,16},{16,0},{1,9},{9,25},{25,17},{17,1},{2,10},{10... | collective-permute-start | bytes 245768 | tf_op jit(solution)/shard_map/ppermute | solution.py:464
  10.7 0.1 shard_map.73
  10.9 1.8 %collective-permute-start.6 = (bf16[1056,128]{1,0:T(8,128)(2,1)S(1)}, bf16[1056,128]{1,0:T(8,128)(2,1)S(1)}, u32[]{:S(2)}, u32[]{:S(2)}) collective-permute-start(bf16[1056,128]{1,0:T(8,128)(2,1)S(1)} %shard_map.73), channel_id=1, source_target_pairs={{16,24},{17,25},{18,26},{19,27},{20,28},{21,29},{22,30},{23,31}} | collective-permute-start | bytes 811016 | tf_op jit(solution)/shard_map/ppermute | solution.py:464
  12.7 0.7 %shard_map.71 = (f32[13,72,128]{2,1,0:T(8,128)S(1)}, f32[12,72,128]{2,1,0:T(8,128)S(1)}, f32[13,72,128]{2,1,0:T(8,128)S(1)}, f32[14,72,128]{2,1,0:T(8,128)S(1)}, f32[2,304,128]{2,1,0:T(8,128)S(1)}) custom-call(bf16[64,2048]{1,0:T(8,128)(2,1)S(1)} %get-tuple-element.47.act_ref, bf16[32,2048]{1,0:T(8,128)(2,1)S(1)} %collective-permute-done.swap_ref, ...), custom_call_target="tpu_custom_call" | custom-call | flops 1000 | bytes 1000 | tf_op jit(solution)/shard_map/pallas_call | solution.py:357
  13.4 0.0 collective-permute-done.2.in_ref
  13.4 0.0 collective-permute-done.3.rim_ref
  13.4 1.3 %collective-permute-start.4 = (bf16[416,128]{1,0:T(8,128)(2,1)S(1)}, bf16[416,128]{1,0:T(8,128)(2,1)S(1)}, u32[]{:S(2)}, u32[]{:S(2)}) collective-permute-start(bf16[416,128]{1,0:T(8,128)(2,1)S(1)} %get-tuple-element.68), channel_id=1, source_target_pairs={{8,16},{9,17},{10,18},{11,19},{12,20},{13,21},{14,22},{15,23}} | collective-permute-start | bytes 319496 | tf_op jit(solution)/shard_map/ppermute | solution.py:464
  14.7 0.1 collective-permute-start.5
  14.8 5.0 %collective-permute-done.4.own_ref = bf16[416,128]{1,0:T(8,128)(2,1)S(1)} collective-permute-done((bf16[416,128]{1,0:T(8,128)(2,1)S(1)}, bf16[416,128]{1,0:T(8,128)(2,1)S(1)}, u32[]{:S(2)}, u32[]{:S(2)}) %collective-permute-start.4) | collective-permute-done | bytes 106528 | tf_op jit(solution)/shard_map/ppermute | solution.py:464
  19.7 0.0 collective-permute-done.6.ship_ref
  19.8 0.0 collective-permute-done.5.last_ref
  19.8 1.4 %shard_map.75 = (f32[304,128]{1,0:T(8,128)S(1)}, f32[304,128]{1,0:T(8,128)S(1)}, f32[9,64,128]{2,1,0:T(8,128)S(1)}) custom-call(f32[2,304,128]{2,1,0:T(8,128)S(1)} %get-tuple-element.67.pair0, bf16[416,128]{1,0:T(8,128)(2,1)S(1)} %collective-permute-done.4.own_ref, bf16[416,128]{1,0:T(8,128)(2,1)S(1)} %collective-permute-done.5.last_ref, ...), custom_call_target="tpu_custom_call" | custom-call | flops 1000 | bytes 1000 | tf_op jit(solution)/shard_map/pallas_call | solution.py:357
  21.1 0.1 collective-permute-start.7
  21.2 1.4 %collective-permute-done.7 = f32[304,128]{1,0:T(8,128)S(1)} collective-permute-done((f32[304,128]{1,0:T(8,128)S(1)}, f32[304,128]{1,0:T(8,128)S(1)}, u32[]{:S(2)}, u32[]{:S(2)}) %collective-permute-start.7) | collective-permute-done | bytes 155680 | tf_op jit(solution)/shard_map/ppermute | solution.py:820
  22.6 4.5 %collective-permute-start.10 = (bf16[304,128]{1,0:T(8,128)(2,1)S(1)}, bf16[304,128]{1,0:T(8,128)(2,1)S(1)}, u32[]{:S(2)}, u32[]{:S(2)}) collective-permute-start(bf16[304,128]{1,0:T(8,128)(2,1)S(1)} %fusion), channel_id=1, source_target_pairs={{0,6},{1,7},{2,4},{3,5},{4,2},{5,3},{6,0},{7,1},{8,14},{9,15},{10,... | collective-permute-start | bytes 233480 | tf_op jit(solution)/shard_map/ppermute | solution.py:826
  27.1 0.0 collective-permute-start.9
  27.1 0.4 collective-permute-start.8
  27.4 2.1 %collective-permute-done.10 = bf16[304,128]{1,0:T(8,128)(2,1)S(1)} collective-permute-done((bf16[304,128]{1,0:T(8,128)(2,1)S(1)}, bf16[304,128]{1,0:T(8,128)(2,1)S(1)}, u32[]{:S(2)}, u32[]{:S(2)}) %collective-permute-start.10) | collective-permute-done | bytes 77856 | tf_op jit(solution)/shard_map/ppermute | solution.py:826
  29.5 4.7 %collective-permute-done.9 = bf16[304,128]{1,0:T(8,128)(2,1)S(1)} collective-permute-done((bf16[304,128]{1,0:T(8,128)(2,1)S(1)}, bf16[304,128]{1,0:T(8,128)(2,1)S(1)}, u32[]{:S(2)}, u32[]{:S(2)}) %collective-permute-start.9) | collective-permute-done | bytes 77856 | tf_op jit(solution)/shard_map/ppermute | solution.py:826
  34.3 0.0 collective-permute-done.8
  34.3 0.1 add_add_fusion.mine_ref
  34.3 0.9 %collective-permute-start.11 = (f32[304,128]{1,0:T(8,128)S(1)}, f32[304,128]{1,0:T(8,128)S(1)}, u32[]{:S(2)}, u32[]{:S(2)}) collective-permute-start(f32[304,128]{1,0:T(8,128)S(1)} %add_add_fusion.mine_ref), channel_id=1, source_target_pairs={{0,1},{1,0},{2,3},{3,2},{4,5},{5,4},{6,7},{7,6},{8,9},{9,8},{10,11... | collective-permute-start | bytes 466952 | tf_op jit(solution)/shard_map/ppermute | solution.py:831
  35.2 0.7 %shard_map.76 = bf16[64,2048]{1,0:T(8,128)(2,1)} custom-call(f32[16,104,128]{2,1,0:T(8,128)S(1)} %get-tuple-element.57.bi_f, f32[12,72,128]{2,1,0:T(8,128)S(1)} %get-tuple-element.66.bi_o, f32[9,64,128]{2,1,0:T(8,128)S(1)} %get-tuple-element.76.bi_l), custom_call_target="tpu_custom_call" | custom-call | flops 1000 | bytes 1000 | tf_op jit(solution)/shard_map/pallas_call | solution.py:357
  35.9 0.3 collective-permute-done.11.other_ref
  36.2 1.0 %shard_map.77 = (f32[2,576,64]{2,1,0:T(8,128)}, f32[2,64]{1,0:T(2,128)}) custom-call(f32[304,128]{1,0:T(8,128)S(1)} %add_add_fusion.mine_ref, f32[304,128]{1,0:T(8,128)S(1)} %collective-permute-done.11.other_ref), custom_call_target="tpu_custom_call" | custom-call | flops 1000 | bytes 1000 | tf_op jit(solution)/shard_map/pallas_call | solution.py:357
  (5 shorter events, 0.1 us)
Async XLA Ops:
  0.6 5.2 %copy-start = (bf16[1,2,3,3,64,64]{5,4,3,2,1,0:T(8,128)(2,1)S(1)}, bf16[1,2,3,3,64,64]{5,4,3,2,1,0:T(8,128)(2,1)}, u32[]{:S(2)}) copy-start(bf16[1,2,3,3,64,64]{5,4,3,2,1,0:T(8,128)(2,1)} %param.6) | copy-start | bytes 442372
  2.0 6.5 %collective-permute-start = (bf16[32,2048]{1,0:T(8,128)(2,1)S(1)}, bf16[32,2048]{1,0:T(8,128)(2,1)S(1)}, u32[]{:S(2)}, u32[]{:S(2)}) collective-permute-start(bf16[32,2048]{1,0:T(8,128)(2,1)S(1)} %get-tuple-element.42), channel_id=1, source_target_pairs={{0,1},{1,0},{2,3},{3,2},{4,5},{5,4},{6,7},{7,6},{8,9},{9,8},{10,11... | collective-permute-start | bytes 393224 | tf_op jit(solution)/shard_map/ppermute | solution.py:448
  2.7 6.6 %collective-permute-start.1 = (bf16[32,2048]{1,0:T(8,128)(2,1)S(1)}, bf16[32,2048]{1,0:T(8,128)(2,1)S(1)}, u32[]{:S(2)}, u32[]{:S(2)}) collective-permute-start(bf16[32,2048]{1,0:T(8,128)(2,1)S(1)} %get-tuple-element.43), channel_id=1, source_target_pairs={{1,2},{3,4},{5,6},{2,1},{4,3},{6,5},{9,10},{11,12},{13,14},{10,9},... | collective-permute-start | bytes 393224 | tf_op jit(solution)/shard_map/ppermute | solution.py:447
  6.2 7.2 %collective-permute-start.2 = (bf16[480,128]{1,0:T(8,128)(2,1)S(1)}, bf16[480,128]{1,0:T(8,128)(2,1)S(1)}, u32[]{:S(2)}, u32[]{:S(2)}) collective-permute-start(bf16[480,128]{1,0:T(8,128)(2,1)S(1)} %get-tuple-element.58), channel_id=1, source_target_pairs={{0,8},{8,24},{24,16},{16,0},{1,9},{9,25},{25,17},{17,1},{2,10},{10... | collective-permute-start | bytes 368648 | tf_op jit(solution)/shard_map/ppermute | solution.py:464
  9.3 4.1 %collective-permute-start.3 = (bf16[320,128]{1,0:T(8,128)(2,1)S(1)}, bf16[320,128]{1,0:T(8,128)(2,1)S(1)}, u32[]{:S(2)}, u32[]{:S(2)}) collective-permute-start(bf16[320,128]{1,0:T(8,128)(2,1)S(1)} %get-tuple-element.59.rim_ref), channel_id=1, source_target_pairs={{0,8},{8,24},{24,16},{16,0},{1,9},{9,25},{25,17},{17,1},{2,10},{10... | collective-permute-start | bytes 245768 | tf_op jit(solution)/shard_map/ppermute | solution.py:464
  10.9 8.9 %collective-permute-start.6 = (bf16[1056,128]{1,0:T(8,128)(2,1)S(1)}, bf16[1056,128]{1,0:T(8,128)(2,1)S(1)}, u32[]{:S(2)}, u32[]{:S(2)}) collective-permute-start(bf16[1056,128]{1,0:T(8,128)(2,1)S(1)} %shard_map.73), channel_id=1, source_target_pairs={{16,24},{17,25},{18,26},{19,27},{20,28},{21,29},{22,30},{23,31}} | collective-permute-start | bytes 811016 | tf_op jit(solution)/shard_map/ppermute | solution.py:464
  13.4 6.3 %collective-permute-start.4 = (bf16[416,128]{1,0:T(8,128)(2,1)S(1)}, bf16[416,128]{1,0:T(8,128)(2,1)S(1)}, u32[]{:S(2)}, u32[]{:S(2)}) collective-permute-start(bf16[416,128]{1,0:T(8,128)(2,1)S(1)} %get-tuple-element.68), channel_id=1, source_target_pairs={{8,16},{9,17},{10,18},{11,19},{12,20},{13,21},{14,22},{15,23}} | collective-permute-start | bytes 319496 | tf_op jit(solution)/shard_map/ppermute | solution.py:464
  14.7 5.1 %collective-permute-start.5 = (bf16[416,128]{1,0:T(8,128)(2,1)S(1)}, bf16[416,128]{1,0:T(8,128)(2,1)S(1)}, u32[]{:S(2)}, u32[]{:S(2)}) collective-permute-start(bf16[416,128]{1,0:T(8,128)(2,1)S(1)} %get-tuple-element.68), channel_id=1, source_target_pairs={{8,24},{24,16},{16,0},{0,8},{9,25},{25,17},{17,1},{1,9},{10,26},{2... | collective-permute-start | bytes 319496 | tf_op jit(solution)/shard_map/ppermute | solution.py:464
  21.1 1.4 %collective-permute-start.7 = (f32[304,128]{1,0:T(8,128)S(1)}, f32[304,128]{1,0:T(8,128)S(1)}, u32[]{:S(2)}, u32[]{:S(2)}) collective-permute-start(f32[304,128]{1,0:T(8,128)S(1)} %get-tuple-element.78), channel_id=1, source_target_pairs={{0,1},{1,0},{2,3},{3,2},{4,5},{5,4},{6,7},{7,6},{8,9},{9,8},{10,11... | collective-permute-start | bytes 466952 | tf_op jit(solution)/shard_map/ppermute | solution.py:820
  22.6 6.9 %collective-permute-start.10 = (bf16[304,128]{1,0:T(8,128)(2,1)S(1)}, bf16[304,128]{1,0:T(8,128)(2,1)S(1)}, u32[]{:S(2)}, u32[]{:S(2)}) collective-permute-start(bf16[304,128]{1,0:T(8,128)(2,1)S(1)} %fusion), channel_id=1, source_target_pairs={{0,6},{1,7},{2,4},{3,5},{4,2},{5,3},{6,0},{7,1},{8,14},{9,15},{10,... | collective-permute-start | bytes 233480 | tf_op jit(solution)/shard_map/ppermute | solution.py:826
  27.1 7.2 %collective-permute-start.9 = (bf16[304,128]{1,0:T(8,128)(2,1)S(1)}, bf16[304,128]{1,0:T(8,128)(2,1)S(1)}, u32[]{:S(2)}, u32[]{:S(2)}) collective-permute-start(bf16[304,128]{1,0:T(8,128)(2,1)S(1)} %fusion), channel_id=1, source_target_pairs={{0,4},{1,5},{2,6},{3,7},{4,0},{5,1},{6,2},{7,3},{8,12},{9,13},{10,... | collective-permute-start | bytes 233480 | tf_op jit(solution)/shard_map/ppermute | solution.py:826
  27.1 7.2 %collective-permute-start.8 = (bf16[304,128]{1,0:T(8,128)(2,1)S(1)}, bf16[304,128]{1,0:T(8,128)(2,1)S(1)}, u32[]{:S(2)}, u32[]{:S(2)}) collective-permute-start(bf16[304,128]{1,0:T(8,128)(2,1)S(1)} %fusion), channel_id=1, source_target_pairs={{0,2},{1,3},{2,0},{3,1},{4,6},{5,7},{6,4},{7,5},{8,10},{9,11},{10,... | collective-permute-start | bytes 233480 | tf_op jit(solution)/shard_map/ppermute | solution.py:826
  34.3 1.9 %collective-permute-start.11 = (f32[304,128]{1,0:T(8,128)S(1)}, f32[304,128]{1,0:T(8,128)S(1)}, u32[]{:S(2)}, u32[]{:S(2)}) collective-permute-start(f32[304,128]{1,0:T(8,128)S(1)} %add_add_fusion.mine_ref), channel_id=1, source_target_pairs={{0,1},{1,0},{2,3},{3,2},{4,5},{5,4},{6,7},{7,6},{8,9},{9,8},{10,11... | collective-permute-start | bytes 466952 | tf_op jit(solution)/shard_map/ppermute | solution.py:831

commit v5 on v4

--- a/solution.py
+++ b/solution.py
@@ -148,14 +148,19 @@
 
 def pack_kernel_terms(out_ref, product, total, scale):
     half = LANES // 2
-    by_tap = product.T * scale
-    lane = lane_index((1, LANES))
+    low = lane_index((1, LANES)) < half
+    thirds = []
     for dy in range(3):
-        block = by_tap[dy * 2 * LANES : (dy + 1) * 2 * LANES]
-        folded = block[: 3 * half] + half_swap(block)[half:]
-        out_ref[dy * 96 : dy * 96 + 96, :] = jnp.where(lane < half, folded[:96], half_swap(folded[96:]))
+        first = product[:, 2 * dy * LANES : (2 * dy + 1) * LANES]
+        then = product[:, (2 * dy + 1) * LANES : (2 * dy + 2) * LANES]
+        moved = half_swap(then[half:])
+        out_ref[dy * half : (dy + 1) * half, :] = (
+            first[:half] + jnp.where(low, half_swap(first[half:]), moved)
+        ) * scale
+        thirds.append((then[:half] + moved) * scale)
     bias = (total + half_swap(total)) * scale
-    out_ref[288:304, :] = jnp.broadcast_to(bias, (16, LANES))
+    out_ref[3 * half : 4 * half, :] = jnp.where(low, thirds[0], half_swap(thirds[1]))
+    out_ref[4 * half : 5 * half, :] = jnp.where(low, thirds[2], bias)
 
 
 def toeplitz(taps):
@@ -623,7 +628,7 @@
     )
     shipped = across(ship, [(2, 3)])
 
-    grad_rows = up_to(packed_rows // 2 + 1, 16)
+    grad_rows = 5 * channels
 
     def gradients(level, source, hidden, err_in, err_out, rows_at, pair_out):
         scale = np.float32(1.0 / math.sqrt(strips * level.rows * level.cols))
@@ -694,20 +699,55 @@
             emit, place(),
         )
 
-    def second_body(
-        in_ref, rim_ref, din_o, dout_o, back_o, third_ref, eo, ei, bi, gb, gu, rc, mid, rims, flat
+    def second_error(gb, d_out, eo, first, rows):
+        mask = image_mask(second, first - second.error, rows, *place())
+        for p in range(second.pairs):
+            part = gb[p, first : first + rows, :] * d_out[p, first : first + rows, :]
+            eo[p + 1, first : first + rows, :] = jnp.where(mask[0], rounded(part), 0.0)
+
+    def second_inside_body(in_ref, din_o, dout_o, back_o, eo, ei, bi, gu, gb, mid):
+        @pl.when(lax.axis_index("section") == 1)
+        def _():
+            mid[...] = in_ref[...].astype(F32)
+            for p in range(second.pairs):
+                gb[p, g_end : g_end + g_in[1], :] = mid[p * g_in[1] : (p + 1) * g_in[1], :]
+            zero_edges(eo, second)
+            zero_tail(ei, second, second.alloc)
+            second_error(gb, dout_o, eo, g_end, g_in[1])
+            parts = [(g_end, g_in[1])]
+            backward(second, eo, ei, [back_o.at[0], back_o.at[1]], din_o, gb, 0, bi, gu, place(), chunk, parts, parts)
+
+    inside_shapes = [
+        field(second, 2), field(second, 1), field(second, 0),
+        sds((second.pairs, second.alloc + 8, LANES), F32), field(second, 0),
+    ]
+    inside_state = call(
+        second_inside_body,
+        inside_shapes,
+        [pltpu.VMEM((in_rows, LANES), F32)],
+        [in_near, din_own, dout_own, back_own],
+    )
+
+    def second_rim_body(
+        rim_ref, din_o, dout_o, back_o, eo_i, ei_i, bi_i, gu_i, gb_i, third_ref, eo, ei, bi, gu, gb, rc, rims, flat
     ):
         @pl.when(lax.axis_index("section") == 1)
         def _():
-            mid[...] = in_ref[...].astype(F32)
             rims[...] = rim_ref[...].astype(F32)
             low = g_end + g_in[1]
             for p in range(second.pairs):
                 at = p * 2 * g_end
                 gb[p, 0:g_end, :] = rims[at : at + g_end, :]
-                gb[p, g_end:low, :] = mid[p * g_in[1] : (p + 1) * g_in[1], :]
                 gb[p, low : low + g_end, :] = rims[at + g_end : at + 2 * g_end, :]
-            step(second, gb, 0, din_o, dout_o, back_o, eo, ei, bi, gu)
+            second_error(gb, dout_o, eo, 0, g_end)
+            second_error(gb, dout_o, eo, low, g_end)
+            rows = up_to(g_end + 2, 8)
+            in_parts = [(0, rows), (low + g_end - rows, rows)]
+            back_parts = [(0, rows), (low + g_end - 2 - rows, rows)]
+            backward(
+                second, eo, ei, [back_o.at[0], back_o.at[1]], din_o, gb, 0, bi, gu, place(), chunk,
+                in_parts, back_parts,
+            )
             hand_down(second, third, gu, rc, gb)
             at = second.up_shift
             for p in range(third.pairs):
@@ -715,24 +755,22 @@
             third_ref[...] = flat[0:third_flat, :].astype(BF16)
 
     coarse_tmp = pltpu.VMEM((second.pairs, 3 * second.k_count + 8, LANES), F32)
-    third_grad, eo_own, ei_own, bi_own = call(
-        second_body,
-        [sds((third_flat, LANES), BF16), field(second, 2), field(second, 1), field(second, 0)],
-        [
-            buffer(second, 0),
-            buffer(fine, 0),
-            coarse_tmp,
-            pltpu.VMEM((in_rows, LANES), F32),
-            pltpu.VMEM((rim_rows, LANES), F32),
-            pltpu.VMEM((third_flat + 16, LANES), F32),
-        ],
-        [in_near, rim_near, din_own, dout_own, back_own],
+    third_grad, eo_own, ei_own, bi_own, *_ = call(
+        second_rim_body,
+        [sds((third_flat, LANES), BF16), *inside_shapes],
+        [coarse_tmp, pltpu.VMEM((rim_rows, LANES), F32), pltpu.VMEM((third_flat + 16, LANES), F32)],
+        [rim_near, din_own, dout_own, back_own, *inside_state],
+        aliases={4 + i: 1 + i for i in range(len(inside_shapes))},
         flops=4 * 10**9,
     )
     third_to_last = across(third_grad, [(1, 3), (3, 2), (2, 0), (0, 1)])
     third_to_own = across(third_grad, [(1, 2)])
 
-    def shipped_body(ship_ref, own_ref, din_s, dout_s, back_s, fwd_s, xb, hb, own):
+    def shipped_body(ship_ref, own_ref, x_o, hid_o, eo_o, ei_o, din_s, dout_s, back_s, pair_ref, fwd_s, xb, hb, own):
+        @pl.when(lax.axis_index("section") == 1)
+        def _():
+            finish(second, x_o, hid_o, ei_o, eo_o, pair_ref)
+
         @pl.when(lax.axis_index("section") == 3)
         def _():
             level = third
@@ -748,20 +786,20 @@
             zero_tail(hb, level, level.hidden_rows)
             forward(level, xb, hb, [fwd_s.at[0], fwd_s.at[1]], bias, din_s, store_in(level, dout_s), place(), chunk)
 
-    din_s, dout_s, back_s = call(
+    din_s, dout_s, back_s, pair_second = call(
         shipped_body,
-        [field(third, 1), field(third, 0), matrix_shape],
+        [field(third, 1), field(third, 0), matrix_shape, pair_shape],
         [
             pltpu.VMEM((2, 2 * LANES, 3 * LANES), BF16),
             buffer(third, 2),
             buffer(third, 1),
             pltpu.VMEM((own_flat + 16, LANES), F32),
         ],
-        [shipped, third_to_own],
+        [shipped, third_to_own, x_own, hid_own, eo_own, ei_own],
     )
 
     def last_body(
-        pair0, own_ref, last_ref, din_o, dout_o, hid_o, x_o, back_o, din_s, dout_s, back_s, eo_o, ei_o,
+        pair0, pair1, own_ref, last_ref, din_o, dout_o, hid_o, x_o, back_o, din_s, dout_s, back_s,
         keep_ref, send_ref, bi, pair_out, gb, eo, ei, gu, rc, flat,
     ):
         section = lax.axis_index("section")
@@ -778,7 +816,7 @@
 
         @pl.when(section == 1)
         def _():
-            finish(second, x_o, hid_o, ei_o, eo_o, pair_out)
+            pair_out[...] = pair1[...]
 
         @pl.when(section == 2)
         def _():
@@ -812,8 +850,8 @@
             pltpu.VMEM((third_flat, LANES), F32),
         ],
         [
-            pair_first, third_to_own, third_to_last, din_own, dout_own, hid_own, x_own, back_own,
-            din_s, dout_s, back_s, eo_own, ei_own,
+            pair_first, pair_second, third_to_own, third_to_last, din_own, dout_own, hid_own, x_own, back_own,
+            din_s, dout_s, back_s,
         ],
     )
 
@@ -843,16 +881,19 @@
 
     def final_body(mine_ref, other_ref, kernel_ref, bias_ref):
         odd = is_odd()
+        half = channels
         for c in range(2):
             if c == 0:
                 value = jnp.where(odd, other_ref[...], mine_ref[...])
             else:
                 value = jnp.where(odd, mine_ref[...], other_ref[...])
-            swapped = half_swap(value)
             for dy in range(3):
-                kernel_ref[c, dy * 192 : dy * 192 + 96, :] = value[dy * 96 : dy * 96 + 96, :channels]
-                kernel_ref[c, dy * 192 + 96 : dy * 192 + 192, :] = swapped[dy * 96 : dy * 96 + 96, :channels]
-            bias_ref[c : c + 1, :] = value[288:289, :channels]
+                kernel_ref[c, dy * 192 : dy * 192 + 128, :] = value[dy * half : (dy + 1) * half].T
+            pair = value[3 * half : 4 * half].T
+            kernel_ref[c, 128:192, :] = pair[:half]
+            kernel_ref[c, 320:384, :] = pair[half:]
+            kernel_ref[c, 512:576, :] = value[4 * half : 5 * half].T[:half]
+            bias_ref[c : c + 1, :] = half_swap(value[4 * half : 4 * half + 1])[:, :half]
 
     kernel_sum, bias_sum = call(
         final_body,

time: 37.6 us -> 37.4 us (level)
    pallas_call x11 -> x12, Pallas kernels: 5.57 us -> 5.24 us  [call(): pl.pallas_call(body, out_shape=out_shape, in_specs=[pl.BlockSpec(memory_s...]
where the time goes in v5:
time: 37.4 us; the launch traced here: 37.2 us
  starting transfers between devices  16.5 us (44%)
  waiting for transfers between devices  14.6 us (39%)
  Pallas kernels  5.24 us (14%)
  between operations  0.78 us (2%)
    ppermute x3, waiting for transfers between devices, local(): lax.ppermute(small, 'strip', [(i, i ^ o) for i in range(strips)])  7.15 us
    ppermute x5, starting transfers between devices, across(): return lax.ppermute(value, 'section', pairs)  6.88 us
    pallas_call x12, Pallas kernels, call(): pl.pallas_call(body, out_shape=out_shape, in_specs=[pl.BlockSpec(memory_s...  5.24 us
    ppermute x5, waiting for transfers between devices, across(): return lax.ppermute(value, 'section', pairs)  4.99 us
    ppermute x3, starting transfers between devices, local(): lax.ppermute(small, 'strip', [(i, i ^ o) for i in range(strips)])  4.82 us
    ppermute x1, starting transfers between devices, local(): from_cross = lax.ppermute(to_cross, 'strip', cross_pairs)  3.1 us
    ppermute x1, waiting for transfers between devices, local(): total = keep + lax.ppermute(send, 'strip', swap_pairs)  1.38 us
    ppermute x1, starting transfers between devices, local(): other = lax.ppermute(total, 'strip', swap_pairs)  0.88 us
  transfers between devices with their start and end apart: 12, of which 6 were waited for; matrix products, arithmetic and copies ran while one was open for 0% of the time, Pallas kernels for 5%

profile of v5, /device:TPU:5, one launch (start us, length us, event | category | flops | bytes accessed | tf_op | source)
XLA Modules:
  0.0 37.2 jit_solution(10735957151348363358)
XLA Ops:
  0.6 0.0 copy-start
  0.6 1.3 %shard_map.67 = (bf16[64,2048]{1,0:T(8,128)(2,1)S(1)}, bf16[64,2048]{1,0:T(8,128)(2,1)S(1)}, f32[8,128]{1,0:T(8,128)S(1)}, bf16[32,2048]{1,0:T(8,128)(2,1)S(1)}, bf16[32,2048]{1,0:T(8,128)(2,1)S(1)}) custom-call(bf16[64,2048]{1,0:T(8,128)(2,1)} %bitcast.10, bf16[64,2048]{1,0:T(8,128)(2,1)} %bitcast.11, f32[2,64]{1,0:T(2,128)} %bitcast.12), custom_call_target="tpu_custom_call" | custom-call | flops 1000 | bytes 1000 | tf_op jit(solution)/shard_map/pallas_call | solution.py:362
  2.0 0.7 %collective-permute-start = (bf16[32,2048]{1,0:T(8,128)(2,1)S(1)}, bf16[32,2048]{1,0:T(8,128)(2,1)S(1)}, u32[]{:S(2)}, u32[]{:S(2)}) collective-permute-start(bf16[32,2048]{1,0:T(8,128)(2,1)S(1)} %get-tuple-element.48), channel_id=1, source_target_pairs={{0,1},{1,0},{2,3},{3,2},{4,5},{5,4},{6,7},{7,6},{8,9},{9,8},{10,11... | collective-permute-start | bytes 393224 | tf_op jit(solution)/shard_map/ppermute | solution.py:453
  2.7 3.1 %collective-permute-start.1 = (bf16[32,2048]{1,0:T(8,128)(2,1)S(1)}, bf16[32,2048]{1,0:T(8,128)(2,1)S(1)}, u32[]{:S(2)}, u32[]{:S(2)}) collective-permute-start(bf16[32,2048]{1,0:T(8,128)(2,1)S(1)} %get-tuple-element.49), channel_id=1, source_target_pairs={{1,2},{3,4},{5,6},{2,1},{4,3},{6,5},{9,10},{11,12},{13,14},{10,9},... | collective-permute-start | bytes 393224 | tf_op jit(solution)/shard_map/ppermute | solution.py:452
  5.8 0.0 copy-done
  5.8 0.3 shard_map.68
  6.2 2.3 %collective-permute-start.3 = (bf16[480,128]{1,0:T(8,128)(2,1)S(1)}, bf16[480,128]{1,0:T(8,128)(2,1)S(1)}, u32[]{:S(2)}, u32[]{:S(2)}) collective-permute-start(bf16[480,128]{1,0:T(8,128)(2,1)S(1)} %get-tuple-element.71), channel_id=1, source_target_pairs={{0,8},{8,24},{24,16},{16,0},{1,9},{9,25},{25,17},{17,1},{2,10},{10... | collective-permute-start | bytes 368648 | tf_op jit(solution)/shard_map/ppermute | solution.py:469
  8.5 0.0 collective-permute-done.swap_ref
  8.5 0.8 %collective-permute-done.1.cross_ref = bf16[32,2048]{1,0:T(8,128)(2,1)S(1)} collective-permute-done((bf16[32,2048]{1,0:T(8,128)(2,1)S(1)}, bf16[32,2048]{1,0:T(8,128)(2,1)S(1)}, u32[]{:S(2)}, u32[]{:S(2)}) %collective-permute-start.1) | collective-permute-done | bytes 131104 | tf_op jit(solution)/shard_map/ppermute | solution.py:452
  9.3 1.5 %collective-permute-start.2 = (bf16[320,128]{1,0:T(8,128)(2,1)S(1)}, bf16[320,128]{1,0:T(8,128)(2,1)S(1)}, u32[]{:S(2)}, u32[]{:S(2)}) collective-permute-start(bf16[320,128]{1,0:T(8,128)(2,1)S(1)} %get-tuple-element.64.rim_ref), channel_id=1, source_target_pairs={{0,8},{8,24},{24,16},{16,0},{1,9},{9,25},{25,17},{17,1},{2,10},{10... | collective-permute-start | bytes 245768 | tf_op jit(solution)/shard_map/ppermute | solution.py:469
  10.7 0.1 shard_map.74
  10.9 1.8 %collective-permute-start.4 = (bf16[1056,128]{1,0:T(8,128)(2,1)S(1)}, bf16[1056,128]{1,0:T(8,128)(2,1)S(1)}, u32[]{:S(2)}, u32[]{:S(2)}) collective-permute-start(bf16[1056,128]{1,0:T(8,128)(2,1)S(1)} %shard_map.74), channel_id=1, source_target_pairs={{16,24},{17,25},{18,26},{19,27},{20,28},{21,29},{22,30},{23,31}} | collective-permute-start | bytes 811016 | tf_op jit(solution)/shard_map/ppermute | solution.py:469
  12.7 0.7 %shard_map.71 = (f32[13,72,128]{2,1,0:T(8,128)S(1)}, f32[12,72,128]{2,1,0:T(8,128)S(1)}, f32[13,72,128]{2,1,0:T(8,128)S(1)}, f32[14,72,128]{2,1,0:T(8,128)S(1)}, f32[2,320,128]{2,1,0:T(8,128)S(1)}) custom-call(bf16[64,2048]{1,0:T(8,128)(2,1)S(1)} %get-tuple-element.53.act_ref, bf16[32,2048]{1,0:T(8,128)(2,1)S(1)} %collective-permute-done.swap_ref, ...), custom_call_target="tpu_custom_call" | custom-call | flops 1000 | bytes 1000 | tf_op jit(solution)/shard_map/pallas_call | solution.py:362
  13.3 0.0 collective-permute-done.3.in_ref
  13.4 0.0 collective-permute-done.2.rim_ref
  13.4 1.3 %collective-permute-start.5 = (bf16[416,128]{1,0:T(8,128)(2,1)S(1)}, bf16[416,128]{1,0:T(8,128)(2,1)S(1)}, u32[]{:S(2)}, u32[]{:S(2)}) collective-permute-start(bf16[416,128]{1,0:T(8,128)(2,1)S(1)} %get-tuple-element.79), channel_id=1, source_target_pairs={{8,16},{9,17},{10,18},{11,19},{12,20},{13,21},{14,22},{15,23}} | collective-permute-start | bytes 319496 | tf_op jit(solution)/shard_map/ppermute | solution.py:469
  14.7 0.1 collective-permute-start.6
  14.8 5.0 %collective-permute-done.5.own_ref = bf16[416,128]{1,0:T(8,128)(2,1)S(1)} collective-permute-done((bf16[416,128]{1,0:T(8,128)(2,1)S(1)}, bf16[416,128]{1,0:T(8,128)(2,1)S(1)}, u32[]{:S(2)}, u32[]{:S(2)}) %collective-permute-start.5) | collective-permute-done | bytes 106528 | tf_op jit(solution)/shard_map/ppermute | solution.py:469
  19.8 0.0 collective-permute-done.4.ship_ref
  19.8 0.0 collective-permute-done.6.last_ref
  19.8 0.9 %shard_map.76 = (f32[320,128]{1,0:T(8,128)S(1)}, f32[320,128]{1,0:T(8,128)S(1)}, f32[9,64,128]{2,1,0:T(8,128)S(1)}) custom-call(f32[2,320,128]{2,1,0:T(8,128)S(1)} %get-tuple-element.78.pair0, f32[2,320,128]{2,1,0:T(8,128)S(1)} %get-tuple-element.84.pair1, bf16[416,128]{1,0:T(8,128)(2,1)S(1)} %collective-permute-done.5.own_ref, ...), custom_call_target="tpu_custom_call" | custom-call | flops 1000 | bytes 1000 | tf_op jit(solution)/shard_map/pallas_call | solution.py:362
  20.7 0.1 collective-permute-start.7
  20.8 1.4 %collective-permute-done.7 = f32[320,128]{1,0:T(8,128)S(1)} collective-permute-done((f32[320,128]{1,0:T(8,128)S(1)}, f32[320,128]{1,0:T(8,128)S(1)}, u32[]{:S(2)}, u32[]{:S(2)}) %collective-permute-start.7) | collective-permute-done | bytes 163872 | tf_op jit(solution)/shard_map/ppermute | solution.py:858
  22.2 4.5 %collective-permute-start.10 = (bf16[320,128]{1,0:T(8,128)(2,1)S(1)}, bf16[320,128]{1,0:T(8,128)(2,1)S(1)}, u32[]{:S(2)}, u32[]{:S(2)}) collective-permute-start(bf16[320,128]{1,0:T(8,128)(2,1)S(1)} %fusion), channel_id=1, source_target_pairs={{0,6},{1,7},{2,4},{3,5},{4,2},{5,3},{6,0},{7,1},{8,14},{9,15},{10,... | collective-permute-start | bytes 245768 | tf_op jit(solution)/shard_map/ppermute | solution.py:864
  26.7 0.0 collective-permute-start.9
  26.7 0.4 collective-permute-start.8
  27.0 2.2 %collective-permute-done.10 = bf16[320,128]{1,0:T(8,128)(2,1)S(1)} collective-permute-done((bf16[320,128]{1,0:T(8,128)(2,1)S(1)}, bf16[320,128]{1,0:T(8,128)(2,1)S(1)}, u32[]{:S(2)}, u32[]{:S(2)}) %collective-permute-start.10) | collective-permute-done | bytes 81952 | tf_op jit(solution)/shard_map/ppermute | solution.py:864
  29.2 4.9 %collective-permute-done.9 = bf16[320,128]{1,0:T(8,128)(2,1)S(1)} collective-permute-done((bf16[320,128]{1,0:T(8,128)(2,1)S(1)}, bf16[320,128]{1,0:T(8,128)(2,1)S(1)}, u32[]{:S(2)}, u32[]{:S(2)}) %collective-permute-start.9) | collective-permute-done | bytes 81952 | tf_op jit(solution)/shard_map/ppermute | solution.py:864
  34.2 0.0 collective-permute-done.8
  34.2 0.9 %collective-permute-start.11 = (f32[320,128]{1,0:T(8,128)S(1)}, f32[320,128]{1,0:T(8,128)S(1)}, u32[]{:S(2)}, u32[]{:S(2)}) collective-permute-start(f32[320,128]{1,0:T(8,128)S(1)} %add_add_fusion.mine_ref), channel_id=1, source_target_pairs={{0,1},{1,0},{2,3},{3,2},{4,5},{5,4},{6,7},{7,6},{8,9},{9,8},{10,11... | collective-permute-start | bytes 491528 | tf_op jit(solution)/shard_map/ppermute | solution.py:869
  35.1 0.7 %shard_map.77 = bf16[64,2048]{1,0:T(8,128)(2,1)} custom-call(f32[16,104,128]{2,1,0:T(8,128)S(1)} %get-tuple-element.63.bi_f, f32[12,72,128]{2,1,0:T(8,128)S(1)} %get-tuple-element.77.bi_o, f32[9,64,128]{2,1,0:T(8,128)S(1)} %get-tuple-element.88.bi_l), custom_call_target="tpu_custom_call" | custom-call | flops 1000 | bytes 1000 | tf_op jit(solution)/shard_map/pallas_call | solution.py:362
  35.9 0.3 collective-permute-done.11.other_ref
  36.1 1.1 %shard_map.78 = (f32[2,576,64]{2,1,0:T(8,128)}, f32[2,64]{1,0:T(2,128)}) custom-call(f32[320,128]{1,0:T(8,128)S(1)} %add_add_fusion.mine_ref, f32[320,128]{1,0:T(8,128)S(1)} %collective-permute-done.11.other_ref), custom_call_target="tpu_custom_call" | custom-call | flops 1000 | bytes 1000 | tf_op jit(solution)/shard_map/pallas_call | solution.py:362
  (7 shorter events, 0.1 us)
Async XLA Ops:
  0.6 5.2 %copy-start = (bf16[1,2,3,3,64,64]{5,4,3,2,1,0:T(8,128)(2,1)S(1)}, bf16[1,2,3,3,64,64]{5,4,3,2,1,0:T(8,128)(2,1)}, u32[]{:S(2)}) copy-start(bf16[1,2,3,3,64,64]{5,4,3,2,1,0:T(8,128)(2,1)} %param.6) | copy-start | bytes 442372
  2.0 6.5 %collective-permute-start = (bf16[32,2048]{1,0:T(8,128)(2,1)S(1)}, bf16[32,2048]{1,0:T(8,128)(2,1)S(1)}, u32[]{:S(2)}, u32[]{:S(2)}) collective-permute-start(bf16[32,2048]{1,0:T(8,128)(2,1)S(1)} %get-tuple-element.48), channel_id=1, source_target_pairs={{0,1},{1,0},{2,3},{3,2},{4,5},{5,4},{6,7},{7,6},{8,9},{9,8},{10,11... | collective-permute-start | bytes 393224 | tf_op jit(solution)/shard_map/ppermute | solution.py:453
  2.7 6.6 %collective-permute-start.1 = (bf16[32,2048]{1,0:T(8,128)(2,1)S(1)}, bf16[32,2048]{1,0:T(8,128)(2,1)S(1)}, u32[]{:S(2)}, u32[]{:S(2)}) collective-permute-start(bf16[32,2048]{1,0:T(8,128)(2,1)S(1)} %get-tuple-element.49), channel_id=1, source_target_pairs={{1,2},{3,4},{5,6},{2,1},{4,3},{6,5},{9,10},{11,12},{13,14},{10,9},... | collective-permute-start | bytes 393224 | tf_op jit(solution)/shard_map/ppermute | solution.py:452
  6.2 7.2 %collective-permute-start.3 = (bf16[480,128]{1,0:T(8,128)(2,1)S(1)}, bf16[480,128]{1,0:T(8,128)(2,1)S(1)}, u32[]{:S(2)}, u32[]{:S(2)}) collective-permute-start(bf16[480,128]{1,0:T(8,128)(2,1)S(1)} %get-tuple-element.71), channel_id=1, source_target_pairs={{0,8},{8,24},{24,16},{16,0},{1,9},{9,25},{25,17},{17,1},{2,10},{10... | collective-permute-start | bytes 368648 | tf_op jit(solution)/shard_map/ppermute | solution.py:469
  9.3 4.1 %collective-permute-start.2 = (bf16[320,128]{1,0:T(8,128)(2,1)S(1)}, bf16[320,128]{1,0:T(8,128)(2,1)S(1)}, u32[]{:S(2)}, u32[]{:S(2)}) collective-permute-start(bf16[320,128]{1,0:T(8,128)(2,1)S(1)} %get-tuple-element.64.rim_ref), channel_id=1, source_target_pairs={{0,8},{8,24},{24,16},{16,0},{1,9},{9,25},{25,17},{17,1},{2,10},{10... | collective-permute-start | bytes 245768 | tf_op jit(solution)/shard_map/ppermute | solution.py:469
  10.9 8.9 %collective-permute-start.4 = (bf16[1056,128]{1,0:T(8,128)(2,1)S(1)}, bf16[1056,128]{1,0:T(8,128)(2,1)S(1)}, u32[]{:S(2)}, u32[]{:S(2)}) collective-permute-start(bf16[1056,128]{1,0:T(8,128)(2,1)S(1)} %shard_map.74), channel_id=1, source_target_pairs={{16,24},{17,25},{18,26},{19,27},{20,28},{21,29},{22,30},{23,31}} | collective-permute-start | bytes 811016 | tf_op jit(solution)/shard_map/ppermute | solution.py:469
  13.4 6.3 %collective-permute-start.5 = (bf16[416,128]{1,0:T(8,128)(2,1)S(1)}, bf16[416,128]{1,0:T(8,128)(2,1)S(1)}, u32[]{:S(2)}, u32[]{:S(2)}) collective-permute-start(bf16[416,128]{1,0:T(8,128)(2,1)S(1)} %get-tuple-element.79), channel_id=1, source_target_pairs={{8,16},{9,17},{10,18},{11,19},{12,20},{13,21},{14,22},{15,23}} | collective-permute-start | bytes 319496 | tf_op jit(solution)/shard_map/ppermute | solution.py:469
  14.7 5.1 %collective-permute-start.6 = (bf16[416,128]{1,0:T(8,128)(2,1)S(1)}, bf16[416,128]{1,0:T(8,128)(2,1)S(1)}, u32[]{:S(2)}, u32[]{:S(2)}) collective-permute-start(bf16[416,128]{1,0:T(8,128)(2,1)S(1)} %get-tuple-element.79), channel_id=1, source_target_pairs={{8,24},{24,16},{16,0},{0,8},{9,25},{25,17},{17,1},{1,9},{10,26},{2... | collective-permute-start | bytes 319496 | tf_op jit(solution)/shard_map/ppermute | solution.py:469
  20.7 1.5 %collective-permute-start.7 = (f32[320,128]{1,0:T(8,128)S(1)}, f32[320,128]{1,0:T(8,128)S(1)}, u32[]{:S(2)}, u32[]{:S(2)}) collective-permute-start(f32[320,128]{1,0:T(8,128)S(1)} %get-tuple-element.90), channel_id=1, source_target_pairs={{0,1},{1,0},{2,3},{3,2},{4,5},{5,4},{6,7},{7,6},{8,9},{9,8},{10,11... | collective-permute-start | bytes 491528 | tf_op jit(solution)/shard_map/ppermute | solution.py:858
  22.2 7.0 %collective-permute-start.10 = (bf16[320,128]{1,0:T(8,128)(2,1)S(1)}, bf16[320,128]{1,0:T(8,128)(2,1)S(1)}, u32[]{:S(2)}, u32[]{:S(2)}) collective-permute-start(bf16[320,128]{1,0:T(8,128)(2,1)S(1)} %fusion), channel_id=1, source_target_pairs={{0,6},{1,7},{2,4},{3,5},{4,2},{5,3},{6,0},{7,1},{8,14},{9,15},{10,... | collective-permute-start | bytes 245768 | tf_op jit(solution)/shard_map/ppermute | solution.py:864
  26.7 7.5 %collective-permute-start.9 = (bf16[320,128]{1,0:T(8,128)(2,1)S(1)}, bf16[320,128]{1,0:T(8,128)(2,1)S(1)}, u32[]{:S(2)}, u32[]{:S(2)}) collective-permute-start(bf16[320,128]{1,0:T(8,128)(2,1)S(1)} %fusion), channel_id=1, source_target_pairs={{0,4},{1,5},{2,6},{3,7},{4,0},{5,1},{6,2},{7,3},{8,12},{9,13},{10,... | collective-permute-start | bytes 245768 | tf_op jit(solution)/shard_map/ppermute | solution.py:864
  26.7 7.5 %collective-permute-start.8 = (bf16[320,128]{1,0:T(8,128)(2,1)S(1)}, bf16[320,128]{1,0:T(8,128)(2,1)S(1)}, u32[]{:S(2)}, u32[]{:S(2)}) collective-permute-start(bf16[320,128]{1,0:T(8,128)(2,1)S(1)} %fusion), channel_id=1, source_target_pairs={{0,2},{1,3},{2,0},{3,1},{4,6},{5,7},{6,4},{7,5},{8,10},{9,11},{10,... | collective-permute-start | bytes 245768 | tf_op jit(solution)/shard_map/ppermute | solution.py:864
  34.2 1.9 %collective-permute-start.11 = (f32[320,128]{1,0:T(8,128)S(1)}, f32[320,128]{1,0:T(8,128)S(1)}, u32[]{:S(2)}, u32[]{:S(2)}) collective-permute-start(f32[320,128]{1,0:T(8,128)S(1)} %add_add_fusion.mine_ref), channel_id=1, source_target_pairs={{0,1},{1,0},{2,3},{3,2},{4,5},{5,4},{6,7},{7,6},{8,9},{9,8},{10,11... | collective-permute-start | bytes 491528 | tf_op jit(solution)/shard_map/ppermute | solution.py:869

commit v6 on v5

--- a/solution.py
+++ b/solution.py
@@ -38,7 +38,7 @@
         self.in_rows = up_to(self.rows + 2 * (error - 1) + 2, 8) - 2
         self.back_rows = up_to(self.rows + 2 * (error - 2) + 2, 8) - 2
         self.own_rows = up_to(self.rows, 16)
-        self.alloc = up_to(max(self.hidden_rows + 2, self.x_margin + self.own_rows + 2), 8)
+        self.alloc = up_to(max(self.hidden_rows + 2, self.x_margin + self.own_rows + 2), 8) + 8
 
 
 def levels_of(rows, cols, count):
@@ -420,8 +420,8 @@
             at = slice(p * LANES, (p + 1) * LANES)
             act_ref[:, at] = act_hbm[:, at]
             cot_ref[:, at] = cot_hbm[:, at]
-            xs[p, :, :] = act_hbm[:, at].astype(F32)
-            cs[p, :, :] = cot_hbm[:, at].astype(F32)
+            xs[p, 0:row_count, :] = act_hbm[:, at].astype(F32)
+            cs[p, 0:row_count, :] = cot_hbm[:, at].astype(F32)
             ts[0, p, 0:x_margin, :] = xs[p, 0:x_margin, :]
             ts[0, p, x_margin : x_margin + g_margin, :] = cs[p, 0:g_margin, :]
             ts[1, p, 0:x_margin, :] = xs[p, pl.ds(live - x_margin, x_margin), :]
@@ -440,9 +440,9 @@
             strip_shape, strip_shape, sds((8, LANES), F32), halo_shape, halo_shape,
         ],
         [
-            pltpu.VMEM((pair_count, row_count, LANES), F32),
-            pltpu.VMEM((pair_count, row_count, LANES), F32),
-            pltpu.VMEM((2, pair_count, payload, LANES), F32),
+            pltpu.VMEM((pair_count, row_count + 16, LANES), F32),
+            pltpu.VMEM((pair_count, row_count + 16, LANES), F32),
+            pltpu.VMEM((2, pair_count, payload + 16, LANES), F32),
         ],
         [activations[0, 0], cotangent[0], biases[0]],
         outside=(0, 1, 2),
@@ -580,7 +580,7 @@
             )
             rim_ref[...] = flat[0:rim_rows, :].astype(BF16)
 
-    tmp_buffer = pltpu.VMEM((2, payload, LANES), F32)
+    tmp_buffer = pltpu.VMEM((2, payload + 16, LANES), F32)
     rim, *state = call(
         rim_body,
         [sds((rim_rows, LANES), BF16), *state_shapes],
@@ -618,12 +618,12 @@
                 bias_tmp[2 * term : 2 * term + 2, :] = part
                 rest = rest - part
             bias_tmp[6:16, :] = jnp.zeros((10, LANES), F32)
-            ship_ref[own_flat + packed_rows : ship_rows, :] = bias_tmp[...].astype(BF16)
+            ship_ref[own_flat + packed_rows : ship_rows, :] = bias_tmp[0:16, :].astype(BF16)
 
     (ship,) = call(
         ship_body,
         [sds((ship_rows, LANES), BF16)],
-        [tmp_buffer, pltpu.VMEM((own_flat + 32, LANES), F32), pltpu.VMEM((16, LANES), F32)],
+        [tmp_buffer, pltpu.VMEM((own_flat + 32, LANES), F32), pltpu.VMEM((32, LANES), F32)],
         [act, from_swap, from_cross, taps, bias_own, rim],
     )
     shipped = across(ship, [(2, 3)])
@@ -806,7 +806,7 @@
         odd = is_odd()
 
         def take(source):
-            flat[...] = source[...].astype(F32)
+            flat[0:third_flat, :] = source[...].astype(F32)
             for p in range(third.pairs):
                 gb[p, 0:third_rows, :] = flat[p * third_rows : (p + 1) * third_rows, :]
 
@@ -847,7 +847,7 @@
             buffer(third, 1),
             buffer(fine, 0),
             coarse_tmp,
-            pltpu.VMEM((third_flat, LANES), F32),
+            pltpu.VMEM((third_flat + 16, LANES), F32),
         ],
         [
             pair_first, pair_second, third_to_own, third_to_last, din_own, dout_own, hid_own, x_own, back_own,
@@ -882,6 +882,7 @@
     def final_body(mine_ref, other_ref, kernel_ref, bias_ref):
         odd = is_odd()
         half = channels
+        bias_rows = []
         for c in range(2):
             if c == 0:
                 value = jnp.where(odd, other_ref[...], mine_ref[...])
@@ -893,7 +894,8 @@
             kernel_ref[c, 128:192, :] = pair[:half]
             kernel_ref[c, 320:384, :] = pair[half:]
             kernel_ref[c, 512:576, :] = value[4 * half : 5 * half].T[:half]
-            bias_ref[c : c + 1, :] = half_swap(value[4 * half : 4 * half + 1])[:, :half]
+            bias_rows.append(half_swap(value[4 * half : 4 * half + 1])[:, :half])
+        bias_ref[...] = jnp.concatenate(bias_rows, axis=0)
 
     kernel_sum, bias_sum = call(
         final_body,

time: 37.4 us -> 37.4 us (level)
  no operation moved by 1% of the time
where the time goes in v6:
time: 37.4 us; the launch traced here: 37.2 us
  starting transfers between devices  16.5 us (44%)
  waiting for transfers between devices  14.6 us (39%)
  Pallas kernels  5.26 us (14%)
  between operations  0.78 us (2%)
    ppermute x3, waiting for transfers between devices, local(): lax.ppermute(small, 'strip', [(i, i ^ o) for i in range(strips)])  7.1 us
    ppermute x5, starting transfers between devices, across(): return lax.ppermute(value, 'section', pairs)  6.89 us
    pallas_call x12, Pallas kernels, call(): pl.pallas_call(body, out_shape=out_shape, in_specs=[pl.BlockSpec(memory_s...  5.26 us
    ppermute x5, waiting for transfers between devices, across(): return lax.ppermute(value, 'section', pairs)  4.99 us
    ppermute x3, starting transfers between devices, local(): lax.ppermute(small, 'strip', [(i, i ^ o) for i in range(strips)])  4.83 us
    ppermute x1, starting transfers between devices, local(): from_cross = lax.ppermute(to_cross, 'strip', cross_pairs)  3.1 us
    ppermute x1, waiting for transfers between devices, local(): total = keep + lax.ppermute(send, 'strip', swap_pairs)  1.38 us
    ppermute x1, starting transfers between devices, local(): other = lax.ppermute(total, 'strip', swap_pairs)  0.9 us
  transfers between devices with their start and end apart: 12, of which 6 were waited for; matrix products, arithmetic and copies ran while one was open for 0% of the time, Pallas kernels for 5%

profile of v6, /device:TPU:5, one launch (start us, length us, event | category | flops | bytes accessed | tf_op | source)
XLA Modules:
  0.0 37.2 jit_solution(3122107844940076638)
XLA Ops:
  0.6 0.0 copy-start
  0.6 1.3 %shard_map.67 = (bf16[64,2048]{1,0:T(8,128)(2,1)S(1)}, bf16[64,2048]{1,0:T(8,128)(2,1)S(1)}, f32[8,128]{1,0:T(8,128)S(1)}, bf16[32,2048]{1,0:T(8,128)(2,1)S(1)}, bf16[32,2048]{1,0:T(8,128)(2,1)S(1)}) custom-call(bf16[64,2048]{1,0:T(8,128)(2,1)} %bitcast.10, bf16[64,2048]{1,0:T(8,128)(2,1)} %bitcast.11, f32[2,64]{1,0:T(2,128)} %bitcast.12), custom_call_target="tpu_custom_call" | custom-call | flops 1000 | bytes 1000 | tf_op jit(solution)/shard_map/pallas_call | solution.py:362
  2.0 0.7 %collective-permute-start = (bf16[32,2048]{1,0:T(8,128)(2,1)S(1)}, bf16[32,2048]{1,0:T(8,128)(2,1)S(1)}, u32[]{:S(2)}, u32[]{:S(2)}) collective-permute-start(bf16[32,2048]{1,0:T(8,128)(2,1)S(1)} %get-tuple-element.48), channel_id=1, source_target_pairs={{0,1},{1,0},{2,3},{3,2},{4,5},{5,4},{6,7},{7,6},{8,9},{9,8},{10,11... | collective-permute-start | bytes 393224 | tf_op jit(solution)/shard_map/ppermute | solution.py:453
  2.7 3.1 %collective-permute-start.1 = (bf16[32,2048]{1,0:T(8,128)(2,1)S(1)}, bf16[32,2048]{1,0:T(8,128)(2,1)S(1)}, u32[]{:S(2)}, u32[]{:S(2)}) collective-permute-start(bf16[32,2048]{1,0:T(8,128)(2,1)S(1)} %get-tuple-element.49), channel_id=1, source_target_pairs={{1,2},{3,4},{5,6},{2,1},{4,3},{6,5},{9,10},{11,12},{13,14},{10,9},... | collective-permute-start | bytes 393224 | tf_op jit(solution)/shard_map/ppermute | solution.py:452
  5.8 0.0 copy-done
  5.8 0.3 shard_map.68
  6.2 2.3 %collective-permute-start.3 = (bf16[480,128]{1,0:T(8,128)(2,1)S(1)}, bf16[480,128]{1,0:T(8,128)(2,1)S(1)}, u32[]{:S(2)}, u32[]{:S(2)}) collective-permute-start(bf16[480,128]{1,0:T(8,128)(2,1)S(1)} %get-tuple-element.71), channel_id=1, source_target_pairs={{0,8},{8,24},{24,16},{16,0},{1,9},{9,25},{25,17},{17,1},{2,10},{10... | collective-permute-start | bytes 368648 | tf_op jit(solution)/shard_map/ppermute | solution.py:469
  8.5 0.0 collective-permute-done.swap_ref
  8.5 0.8 %collective-permute-done.1.cross_ref = bf16[32,2048]{1,0:T(8,128)(2,1)S(1)} collective-permute-done((bf16[32,2048]{1,0:T(8,128)(2,1)S(1)}, bf16[32,2048]{1,0:T(8,128)(2,1)S(1)}, u32[]{:S(2)}, u32[]{:S(2)}) %collective-permute-start.1) | collective-permute-done | bytes 131104 | tf_op jit(solution)/shard_map/ppermute | solution.py:452
  9.3 1.5 %collective-permute-start.2 = (bf16[320,128]{1,0:T(8,128)(2,1)S(1)}, bf16[320,128]{1,0:T(8,128)(2,1)S(1)}, u32[]{:S(2)}, u32[]{:S(2)}) collective-permute-start(bf16[320,128]{1,0:T(8,128)(2,1)S(1)} %get-tuple-element.64.rim_ref), channel_id=1, source_target_pairs={{0,8},{8,24},{24,16},{16,0},{1,9},{9,25},{25,17},{17,1},{2,10},{10... | collective-permute-start | bytes 245768 | tf_op jit(solution)/shard_map/ppermute | solution.py:469
  10.7 0.1 shard_map.74
  10.9 1.8 %collective-permute-start.4 = (bf16[1056,128]{1,0:T(8,128)(2,1)S(1)}, bf16[1056,128]{1,0:T(8,128)(2,1)S(1)}, u32[]{:S(2)}, u32[]{:S(2)}) collective-permute-start(bf16[1056,128]{1,0:T(8,128)(2,1)S(1)} %shard_map.74), channel_id=1, source_target_pairs={{16,24},{17,25},{18,26},{19,27},{20,28},{21,29},{22,30},{23,31}} | collective-permute-start | bytes 811016 | tf_op jit(solution)/shard_map/ppermute | solution.py:469
  12.7 0.7 %shard_map.71 = (f32[13,80,128]{2,1,0:T(8,128)S(1)}, f32[12,80,128]{2,1,0:T(8,128)S(1)}, f32[13,80,128]{2,1,0:T(8,128)S(1)}, f32[14,80,128]{2,1,0:T(8,128)S(1)}, f32[2,320,128]{2,1,0:T(8,128)S(1)}) custom-call(bf16[64,2048]{1,0:T(8,128)(2,1)S(1)} %get-tuple-element.53.act_ref, bf16[32,2048]{1,0:T(8,128)(2,1)S(1)} %collective-permute-done.swap_ref, ...), custom_call_target="tpu_custom_call" | custom-call | flops 1000 | bytes 1000 | tf_op jit(solution)/shard_map/pallas_call | solution.py:362
  13.4 0.0 collective-permute-done.3.in_ref
  13.4 0.0 collective-permute-done.2.rim_ref
  13.4 1.3 %collective-permute-start.5 = (bf16[416,128]{1,0:T(8,128)(2,1)S(1)}, bf16[416,128]{1,0:T(8,128)(2,1)S(1)}, u32[]{:S(2)}, u32[]{:S(2)}) collective-permute-start(bf16[416,128]{1,0:T(8,128)(2,1)S(1)} %get-tuple-element.79), channel_id=1, source_target_pairs={{8,16},{9,17},{10,18},{11,19},{12,20},{13,21},{14,22},{15,23}} | collective-permute-start | bytes 319496 | tf_op jit(solution)/shard_map/ppermute | solution.py:469
  14.7 0.1 collective-permute-start.6
  14.8 5.0 %collective-permute-done.5.own_ref = bf16[416,128]{1,0:T(8,128)(2,1)S(1)} collective-permute-done((bf16[416,128]{1,0:T(8,128)(2,1)S(1)}, bf16[416,128]{1,0:T(8,128)(2,1)S(1)}, u32[]{:S(2)}, u32[]{:S(2)}) %collective-permute-start.5) | collective-permute-done | bytes 106528 | tf_op jit(solution)/shard_map/ppermute | solution.py:469
  19.8 0.0 collective-permute-done.4.ship_ref
  19.8 0.0 collective-permute-done.6.last_ref
  19.8 0.9 %shard_map.76 = (f32[320,128]{1,0:T(8,128)S(1)}, f32[320,128]{1,0:T(8,128)S(1)}, f32[9,72,128]{2,1,0:T(8,128)S(1)}) custom-call(f32[2,320,128]{2,1,0:T(8,128)S(1)} %get-tuple-element.78.pair0, f32[2,320,128]{2,1,0:T(8,128)S(1)} %get-tuple-element.84.pair1, bf16[416,128]{1,0:T(8,128)(2,1)S(1)} %collective-permute-done.5.own_ref, ...), custom_call_target="tpu_custom_call" | custom-call | flops 1000 | bytes 1000 | tf_op jit(solution)/shard_map/pallas_call | solution.py:362
  20.7 0.1 collective-permute-start.7
  20.8 1.4 %collective-permute-done.7 = f32[320,128]{1,0:T(8,128)S(1)} collective-permute-done((f32[320,128]{1,0:T(8,128)S(1)}, f32[320,128]{1,0:T(8,128)S(1)}, u32[]{:S(2)}, u32[]{:S(2)}) %collective-permute-start.7) | collective-permute-done | bytes 163872 | tf_op jit(solution)/shard_map/ppermute | solution.py:858
  22.2 4.5 %collective-permute-start.10 = (bf16[320,128]{1,0:T(8,128)(2,1)S(1)}, bf16[320,128]{1,0:T(8,128)(2,1)S(1)}, u32[]{:S(2)}, u32[]{:S(2)}) collective-permute-start(bf16[320,128]{1,0:T(8,128)(2,1)S(1)} %fusion), channel_id=1, source_target_pairs={{0,6},{1,7},{2,4},{3,5},{4,2},{5,3},{6,0},{7,1},{8,14},{9,15},{10,... | collective-permute-start | bytes 245768 | tf_op jit(solution)/shard_map/ppermute | solution.py:864
  26.7 0.0 collective-permute-start.9
  26.7 0.4 collective-permute-start.8
  27.1 2.2 %collective-permute-done.10 = bf16[320,128]{1,0:T(8,128)(2,1)S(1)} collective-permute-done((bf16[320,128]{1,0:T(8,128)(2,1)S(1)}, bf16[320,128]{1,0:T(8,128)(2,1)S(1)}, u32[]{:S(2)}, u32[]{:S(2)}) %collective-permute-start.10) | collective-permute-done | bytes 81952 | tf_op jit(solution)/shard_map/ppermute | solution.py:864
  29.3 4.9 %collective-permute-done.9 = bf16[320,128]{1,0:T(8,128)(2,1)S(1)} collective-permute-done((bf16[320,128]{1,0:T(8,128)(2,1)S(1)}, bf16[320,128]{1,0:T(8,128)(2,1)S(1)}, u32[]{:S(2)}, u32[]{:S(2)}) %collective-permute-start.9) | collective-permute-done | bytes 81952 | tf_op jit(solution)/shard_map/ppermute | solution.py:864
  34.2 0.0 collective-permute-done.8
  34.2 0.1 add_add_fusion.mine_ref
  34.2 0.9 %collective-permute-start.11 = (f32[320,128]{1,0:T(8,128)S(1)}, f32[320,128]{1,0:T(8,128)S(1)}, u32[]{:S(2)}, u32[]{:S(2)}) collective-permute-start(f32[320,128]{1,0:T(8,128)S(1)} %add_add_fusion.mine_ref), channel_id=1, source_target_pairs={{0,1},{1,0},{2,3},{3,2},{4,5},{5,4},{6,7},{7,6},{8,9},{9,8},{10,11... | collective-permute-start | bytes 491528 | tf_op jit(solution)/shard_map/ppermute | solution.py:869
  35.1 0.7 %shard_map.77 = bf16[64,2048]{1,0:T(8,128)(2,1)} custom-call(f32[16,112,128]{2,1,0:T(8,128)S(1)} %get-tuple-element.63.bi_f, f32[12,80,128]{2,1,0:T(8,128)S(1)} %get-tuple-element.77.bi_o, f32[9,72,128]{2,1,0:T(8,128)S(1)} %get-tuple-element.88.bi_l), custom_call_target="tpu_custom_call" | custom-call | flops 1000 | bytes 1000 | tf_op jit(solution)/shard_map/pallas_call | solution.py:362
  35.9 0.3 collective-permute-done.11.other_ref
  36.1 1.1 %shard_map.78 = (f32[2,576,64]{2,1,0:T(8,128)}, f32[2,64]{1,0:T(2,128)}) custom-call(f32[320,128]{1,0:T(8,128)S(1)} %add_add_fusion.mine_ref, f32[320,128]{1,0:T(8,128)S(1)} %collective-permute-done.11.other_ref), custom_call_target="tpu_custom_call" | custom-call | flops 1000 | bytes 1000 | tf_op jit(solution)/shard_map/pallas_call | solution.py:362
  (6 shorter events, 0.1 us)
Async XLA Ops:
  0.6 5.2 %copy-start = (bf16[1,2,3,3,64,64]{5,4,3,2,1,0:T(8,128)(2,1)S(1)}, bf16[1,2,3,3,64,64]{5,4,3,2,1,0:T(8,128)(2,1)}, u32[]{:S(2)}) copy-start(bf16[1,2,3,3,64,64]{5,4,3,2,1,0:T(8,128)(2,1)} %param.6) | copy-start | bytes 442372
  2.0 6.5 %collective-permute-start = (bf16[32,2048]{1,0:T(8,128)(2,1)S(1)}, bf16[32,2048]{1,0:T(8,128)(2,1)S(1)}, u32[]{:S(2)}, u32[]{:S(2)}) collective-permute-start(bf16[32,2048]{1,0:T(8,128)(2,1)S(1)} %get-tuple-element.48), channel_id=1, source_target_pairs={{0,1},{1,0},{2,3},{3,2},{4,5},{5,4},{6,7},{7,6},{8,9},{9,8},{10,11... | collective-permute-start | bytes 393224 | tf_op jit(solution)/shard_map/ppermute | solution.py:453
  2.7 6.6 %collective-permute-start.1 = (bf16[32,2048]{1,0:T(8,128)(2,1)S(1)}, bf16[32,2048]{1,0:T(8,128)(2,1)S(1)}, u32[]{:S(2)}, u32[]{:S(2)}) collective-permute-start(bf16[32,2048]{1,0:T(8,128)(2,1)S(1)} %get-tuple-element.49), channel_id=1, source_target_pairs={{1,2},{3,4},{5,6},{2,1},{4,3},{6,5},{9,10},{11,12},{13,14},{10,9},... | collective-permute-start | bytes 393224 | tf_op jit(solution)/shard_map/ppermute | solution.py:452
  6.2 7.2 %collective-permute-start.3 = (bf16[480,128]{1,0:T(8,128)(2,1)S(1)}, bf16[480,128]{1,0:T(8,128)(2,1)S(1)}, u32[]{:S(2)}, u32[]{:S(2)}) collective-permute-start(bf16[480,128]{1,0:T(8,128)(2,1)S(1)} %get-tuple-element.71), channel_id=1, source_target_pairs={{0,8},{8,24},{24,16},{16,0},{1,9},{9,25},{25,17},{17,1},{2,10},{10... | collective-permute-start | bytes 368648 | tf_op jit(solution)/shard_map/ppermute | solution.py:469
  9.3 4.1 %collective-permute-start.2 = (bf16[320,128]{1,0:T(8,128)(2,1)S(1)}, bf16[320,128]{1,0:T(8,128)(2,1)S(1)}, u32[]{:S(2)}, u32[]{:S(2)}) collective-permute-start(bf16[320,128]{1,0:T(8,128)(2,1)S(1)} %get-tuple-element.64.rim_ref), channel_id=1, source_target_pairs={{0,8},{8,24},{24,16},{16,0},{1,9},{9,25},{25,17},{17,1},{2,10},{10... | collective-permute-start | bytes 245768 | tf_op jit(solution)/shard_map/ppermute | solution.py:469
  10.9 8.9 %collective-permute-start.4 = (bf16[1056,128]{1,0:T(8,128)(2,1)S(1)}, bf16[1056,128]{1,0:T(8,128)(2,1)S(1)}, u32[]{:S(2)}, u32[]{:S(2)}) collective-permute-start(bf16[1056,128]{1,0:T(8,128)(2,1)S(1)} %shard_map.74), channel_id=1, source_target_pairs={{16,24},{17,25},{18,26},{19,27},{20,28},{21,29},{22,30},{23,31}} | collective-permute-start | bytes 811016 | tf_op jit(solution)/shard_map/ppermute | solution.py:469
  13.4 6.3 %collective-permute-start.5 = (bf16[416,128]{1,0:T(8,128)(2,1)S(1)}, bf16[416,128]{1,0:T(8,128)(2,1)S(1)}, u32[]{:S(2)}, u32[]{:S(2)}) collective-permute-start(bf16[416,128]{1,0:T(8,128)(2,1)S(1)} %get-tuple-element.79), channel_id=1, source_target_pairs={{8,16},{9,17},{10,18},{11,19},{12,20},{13,21},{14,22},{15,23}} | collective-permute-start | bytes 319496 | tf_op jit(solution)/shard_map/ppermute | solution.py:469
  14.7 5.1 %collective-permute-start.6 = (bf16[416,128]{1,0:T(8,128)(2,1)S(1)}, bf16[416,128]{1,0:T(8,128)(2,1)S(1)}, u32[]{:S(2)}, u32[]{:S(2)}) collective-permute-start(bf16[416,128]{1,0:T(8,128)(2,1)S(1)} %get-tuple-element.79), channel_id=1, source_target_pairs={{8,24},{24,16},{16,0},{0,8},{9,25},{25,17},{17,1},{1,9},{10,26},{2... | collective-permute-start | bytes 319496 | tf_op jit(solution)/shard_map/ppermute | solution.py:469
  20.7 1.5 %collective-permute-start.7 = (f32[320,128]{1,0:T(8,128)S(1)}, f32[320,128]{1,0:T(8,128)S(1)}, u32[]{:S(2)}, u32[]{:S(2)}) collective-permute-start(f32[320,128]{1,0:T(8,128)S(1)} %get-tuple-element.90), channel_id=1, source_target_pairs={{0,1},{1,0},{2,3},{3,2},{4,5},{5,4},{6,7},{7,6},{8,9},{9,8},{10,11... | collective-permute-start | bytes 491528 | tf_op jit(solution)/shard_map/ppermute | solution.py:858
  22.2 7.0 %collective-permute-start.10 = (bf16[320,128]{1,0:T(8,128)(2,1)S(1)}, bf16[320,128]{1,0:T(8,128)(2,1)S(1)}, u32[]{:S(2)}, u32[]{:S(2)}) collective-permute-start(bf16[320,128]{1,0:T(8,128)(2,1)S(1)} %fusion), channel_id=1, source_target_pairs={{0,6},{1,7},{2,4},{3,5},{4,2},{5,3},{6,0},{7,1},{8,14},{9,15},{10,... | collective-permute-start | bytes 245768 | tf_op jit(solution)/shard_map/ppermute | solution.py:864
  26.7 7.5 %collective-permute-start.9 = (bf16[320,128]{1,0:T(8,128)(2,1)S(1)}, bf16[320,128]{1,0:T(8,128)(2,1)S(1)}, u32[]{:S(2)}, u32[]{:S(2)}) collective-permute-start(bf16[320,128]{1,0:T(8,128)(2,1)S(1)} %fusion), channel_id=1, source_target_pairs={{0,4},{1,5},{2,6},{3,7},{4,0},{5,1},{6,2},{7,3},{8,12},{9,13},{10,... | collective-permute-start | bytes 245768 | tf_op jit(solution)/shard_map/ppermute | solution.py:864
  26.7 7.5 %collective-permute-start.8 = (bf16[320,128]{1,0:T(8,128)(2,1)S(1)}, bf16[320,128]{1,0:T(8,128)(2,1)S(1)}, u32[]{:S(2)}, u32[]{:S(2)}) collective-permute-start(bf16[320,128]{1,0:T(8,128)(2,1)S(1)} %fusion), channel_id=1, source_target_pairs={{0,2},{1,3},{2,0},{3,1},{4,6},{5,7},{6,4},{7,5},{8,10},{9,11},{10,... | collective-permute-start | bytes 245768 | tf_op jit(solution)/shard_map/ppermute | solution.py:864
  34.2 1.9 %collective-permute-start.11 = (f32[320,128]{1,0:T(8,128)S(1)}, f32[320,128]{1,0:T(8,128)S(1)}, u32[]{:S(2)}, u32[]{:S(2)}) collective-permute-start(f32[320,128]{1,0:T(8,128)S(1)} %add_add_fusion.mine_ref), channel_id=1, source_target_pairs={{0,1},{1,0},{2,3},{3,2},{4,5},{5,4},{6,7},{7,6},{8,9},{9,8},{10,11... | collective-permute-start | bytes 491528 | tf_op jit(solution)/shard_map/ppermute | solution.py:869

commit v7 on v6

--- a/solution.py
+++ b/solution.py
@@ -160,7 +160,9 @@
         thirds.append((then[:half] + moved) * scale)
     bias = (total + half_swap(total)) * scale
     out_ref[3 * half : 4 * half, :] = jnp.where(low, thirds[0], half_swap(thirds[1]))
-    out_ref[4 * half : 5 * half, :] = jnp.where(low, thirds[2], bias)
+    at = 4 * half + half // 2
+    out_ref[4 * half : at, :] = jnp.where(low, thirds[2][: half // 2], half_swap(thirds[2][half // 2 :]))
+    out_ref[at : at + 16, :] = jnp.broadcast_to(bias, (16, LANES))
 
 
 def toeplitz(taps):
@@ -628,7 +630,7 @@
     )
     shipped = across(ship, [(2, 3)])
 
-    grad_rows = 5 * channels
+    grad_rows = 4 * channels + half + 16
 
     def gradients(level, source, hidden, err_in, err_out, rows_at, pair_out):
         scale = np.float32(1.0 / math.sqrt(strips * level.rows * level.cols))
@@ -893,8 +895,10 @@
             pair = value[3 * half : 4 * half].T
             kernel_ref[c, 128:192, :] = pair[:half]
             kernel_ref[c, 320:384, :] = pair[half:]
-            kernel_ref[c, 512:576, :] = value[4 * half : 5 * half].T[:half]
-            bias_rows.append(half_swap(value[4 * half : 4 * half + 1])[:, :half])
+            at = 4 * half + half // 2
+            pair = value[4 * half : at].T
+            kernel_ref[c, 512:576, :] = jnp.concatenate([pair[:half], pair[half:]], axis=1)
+            bias_rows.append(value[at : at + 1, :half])
         bias_ref[...] = jnp.concatenate(bias_rows, axis=0)
 
     kernel_sum, bias_sum = call(

time: 37.4 us -> 37.1 us (level)
  waiting for transfers between devices: 14.6 us -> 14.2 us
where the time goes in v7:
time: 37.1 us; the launch traced here: 36.9 us
  starting transfers between devices  16.5 us (44%)
  waiting for transfers between devices  14.2 us (38%)
  Pallas kernels  5.35 us (14%)
  between operations  0.78 us (2%)
    ppermute x5, starting transfers between devices, across(): return lax.ppermute(value, 'section', pairs)  6.89 us
    ppermute x3, waiting for transfers between devices, local(): lax.ppermute(small, 'strip', [(i, i ^ o) for i in range(strips)])  6.77 us
    pallas_call x12, Pallas kernels, call(): pl.pallas_call(body, out_shape=out_shape, in_specs=[pl.BlockSpec(memory_s...  5.35 us
    ppermute x5, waiting for transfers between devices, across(): return lax.ppermute(value, 'section', pairs)  4.99 us
    ppermute x3, starting transfers between devices, local(): lax.ppermute(small, 'strip', [(i, i ^ o) for i in range(strips)])  4.82 us
    ppermute x1, starting transfers between devices, local(): from_cross = lax.ppermute(to_cross, 'strip', cross_pairs)  3.1 us
    ppermute x1, waiting for transfers between devices, local(): total = keep + lax.ppermute(send, 'strip', swap_pairs)  1.37 us
    ppermute x1, starting transfers between devices, local(): other = lax.ppermute(total, 'strip', swap_pairs)  0.89 us
  transfers between devices with their start and end apart: 12, of which 6 were waited for; matrix products, arithmetic and copies ran while one was open for 0% of the time, Pallas kernels for 5%

profile of v7, /device:TPU:5, one launch (start us, length us, event | category | flops | bytes accessed | tf_op | source)
XLA Modules:
  0.0 36.9 jit_solution(8867615982310650140)
XLA Ops:
  0.6 0.0 copy-start
  0.6 1.3 %shard_map.67 = (bf16[64,2048]{1,0:T(8,128)(2,1)S(1)}, bf16[64,2048]{1,0:T(8,128)(2,1)S(1)}, f32[8,128]{1,0:T(8,128)S(1)}, bf16[32,2048]{1,0:T(8,128)(2,1)S(1)}, bf16[32,2048]{1,0:T(8,128)(2,1)S(1)}) custom-call(bf16[64,2048]{1,0:T(8,128)(2,1)} %bitcast.10, bf16[64,2048]{1,0:T(8,128)(2,1)} %bitcast.11, f32[2,64]{1,0:T(2,128)} %bitcast.12), custom_call_target="tpu_custom_call" | custom-call | flops 1000 | bytes 1000 | tf_op jit(solution)/shard_map/pallas_call | solution.py:364
  2.0 0.7 %collective-permute-start = (bf16[32,2048]{1,0:T(8,128)(2,1)S(1)}, bf16[32,2048]{1,0:T(8,128)(2,1)S(1)}, u32[]{:S(2)}, u32[]{:S(2)}) collective-permute-start(bf16[32,2048]{1,0:T(8,128)(2,1)S(1)} %get-tuple-element.48), channel_id=1, source_target_pairs={{0,1},{1,0},{2,3},{3,2},{4,5},{5,4},{6,7},{7,6},{8,9},{9,8},{10,11... | collective-permute-start | bytes 393224 | tf_op jit(solution)/shard_map/ppermute | solution.py:455
  2.7 3.1 %collective-permute-start.1 = (bf16[32,2048]{1,0:T(8,128)(2,1)S(1)}, bf16[32,2048]{1,0:T(8,128)(2,1)S(1)}, u32[]{:S(2)}, u32[]{:S(2)}) collective-permute-start(bf16[32,2048]{1,0:T(8,128)(2,1)S(1)} %get-tuple-element.49), channel_id=1, source_target_pairs={{1,2},{3,4},{5,6},{2,1},{4,3},{6,5},{9,10},{11,12},{13,14},{10,9},... | collective-permute-start | bytes 393224 | tf_op jit(solution)/shard_map/ppermute | solution.py:454
  5.8 0.0 copy-done
  5.8 0.3 shard_map.68
  6.2 2.3 %collective-permute-start.3 = (bf16[480,128]{1,0:T(8,128)(2,1)S(1)}, bf16[480,128]{1,0:T(8,128)(2,1)S(1)}, u32[]{:S(2)}, u32[]{:S(2)}) collective-permute-start(bf16[480,128]{1,0:T(8,128)(2,1)S(1)} %get-tuple-element.71), channel_id=1, source_target_pairs={{0,8},{8,24},{24,16},{16,0},{1,9},{9,25},{25,17},{17,1},{2,10},{10... | collective-permute-start | bytes 368648 | tf_op jit(solution)/shard_map/ppermute | solution.py:471
  8.5 0.0 collective-permute-done.swap_ref
  8.5 0.8 %collective-permute-done.1.cross_ref = bf16[32,2048]{1,0:T(8,128)(2,1)S(1)} collective-permute-done((bf16[32,2048]{1,0:T(8,128)(2,1)S(1)}, bf16[32,2048]{1,0:T(8,128)(2,1)S(1)}, u32[]{:S(2)}, u32[]{:S(2)}) %collective-permute-start.1) | collective-permute-done | bytes 131104 | tf_op jit(solution)/shard_map/ppermute | solution.py:454
  9.3 1.5 %collective-permute-start.2 = (bf16[320,128]{1,0:T(8,128)(2,1)S(1)}, bf16[320,128]{1,0:T(8,128)(2,1)S(1)}, u32[]{:S(2)}, u32[]{:S(2)}) collective-permute-start(bf16[320,128]{1,0:T(8,128)(2,1)S(1)} %get-tuple-element.64.rim_ref), channel_id=1, source_target_pairs={{0,8},{8,24},{24,16},{16,0},{1,9},{9,25},{25,17},{17,1},{2,10},{10... | collective-permute-start | bytes 245768 | tf_op jit(solution)/shard_map/ppermute | solution.py:471
  10.7 0.1 shard_map.74
  10.9 1.8 %collective-permute-start.4 = (bf16[1056,128]{1,0:T(8,128)(2,1)S(1)}, bf16[1056,128]{1,0:T(8,128)(2,1)S(1)}, u32[]{:S(2)}, u32[]{:S(2)}) collective-permute-start(bf16[1056,128]{1,0:T(8,128)(2,1)S(1)} %shard_map.74), channel_id=1, source_target_pairs={{16,24},{17,25},{18,26},{19,27},{20,28},{21,29},{22,30},{23,31}} | collective-permute-start | bytes 811016 | tf_op jit(solution)/shard_map/ppermute | solution.py:471
  12.7 0.7 %shard_map.71 = (f32[13,80,128]{2,1,0:T(8,128)S(1)}, f32[12,80,128]{2,1,0:T(8,128)S(1)}, f32[13,80,128]{2,1,0:T(8,128)S(1)}, f32[14,80,128]{2,1,0:T(8,128)S(1)}, f32[2,304,128]{2,1,0:T(8,128)S(1)}) custom-call(bf16[64,2048]{1,0:T(8,128)(2,1)S(1)} %get-tuple-element.53.act_ref, bf16[32,2048]{1,0:T(8,128)(2,1)S(1)} %collective-permute-done.swap_ref, ...), custom_call_target="tpu_custom_call" | custom-call | flops 1000 | bytes 1000 | tf_op jit(solution)/shard_map/pallas_call | solution.py:364
  13.4 0.0 collective-permute-done.3.in_ref
  13.4 0.0 collective-permute-done.2.rim_ref
  13.4 1.3 %collective-permute-start.5 = (bf16[416,128]{1,0:T(8,128)(2,1)S(1)}, bf16[416,128]{1,0:T(8,128)(2,1)S(1)}, u32[]{:S(2)}, u32[]{:S(2)}) collective-permute-start(bf16[416,128]{1,0:T(8,128)(2,1)S(1)} %get-tuple-element.79), channel_id=1, source_target_pairs={{8,16},{9,17},{10,18},{11,19},{12,20},{13,21},{14,22},{15,23}} | collective-permute-start | bytes 319496 | tf_op jit(solution)/shard_map/ppermute | solution.py:471
  14.7 0.1 collective-permute-start.6
  14.8 5.0 %collective-permute-done.5.own_ref = bf16[416,128]{1,0:T(8,128)(2,1)S(1)} collective-permute-done((bf16[416,128]{1,0:T(8,128)(2,1)S(1)}, bf16[416,128]{1,0:T(8,128)(2,1)S(1)}, u32[]{:S(2)}, u32[]{:S(2)}) %collective-permute-start.5) | collective-permute-done | bytes 106528 | tf_op jit(solution)/shard_map/ppermute | solution.py:471
  19.8 0.0 collective-permute-done.4.ship_ref
  19.8 0.0 collective-permute-done.6.last_ref
  19.8 1.0 %shard_map.76 = (f32[304,128]{1,0:T(8,128)S(1)}, f32[304,128]{1,0:T(8,128)S(1)}, f32[9,72,128]{2,1,0:T(8,128)S(1)}) custom-call(f32[2,304,128]{2,1,0:T(8,128)S(1)} %get-tuple-element.78.pair0, f32[2,304,128]{2,1,0:T(8,128)S(1)} %get-tuple-element.84.pair1, bf16[416,128]{1,0:T(8,128)(2,1)S(1)} %collective-permute-done.5.own_ref, ...), custom_call_target="tpu_custom_call" | custom-call | flops 1000 | bytes 1000 | tf_op jit(solution)/shard_map/pallas_call | solution.py:364
  20.8 0.1 collective-permute-start.7
  20.9 1.4 %collective-permute-done.7 = f32[304,128]{1,0:T(8,128)S(1)} collective-permute-done((f32[304,128]{1,0:T(8,128)S(1)}, f32[304,128]{1,0:T(8,128)S(1)}, u32[]{:S(2)}, u32[]{:S(2)}) %collective-permute-start.7) | collective-permute-done | bytes 155680 | tf_op jit(solution)/shard_map/ppermute | solution.py:860
  22.3 4.5 %collective-permute-start.10 = (bf16[304,128]{1,0:T(8,128)(2,1)S(1)}, bf16[304,128]{1,0:T(8,128)(2,1)S(1)}, u32[]{:S(2)}, u32[]{:S(2)}) collective-permute-start(bf16[304,128]{1,0:T(8,128)(2,1)S(1)} %fusion), channel_id=1, source_target_pairs={{0,6},{1,7},{2,4},{3,5},{4,2},{5,3},{6,0},{7,1},{8,14},{9,15},{10,... | collective-permute-start | bytes 233480 | tf_op jit(solution)/shard_map/ppermute | solution.py:866
  26.7 0.0 collective-permute-start.9
  26.7 0.4 collective-permute-start.8
  27.1 2.1 %collective-permute-done.10 = bf16[304,128]{1,0:T(8,128)(2,1)S(1)} collective-permute-done((bf16[304,128]{1,0:T(8,128)(2,1)S(1)}, bf16[304,128]{1,0:T(8,128)(2,1)S(1)}, u32[]{:S(2)}, u32[]{:S(2)}) %collective-permute-start.10) | collective-permute-done | bytes 77856 | tf_op jit(solution)/shard_map/ppermute | solution.py:866
  29.2 4.6 %collective-permute-done.9 = bf16[304,128]{1,0:T(8,128)(2,1)S(1)} collective-permute-done((bf16[304,128]{1,0:T(8,128)(2,1)S(1)}, bf16[304,128]{1,0:T(8,128)(2,1)S(1)}, u32[]{:S(2)}, u32[]{:S(2)}) %collective-permute-start.9) | collective-permute-done | bytes 77856 | tf_op jit(solution)/shard_map/ppermute | solution.py:866
  33.8 0.0 collective-permute-done.8
  33.8 0.1 add_add_fusion.mine_ref
  33.9 0.9 %collective-permute-start.11 = (f32[304,128]{1,0:T(8,128)S(1)}, f32[304,128]{1,0:T(8,128)S(1)}, u32[]{:S(2)}, u32[]{:S(2)}) collective-permute-start(f32[304,128]{1,0:T(8,128)S(1)} %add_add_fusion.mine_ref), channel_id=1, source_target_pairs={{0,1},{1,0},{2,3},{3,2},{4,5},{5,4},{6,7},{7,6},{8,9},{9,8},{10,11... | collective-permute-start | bytes 466952 | tf_op jit(solution)/shard_map/ppermute | solution.py:871
  34.8 0.7 %shard_map.77 = bf16[64,2048]{1,0:T(8,128)(2,1)} custom-call(f32[16,112,128]{2,1,0:T(8,128)S(1)} %get-tuple-element.63.bi_f, f32[12,80,128]{2,1,0:T(8,128)S(1)} %get-tuple-element.77.bi_o, f32[9,72,128]{2,1,0:T(8,128)S(1)} %get-tuple-element.88.bi_l), custom_call_target="tpu_custom_call" | custom-call | flops 1000 | bytes 1000 | tf_op jit(solution)/shard_map/pallas_call | solution.py:364
  35.5 0.3 collective-permute-done.11.other_ref
  35.8 1.1 %shard_map.78 = (f32[2,576,64]{2,1,0:T(8,128)}, f32[2,64]{1,0:T(2,128)}) custom-call(f32[304,128]{1,0:T(8,128)S(1)} %add_add_fusion.mine_ref, f32[304,128]{1,0:T(8,128)S(1)} %collective-permute-done.11.other_ref), custom_call_target="tpu_custom_call" | custom-call | flops 1000 | bytes 1000 | tf_op jit(solution)/shard_map/pallas_call | solution.py:364
  (6 shorter events, 0.1 us)
Async XLA Ops:
  0.6 5.2 %copy-start = (bf16[1,2,3,3,64,64]{5,4,3,2,1,0:T(8,128)(2,1)S(1)}, bf16[1,2,3,3,64,64]{5,4,3,2,1,0:T(8,128)(2,1)}, u32[]{:S(2)}) copy-start(bf16[1,2,3,3,64,64]{5,4,3,2,1,0:T(8,128)(2,1)} %param.6) | copy-start | bytes 442372
  2.0 6.5 %collective-permute-start = (bf16[32,2048]{1,0:T(8,128)(2,1)S(1)}, bf16[32,2048]{1,0:T(8,128)(2,1)S(1)}, u32[]{:S(2)}, u32[]{:S(2)}) collective-permute-start(bf16[32,2048]{1,0:T(8,128)(2,1)S(1)} %get-tuple-element.48), channel_id=1, source_target_pairs={{0,1},{1,0},{2,3},{3,2},{4,5},{5,4},{6,7},{7,6},{8,9},{9,8},{10,11... | collective-permute-start | bytes 393224 | tf_op jit(solution)/shard_map/ppermute | solution.py:455
  2.7 6.6 %collective-permute-start.1 = (bf16[32,2048]{1,0:T(8,128)(2,1)S(1)}, bf16[32,2048]{1,0:T(8,128)(2,1)S(1)}, u32[]{:S(2)}, u32[]{:S(2)}) collective-permute-start(bf16[32,2048]{1,0:T(8,128)(2,1)S(1)} %get-tuple-element.49), channel_id=1, source_target_pairs={{1,2},{3,4},{5,6},{2,1},{4,3},{6,5},{9,10},{11,12},{13,14},{10,9},... | collective-permute-start | bytes 393224 | tf_op jit(solution)/shard_map/ppermute | solution.py:454
  6.2 7.2 %collective-permute-start.3 = (bf16[480,128]{1,0:T(8,128)(2,1)S(1)}, bf16[480,128]{1,0:T(8,128)(2,1)S(1)}, u32[]{:S(2)}, u32[]{:S(2)}) collective-permute-start(bf16[480,128]{1,0:T(8,128)(2,1)S(1)} %get-tuple-element.71), channel_id=1, source_target_pairs={{0,8},{8,24},{24,16},{16,0},{1,9},{9,25},{25,17},{17,1},{2,10},{10... | collective-permute-start | bytes 368648 | tf_op jit(solution)/shard_map/ppermute | solution.py:471
  9.3 4.1 %collective-permute-start.2 = (bf16[320,128]{1,0:T(8,128)(2,1)S(1)}, bf16[320,128]{1,0:T(8,128)(2,1)S(1)}, u32[]{:S(2)}, u32[]{:S(2)}) collective-permute-start(bf16[320,128]{1,0:T(8,128)(2,1)S(1)} %get-tuple-element.64.rim_ref), channel_id=1, source_target_pairs={{0,8},{8,24},{24,16},{16,0},{1,9},{9,25},{25,17},{17,1},{2,10},{10... | collective-permute-start | bytes 245768 | tf_op jit(solution)/shard_map/ppermute | solution.py:471
  10.9 8.9 %collective-permute-start.4 = (bf16[1056,128]{1,0:T(8,128)(2,1)S(1)}, bf16[1056,128]{1,0:T(8,128)(2,1)S(1)}, u32[]{:S(2)}, u32[]{:S(2)}) collective-permute-start(bf16[1056,128]{1,0:T(8,128)(2,1)S(1)} %shard_map.74), channel_id=1, source_target_pairs={{16,24},{17,25},{18,26},{19,27},{20,28},{21,29},{22,30},{23,31}} | collective-permute-start | bytes 811016 | tf_op jit(solution)/shard_map/ppermute | solution.py:471
  13.4 6.3 %collective-permute-start.5 = (bf16[416,128]{1,0:T(8,128)(2,1)S(1)}, bf16[416,128]{1,0:T(8,128)(2,1)S(1)}, u32[]{:S(2)}, u32[]{:S(2)}) collective-permute-start(bf16[416,128]{1,0:T(8,128)(2,1)S(1)} %get-tuple-element.79), channel_id=1, source_target_pairs={{8,16},{9,17},{10,18},{11,19},{12,20},{13,21},{14,22},{15,23}} | collective-permute-start | bytes 319496 | tf_op jit(solution)/shard_map/ppermute | solution.py:471
  14.7 5.1 %collective-permute-start.6 = (bf16[416,128]{1,0:T(8,128)(2,1)S(1)}, bf16[416,128]{1,0:T(8,128)(2,1)S(1)}, u32[]{:S(2)}, u32[]{:S(2)}) collective-permute-start(bf16[416,128]{1,0:T(8,128)(2,1)S(1)} %get-tuple-element.79), channel_id=1, source_target_pairs={{8,24},{24,16},{16,0},{0,8},{9,25},{25,17},{17,1},{1,9},{10,26},{2... | collective-permute-start | bytes 319496 | tf_op jit(solution)/shard_map/ppermute | solution.py:471
  20.8 1.4 %collective-permute-start.7 = (f32[304,128]{1,0:T(8,128)S(1)}, f32[304,128]{1,0:T(8,128)S(1)}, u32[]{:S(2)}, u32[]{:S(2)}) collective-permute-start(f32[304,128]{1,0:T(8,128)S(1)} %get-tuple-element.90), channel_id=1, source_target_pairs={{0,1},{1,0},{2,3},{3,2},{4,5},{5,4},{6,7},{7,6},{8,9},{9,8},{10,11... | collective-permute-start | bytes 466952 | tf_op jit(solution)/shard_map/ppermute | solution.py:860
  22.3 6.9 %collective-permute-start.10 = (bf16[304,128]{1,0:T(8,128)(2,1)S(1)}, bf16[304,128]{1,0:T(8,128)(2,1)S(1)}, u32[]{:S(2)}, u32[]{:S(2)}) collective-permute-start(bf16[304,128]{1,0:T(8,128)(2,1)S(1)} %fusion), channel_id=1, source_target_pairs={{0,6},{1,7},{2,4},{3,5},{4,2},{5,3},{6,0},{7,1},{8,14},{9,15},{10,... | collective-permute-start | bytes 233480 | tf_op jit(solution)/shard_map/ppermute | solution.py:866
  26.7 7.1 %collective-permute-start.9 = (bf16[304,128]{1,0:T(8,128)(2,1)S(1)}, bf16[304,128]{1,0:T(8,128)(2,1)S(1)}, u32[]{:S(2)}, u32[]{:S(2)}) collective-permute-start(bf16[304,128]{1,0:T(8,128)(2,1)S(1)} %fusion), channel_id=1, source_target_pairs={{0,4},{1,5},{2,6},{3,7},{4,0},{5,1},{6,2},{7,3},{8,12},{9,13},{10,... | collective-permute-start | bytes 233480 | tf_op jit(solution)/shard_map/ppermute | solution.py:866
  26.7 7.1 %collective-permute-start.8 = (bf16[304,128]{1,0:T(8,128)(2,1)S(1)}, bf16[304,128]{1,0:T(8,128)(2,1)S(1)}, u32[]{:S(2)}, u32[]{:S(2)}) collective-permute-start(bf16[304,128]{1,0:T(8,128)(2,1)S(1)} %fusion), channel_id=1, source_target_pairs={{0,2},{1,3},{2,0},{3,1},{4,6},{5,7},{6,4},{7,5},{8,10},{9,11},{10,... | collective-permute-start | bytes 233480 | tf_op jit(solution)/shard_map/ppermute | solution.py:866
  33.9 1.9 %collective-permute-start.11 = (f32[304,128]{1,0:T(8,128)S(1)}, f32[304,128]{1,0:T(8,128)S(1)}, u32[]{:S(2)}, u32[]{:S(2)}) collective-permute-start(f32[304,128]{1,0:T(8,128)S(1)} %add_add_fusion.mine_ref), channel_id=1, source_target_pairs={{0,1},{1,0},{2,3},{3,2},{4,5},{5,4},{6,7},{7,6},{8,9},{9,8},{10,11... | collective-permute-start | bytes 466952 | tf_op jit(solution)/shard_map/ppermute | solution.py:871

commit v8 on v7

--- a/solution.py
+++ b/solution.py
@@ -881,31 +881,39 @@
 
     (noise,) = call(noise_body, [strip_shape], [], [state[6], bi_own, bi_last], final=(0,))
 
-    def final_body(mine_ref, other_ref, kernel_ref, bias_ref):
+    def in_taps(value, ref):
+        half = channels
+        for dy in range(3):
+            ref[dy * 192 : dy * 192 + 128, :] = value[dy * half : (dy + 1) * half].T
+        pair = value[3 * half : 4 * half].T
+        ref[128:192, :] = pair[:half]
+        ref[320:384, :] = pair[half:]
+        at = 4 * half + half // 2
+        pair = value[4 * half : at].T
+        ref[512:576, :] = jnp.concatenate([pair[:half], pair[half:]], axis=1)
+        ref[576:584, :] = value[at : at + 8, :half]
+
+    tap_rows = TAPS * channels + 8
+
+    def mine_body(mine_ref, taps_ref):
+        in_taps(mine_ref[...], taps_ref)
+
+    (mine_taps,) = call(mine_body, [sds((tap_rows, channels), F32)], [], [total])
+
+    def final_body(mine_ref, other_ref, kernel_ref, bias_ref, other_taps):
         odd = is_odd()
-        half = channels
-        bias_rows = []
-        for c in range(2):
-            if c == 0:
-                value = jnp.where(odd, other_ref[...], mine_ref[...])
-            else:
-                value = jnp.where(odd, mine_ref[...], other_ref[...])
-            for dy in range(3):
-                kernel_ref[c, dy * 192 : dy * 192 + 128, :] = value[dy * half : (dy + 1) * half].T
-            pair = value[3 * half : 4 * half].T
-            kernel_ref[c, 128:192, :] = pair[:half]
-            kernel_ref[c, 320:384, :] = pair[half:]
-            at = 4 * half + half // 2
-            pair = value[4 * half : at].T
-            kernel_ref[c, 512:576, :] = jnp.concatenate([pair[:half], pair[half:]], axis=1)
-            bias_rows.append(value[at : at + 1, :half])
-        bias_ref[...] = jnp.concatenate(bias_rows, axis=0)
+        in_taps(other_ref[...], other_taps)
+        mine, theirs = mine_ref[...], other_taps[...]
+        first, then = jnp.where(odd, theirs, mine), jnp.where(odd, mine, theirs)
+        kernel_ref[0, :, :] = first[: tap_rows - 8]
+        kernel_ref[1, :, :] = then[: tap_rows - 8]
+        bias_ref[...] = jnp.concatenate([first[tap_rows - 8 : tap_rows - 7], then[tap_rows - 8 : tap_rows - 7]], axis=0)
 
     kernel_sum, bias_sum = call(
         final_body,
         [sds((2, TAPS * channels, channels), F32), sds((2, channels), F32)],
-        [],
-        [total, other],
+        [pltpu.VMEM((tap_rows, channels), F32)],
+        [mine_taps, other],
         final=(0, 1),
     )
     return (

time: 37.1 us -> 37.1 us (level)
    pallas_call x12 -> x13, Pallas kernels: 5.35 us -> 5.49 us  [call(): pl.pallas_call(body, out_shape=out_shape, in_specs=[pl.BlockSpec(memory_s...]
  transfers between devices with their start and end apart: 12 -> 12, of which waited for: 6 -> 6; matrix products, arithmetic and copies ran while one was open for 0% -> 0% of each run, Pallas kernels for 5% -> 6%
where the time goes in v8:
time: 37.1 us; the launch traced here: 36.9 us
  starting transfers between devices  16.5 us (44%)
  waiting for transfers between devices  14 us (38%)
  Pallas kernels  5.49 us (15%)
  between operations  0.78 us (2%)
    ppermute x5, starting transfers between devices, across(): return lax.ppermute(value, 'section', pairs)  6.89 us
    ppermute x3, waiting for transfers between devices, local(): lax.ppermute(small, 'strip', [(i, i ^ o) for i in range(strips)])  6.77 us
    pallas_call x13, Pallas kernels, call(): pl.pallas_call(body, out_shape=out_shape, in_specs=[pl.BlockSpec(memory_s...  5.49 us
    ppermute x5, waiting for transfers between devices, across(): return lax.ppermute(value, 'section', pairs)  4.99 us
    ppermute x3, starting transfers between devices, local(): lax.ppermute(small, 'strip', [(i, i ^ o) for i in range(strips)])  4.82 us
    ppermute x1, starting transfers between devices, local(): from_cross = lax.ppermute(to_cross, 'strip', cross_pairs)  3.1 us
    ppermute x1, waiting for transfers between devices, local(): total = keep + lax.ppermute(send, 'strip', swap_pairs)  1.37 us
    ppermute x1, starting transfers between devices, local(): other = lax.ppermute(total, 'strip', swap_pairs)  0.89 us
  transfers between devices with their start and end apart: 12, of which 6 were waited for; matrix products, arithmetic and copies ran while one was open for 0% of the time, Pallas kernels for 6%

profile of v8, /device:TPU:5, one launch (start us, length us, event | category | flops | bytes accessed | tf_op | source)
XLA Modules:
  0.0 36.9 jit_solution(3312418447864271940)
XLA Ops:
  0.6 0.0 copy-start
  0.6 1.3 %shard_map.67 = (bf16[64,2048]{1,0:T(8,128)(2,1)S(1)}, bf16[64,2048]{1,0:T(8,128)(2,1)S(1)}, f32[8,128]{1,0:T(8,128)S(1)}, bf16[32,2048]{1,0:T(8,128)(2,1)S(1)}, bf16[32,2048]{1,0:T(8,128)(2,1)S(1)}) custom-call(bf16[64,2048]{1,0:T(8,128)(2,1)} %bitcast.10, bf16[64,2048]{1,0:T(8,128)(2,1)} %bitcast.11, f32[2,64]{1,0:T(2,128)} %bitcast.12), custom_call_target="tpu_custom_call" | custom-call | flops 1000 | bytes 1000 | tf_op jit(solution)/shard_map/pallas_call | solution.py:364
  2.0 0.7 %collective-permute-start = (bf16[32,2048]{1,0:T(8,128)(2,1)S(1)}, bf16[32,2048]{1,0:T(8,128)(2,1)S(1)}, u32[]{:S(2)}, u32[]{:S(2)}) collective-permute-start(bf16[32,2048]{1,0:T(8,128)(2,1)S(1)} %get-tuple-element.48), channel_id=1, source_target_pairs={{0,1},{1,0},{2,3},{3,2},{4,5},{5,4},{6,7},{7,6},{8,9},{9,8},{10,11... | collective-permute-start | bytes 393224 | tf_op jit(solution)/shard_map/ppermute | solution.py:455
  2.7 3.1 %collective-permute-start.1 = (bf16[32,2048]{1,0:T(8,128)(2,1)S(1)}, bf16[32,2048]{1,0:T(8,128)(2,1)S(1)}, u32[]{:S(2)}, u32[]{:S(2)}) collective-permute-start(bf16[32,2048]{1,0:T(8,128)(2,1)S(1)} %get-tuple-element.49), channel_id=1, source_target_pairs={{1,2},{3,4},{5,6},{2,1},{4,3},{6,5},{9,10},{11,12},{13,14},{10,9},... | collective-permute-start | bytes 393224 | tf_op jit(solution)/shard_map/ppermute | solution.py:454
  5.8 0.0 copy-done
  5.8 0.3 shard_map.68
  6.2 2.3 %collective-permute-start.3 = (bf16[480,128]{1,0:T(8,128)(2,1)S(1)}, bf16[480,128]{1,0:T(8,128)(2,1)S(1)}, u32[]{:S(2)}, u32[]{:S(2)}) collective-permute-start(bf16[480,128]{1,0:T(8,128)(2,1)S(1)} %get-tuple-element.71), channel_id=1, source_target_pairs={{0,8},{8,24},{24,16},{16,0},{1,9},{9,25},{25,17},{17,1},{2,10},{10... | collective-permute-start | bytes 368648 | tf_op jit(solution)/shard_map/ppermute | solution.py:471
  8.5 0.0 collective-permute-done.swap_ref
  8.5 0.8 %collective-permute-done.1.cross_ref = bf16[32,2048]{1,0:T(8,128)(2,1)S(1)} collective-permute-done((bf16[32,2048]{1,0:T(8,128)(2,1)S(1)}, bf16[32,2048]{1,0:T(8,128)(2,1)S(1)}, u32[]{:S(2)}, u32[]{:S(2)}) %collective-permute-start.1) | collective-permute-done | bytes 131104 | tf_op jit(solution)/shard_map/ppermute | solution.py:454
  9.3 1.5 %collective-permute-start.2 = (bf16[320,128]{1,0:T(8,128)(2,1)S(1)}, bf16[320,128]{1,0:T(8,128)(2,1)S(1)}, u32[]{:S(2)}, u32[]{:S(2)}) collective-permute-start(bf16[320,128]{1,0:T(8,128)(2,1)S(1)} %get-tuple-element.64.rim_ref), channel_id=1, source_target_pairs={{0,8},{8,24},{24,16},{16,0},{1,9},{9,25},{25,17},{17,1},{2,10},{10... | collective-permute-start | bytes 245768 | tf_op jit(solution)/shard_map/ppermute | solution.py:471
  10.7 0.1 shard_map.74
  10.9 1.8 %collective-permute-start.4 = (bf16[1056,128]{1,0:T(8,128)(2,1)S(1)}, bf16[1056,128]{1,0:T(8,128)(2,1)S(1)}, u32[]{:S(2)}, u32[]{:S(2)}) collective-permute-start(bf16[1056,128]{1,0:T(8,128)(2,1)S(1)} %shard_map.74), channel_id=1, source_target_pairs={{16,24},{17,25},{18,26},{19,27},{20,28},{21,29},{22,30},{23,31}} | collective-permute-start | bytes 811016 | tf_op jit(solution)/shard_map/ppermute | solution.py:471
  12.7 0.7 %shard_map.71 = (f32[13,80,128]{2,1,0:T(8,128)S(1)}, f32[12,80,128]{2,1,0:T(8,128)S(1)}, f32[13,80,128]{2,1,0:T(8,128)S(1)}, f32[14,80,128]{2,1,0:T(8,128)S(1)}, f32[2,304,128]{2,1,0:T(8,128)S(1)}) custom-call(bf16[64,2048]{1,0:T(8,128)(2,1)S(1)} %get-tuple-element.53.act_ref, bf16[32,2048]{1,0:T(8,128)(2,1)S(1)} %collective-permute-done.swap_ref, ...), custom_call_target="tpu_custom_call" | custom-call | flops 1000 | bytes 1000 | tf_op jit(solution)/shard_map/pallas_call | solution.py:364
  13.4 0.0 collective-permute-done.3.in_ref
  13.4 0.0 collective-permute-done.2.rim_ref
  13.4 1.3 %collective-permute-start.5 = (bf16[416,128]{1,0:T(8,128)(2,1)S(1)}, bf16[416,128]{1,0:T(8,128)(2,1)S(1)}, u32[]{:S(2)}, u32[]{:S(2)}) collective-permute-start(bf16[416,128]{1,0:T(8,128)(2,1)S(1)} %get-tuple-element.79), channel_id=1, source_target_pairs={{8,16},{9,17},{10,18},{11,19},{12,20},{13,21},{14,22},{15,23}} | collective-permute-start | bytes 319496 | tf_op jit(solution)/shard_map/ppermute | solution.py:471
  14.7 0.1 collective-permute-start.6
  14.8 5.0 %collective-permute-done.5.own_ref = bf16[416,128]{1,0:T(8,128)(2,1)S(1)} collective-permute-done((bf16[416,128]{1,0:T(8,128)(2,1)S(1)}, bf16[416,128]{1,0:T(8,128)(2,1)S(1)}, u32[]{:S(2)}, u32[]{:S(2)}) %collective-permute-start.5) | collective-permute-done | bytes 106528 | tf_op jit(solution)/shard_map/ppermute | solution.py:471
  19.8 0.0 collective-permute-done.4.ship_ref
  19.8 0.0 collective-permute-done.6.last_ref
  19.8 1.0 %shard_map.76 = (f32[304,128]{1,0:T(8,128)S(1)}, f32[304,128]{1,0:T(8,128)S(1)}, f32[9,72,128]{2,1,0:T(8,128)S(1)}) custom-call(f32[2,304,128]{2,1,0:T(8,128)S(1)} %get-tuple-element.78.pair0, f32[2,304,128]{2,1,0:T(8,128)S(1)} %get-tuple-element.84.pair1, bf16[416,128]{1,0:T(8,128)(2,1)S(1)} %collective-permute-done.5.own_ref, ...), custom_call_target="tpu_custom_call" | custom-call | flops 1000 | bytes 1000 | tf_op jit(solution)/shard_map/pallas_call | solution.py:364
  20.8 0.1 collective-permute-start.7
  20.9 1.4 %collective-permute-done.7 = f32[304,128]{1,0:T(8,128)S(1)} collective-permute-done((f32[304,128]{1,0:T(8,128)S(1)}, f32[304,128]{1,0:T(8,128)S(1)}, u32[]{:S(2)}, u32[]{:S(2)}) %collective-permute-start.7) | collective-permute-done | bytes 155680 | tf_op jit(solution)/shard_map/ppermute | solution.py:860
  22.3 4.5 %collective-permute-start.10 = (bf16[304,128]{1,0:T(8,128)(2,1)S(1)}, bf16[304,128]{1,0:T(8,128)(2,1)S(1)}, u32[]{:S(2)}, u32[]{:S(2)}) collective-permute-start(bf16[304,128]{1,0:T(8,128)(2,1)S(1)} %fusion), channel_id=1, source_target_pairs={{0,6},{1,7},{2,4},{3,5},{4,2},{5,3},{6,0},{7,1},{8,14},{9,15},{10,... | collective-permute-start | bytes 233480 | tf_op jit(solution)/shard_map/ppermute | solution.py:866
  26.7 0.0 collective-permute-start.9
  26.7 0.4 collective-permute-start.8
  27.1 2.1 %collective-permute-done.10 = bf16[304,128]{1,0:T(8,128)(2,1)S(1)} collective-permute-done((bf16[304,128]{1,0:T(8,128)(2,1)S(1)}, bf16[304,128]{1,0:T(8,128)(2,1)S(1)}, u32[]{:S(2)}, u32[]{:S(2)}) %collective-permute-start.10) | collective-permute-done | bytes 77856 | tf_op jit(solution)/shard_map/ppermute | solution.py:866
  29.2 4.6 %collective-permute-done.9 = bf16[304,128]{1,0:T(8,128)(2,1)S(1)} collective-permute-done((bf16[304,128]{1,0:T(8,128)(2,1)S(1)}, bf16[304,128]{1,0:T(8,128)(2,1)S(1)}, u32[]{:S(2)}, u32[]{:S(2)}) %collective-permute-start.9) | collective-permute-done | bytes 77856 | tf_op jit(solution)/shard_map/ppermute | solution.py:866
  33.8 0.0 collective-permute-done.8
  33.8 0.1 add_add_fusion.mine_ref
  33.9 0.9 %collective-permute-start.11 = (f32[304,128]{1,0:T(8,128)S(1)}, f32[304,128]{1,0:T(8,128)S(1)}, u32[]{:S(2)}, u32[]{:S(2)}) collective-permute-start(f32[304,128]{1,0:T(8,128)S(1)} %add_add_fusion.mine_ref), channel_id=1, source_target_pairs={{0,1},{1,0},{2,3},{3,2},{4,5},{5,4},{6,7},{7,6},{8,9},{9,8},{10,11... | collective-permute-start | bytes 466952 | tf_op jit(solution)/shard_map/ppermute | solution.py:871
  34.8 0.7 %shard_map.77 = bf16[64,2048]{1,0:T(8,128)(2,1)} custom-call(f32[16,112,128]{2,1,0:T(8,128)S(1)} %get-tuple-element.63.bi_f, f32[12,80,128]{2,1,0:T(8,128)S(1)} %get-tuple-element.77.bi_o, f32[9,72,128]{2,1,0:T(8,128)S(1)} %get-tuple-element.88.bi_l), custom_call_target="tpu_custom_call" | custom-call | flops 1000 | bytes 1000 | tf_op jit(solution)/shard_map/pallas_call | solution.py:364
  35.5 0.2 shard_map.78.mine_ref
  35.7 0.1 collective-permute-done.11.other_ref
  35.8 1.1 %shard_map.79 = (f32[2,576,64]{2,1,0:T(8,128)}, f32[2,64]{1,0:T(2,128)}) custom-call(f32[584,64]{1,0:T(8,128)S(1)} %shard_map.78.mine_ref, f32[304,128]{1,0:T(8,128)S(1)} %collective-permute-done.11.other_ref), custom_call_target="tpu_custom_call" | custom-call | flops 1000 | bytes 1000 | tf_op jit(solution)/shard_map/pallas_call | solution.py:364
  (6 shorter events, 0.1 us)
Async XLA Ops:
  0.6 5.2 %copy-start = (bf16[1,2,3,3,64,64]{5,4,3,2,1,0:T(8,128)(2,1)S(1)}, bf16[1,2,3,3,64,64]{5,4,3,2,1,0:T(8,128)(2,1)}, u32[]{:S(2)}) copy-start(bf16[1,2,3,3,64,64]{5,4,3,2,1,0:T(8,128)(2,1)} %param.6) | copy-start | bytes 442372
  2.0 6.5 %collective-permute-start = (bf16[32,2048]{1,0:T(8,128)(2,1)S(1)}, bf16[32,2048]{1,0:T(8,128)(2,1)S(1)}, u32[]{:S(2)}, u32[]{:S(2)}) collective-permute-start(bf16[32,2048]{1,0:T(8,128)(2,1)S(1)} %get-tuple-element.48), channel_id=1, source_target_pairs={{0,1},{1,0},{2,3},{3,2},{4,5},{5,4},{6,7},{7,6},{8,9},{9,8},{10,11... | collective-permute-start | bytes 393224 | tf_op jit(solution)/shard_map/ppermute | solution.py:455
  2.7 6.6 %collective-permute-start.1 = (bf16[32,2048]{1,0:T(8,128)(2,1)S(1)}, bf16[32,2048]{1,0:T(8,128)(2,1)S(1)}, u32[]{:S(2)}, u32[]{:S(2)}) collective-permute-start(bf16[32,2048]{1,0:T(8,128)(2,1)S(1)} %get-tuple-element.49), channel_id=1, source_target_pairs={{1,2},{3,4},{5,6},{2,1},{4,3},{6,5},{9,10},{11,12},{13,14},{10,9},... | collective-permute-start | bytes 393224 | tf_op jit(solution)/shard_map/ppermute | solution.py:454
  6.2 7.2 %collective-permute-start.3 = (bf16[480,128]{1,0:T(8,128)(2,1)S(1)}, bf16[480,128]{1,0:T(8,128)(2,1)S(1)}, u32[]{:S(2)}, u32[]{:S(2)}) collective-permute-start(bf16[480,128]{1,0:T(8,128)(2,1)S(1)} %get-tuple-element.71), channel_id=1, source_target_pairs={{0,8},{8,24},{24,16},{16,0},{1,9},{9,25},{25,17},{17,1},{2,10},{10... | collective-permute-start | bytes 368648 | tf_op jit(solution)/shard_map/ppermute | solution.py:471
  9.3 4.1 %collective-permute-start.2 = (bf16[320,128]{1,0:T(8,128)(2,1)S(1)}, bf16[320,128]{1,0:T(8,128)(2,1)S(1)}, u32[]{:S(2)}, u32[]{:S(2)}) collective-permute-start(bf16[320,128]{1,0:T(8,128)(2,1)S(1)} %get-tuple-element.64.rim_ref), channel_id=1, source_target_pairs={{0,8},{8,24},{24,16},{16,0},{1,9},{9,25},{25,17},{17,1},{2,10},{10... | collective-permute-start | bytes 245768 | tf_op jit(solution)/shard_map/ppermute | solution.py:471
  10.9 8.9 %collective-permute-start.4 = (bf16[1056,128]{1,0:T(8,128)(2,1)S(1)}, bf16[1056,128]{1,0:T(8,128)(2,1)S(1)}, u32[]{:S(2)}, u32[]{:S(2)}) collective-permute-start(bf16[1056,128]{1,0:T(8,128)(2,1)S(1)} %shard_map.74), channel_id=1, source_target_pairs={{16,24},{17,25},{18,26},{19,27},{20,28},{21,29},{22,30},{23,31}} | collective-permute-start | bytes 811016 | tf_op jit(solution)/shard_map/ppermute | solution.py:471
  13.4 6.3 %collective-permute-start.5 = (bf16[416,128]{1,0:T(8,128)(2,1)S(1)}, bf16[416,128]{1,0:T(8,128)(2,1)S(1)}, u32[]{:S(2)}, u32[]{:S(2)}) collective-permute-start(bf16[416,128]{1,0:T(8,128)(2,1)S(1)} %get-tuple-element.79), channel_id=1, source_target_pairs={{8,16},{9,17},{10,18},{11,19},{12,20},{13,21},{14,22},{15,23}} | collective-permute-start | bytes 319496 | tf_op jit(solution)/shard_map/ppermute | solution.py:471
  14.7 5.1 %collective-permute-start.6 = (bf16[416,128]{1,0:T(8,128)(2,1)S(1)}, bf16[416,128]{1,0:T(8,128)(2,1)S(1)}, u32[]{:S(2)}, u32[]{:S(2)}) collective-permute-start(bf16[416,128]{1,0:T(8,128)(2,1)S(1)} %get-tuple-element.79), channel_id=1, source_target_pairs={{8,24},{24,16},{16,0},{0,8},{9,25},{25,17},{17,1},{1,9},{10,26},{2... | collective-permute-start | bytes 319496 | tf_op jit(solution)/shard_map/ppermute | solution.py:471
  20.8 1.4 %collective-permute-start.7 = (f32[304,128]{1,0:T(8,128)S(1)}, f32[304,128]{1,0:T(8,128)S(1)}, u32[]{:S(2)}, u32[]{:S(2)}) collective-permute-start(f32[304,128]{1,0:T(8,128)S(1)} %get-tuple-element.90), channel_id=1, source_target_pairs={{0,1},{1,0},{2,3},{3,2},{4,5},{5,4},{6,7},{7,6},{8,9},{9,8},{10,11... | collective-permute-start | bytes 466952 | tf_op jit(solution)/shard_map/ppermute | solution.py:860
  22.3 6.9 %collective-permute-start.10 = (bf16[304,128]{1,0:T(8,128)(2,1)S(1)}, bf16[304,128]{1,0:T(8,128)(2,1)S(1)}, u32[]{:S(2)}, u32[]{:S(2)}) collective-permute-start(bf16[304,128]{1,0:T(8,128)(2,1)S(1)} %fusion), channel_id=1, source_target_pairs={{0,6},{1,7},{2,4},{3,5},{4,2},{5,3},{6,0},{7,1},{8,14},{9,15},{10,... | collective-permute-start | bytes 233480 | tf_op jit(solution)/shard_map/ppermute | solution.py:866
  26.7 7.1 %collective-permute-start.9 = (bf16[304,128]{1,0:T(8,128)(2,1)S(1)}, bf16[304,128]{1,0:T(8,128)(2,1)S(1)}, u32[]{:S(2)}, u32[]{:S(2)}) collective-permute-start(bf16[304,128]{1,0:T(8,128)(2,1)S(1)} %fusion), channel_id=1, source_target_pairs={{0,4},{1,5},{2,6},{3,7},{4,0},{5,1},{6,2},{7,3},{8,12},{9,13},{10,... | collective-permute-start | bytes 233480 | tf_op jit(solution)/shard_map/ppermute | solution.py:866
  26.7 7.1 %collective-permute-start.8 = (bf16[304,128]{1,0:T(8,128)(2,1)S(1)}, bf16[304,128]{1,0:T(8,128)(2,1)S(1)}, u32[]{:S(2)}, u32[]{:S(2)}) collective-permute-start(bf16[304,128]{1,0:T(8,128)(2,1)S(1)} %fusion), channel_id=1, source_target_pairs={{0,2},{1,3},{2,0},{3,1},{4,6},{5,7},{6,4},{7,5},{8,10},{9,11},{10,... | collective-permute-start | bytes 233480 | tf_op jit(solution)/shard_map/ppermute | solution.py:866
  33.9 1.9 %collective-permute-start.11 = (f32[304,128]{1,0:T(8,128)S(1)}, f32[304,128]{1,0:T(8,128)S(1)}, u32[]{:S(2)}, u32[]{:S(2)}) collective-permute-start(f32[304,128]{1,0:T(8,128)S(1)} %add_add_fusion.mine_ref), channel_id=1, source_target_pairs={{0,1},{1,0},{2,3},{3,2},{4,5},{5,4},{6,7},{7,6},{8,9},{9,8},{10,11... | collective-permute-start | bytes 466952 | tf_op jit(solution)/shard_map/ppermute | solution.py:871
